TPU v7x, 512 devices: a whole 4x8x8 slice. The times are simulated.
512 devices in a mesh: dp: 64 (over x, z, core), tensor: 8 (over y).
Axes of the slice: x: 4, y: 8, z: 8, core: 2. Of those that a mesh axis runs over, the one named last changes fastest.
Arguments:
- tokens: bfloat16 [24576, 4096], P('dp', 'tensor'), may hold values from -6 to 6
- w_gate: bfloat16 [640, 4096], P('tensor'), may hold values from -0.09375 to 0.09375
- w_up: bfloat16 [640, 4096], P('tensor'), may hold values from -0.09375 to 0.09375
- d_hidden: bfloat16 [24576, 640], P('dp', 'tensor'), may hold values from -6 to 6
- error_fb: bfloat16 [64, 2, 640, 4096], P('dp', None, 'tensor'), may hold values from -3 to 3
- q_prev: float32 [2, 640, 64], P(None, 'tensor'), may hold values from -6 to 6
Outputs:
- d_tokens: bfloat16 [24576, 4096], P('dp', 'tensor')
- new_error: bfloat16 [64, 2, 640, 4096], P('dp', None, 'tensor')
- q_next: float32 [2, 640, 64], P(None, 'tensor')
All inputs are finite; a program needn't handle non-finite values.
Results may differ from a plain program's by a relative error of at most 0.017.
Values may be sent and summed in bfloat16 or wider, within the bound.
No kernel may reach another device: no remote copies, remote signals or barrier semaphores. Data moves between devices by JAX's collectives and lax.ppermute only.
A program may use at most 64 MiB of HBM per device.

v0:
```python
import math

import jax
import jax.numpy as jnp
from jax import lax
from jax.sharding import PartitionSpec as P

HIGH_PRECISION = lax.Precision.HIGHEST


def on_device(tokens, w_gate, w_up, d_hidden, error_fb, q_prev):
    contract_last = (((1,), (1,)), ((), ()))
    contract_first = (((0,), (0,)), ((), ()))
    whole = lax.all_gather(tokens, "tensor", axis=1, tiled=True)
    gate_pre = lax.dot_general(whole, w_gate, contract_last, preferred_element_type=jnp.float32)
    up_pre = lax.dot_general(whole, w_up, contract_last, preferred_element_type=jnp.float32)
    squash = jax.nn.sigmoid(gate_pre)
    upstream = d_hidden.astype(jnp.float32)
    d_gate = (upstream * up_pre * squash * (1.0 + gate_pre * (1.0 - squash))).astype(jnp.bfloat16)
    d_up = (upstream * gate_pre * squash).astype(jnp.bfloat16)
    act_terms = jnp.dot(d_gate, w_gate, preferred_element_type=jnp.float32) + jnp.dot(
        d_up, w_up, preferred_element_type=jnp.float32
    )
    summed = lax.psum(act_terms.astype(jnp.bfloat16), "tensor").astype(jnp.float32)
    slice_width = act_terms.shape[1] // lax.axis_size("tensor")
    d_tokens = lax.dynamic_slice_in_dim(
        summed, lax.axis_index("tensor") * slice_width, slice_width, 1
    ).astype(jnp.bfloat16)
    grads = jnp.concatenate(
        [
            lax.dot_general(d_gate, whole, contract_first, preferred_element_type=jnp.float32),
            lax.dot_general(d_up, whole, contract_first, preferred_element_type=jnp.float32),
        ],
        0,
    )
    grad_scale = 1.0 / math.sqrt(whole.shape[0])
    merged = grads * grad_scale + error_fb.reshape(grads.shape).astype(jnp.float32)
    q_matrix = q_prev.reshape(grads.shape[0], q_prev.shape[2])
    p_local = lax.dot_general(
        q_matrix,
        merged,
        contract_first,
        precision=HIGH_PRECISION,
        preferred_element_type=jnp.float32,
    )
    data_ways = lax.axis_size("dp")
    p_mean = lax.psum(p_local, "dp") / data_ways
    gram_matrix = jnp.dot(p_mean, p_mean.T, precision=HIGH_PRECISION)
    lower_factor = jnp.linalg.cholesky(gram_matrix)
    p_orth = jax.scipy.linalg.solve_triangular(lower_factor, p_mean, lower=True)
    q_local = lax.dot_general(
        merged, p_orth, contract_last, precision=HIGH_PRECISION, preferred_element_type=jnp.float32
    )
    q_group = lax.psum(q_local, "dp") / data_ways
    approximation = jnp.dot(q_group, p_orth, precision=HIGH_PRECISION)
    new_error = (merged - approximation).astype(jnp.bfloat16).reshape(error_fb.shape)
    return (d_tokens, new_error, q_group.reshape(q_prev.shape))


def solution(mesh):
    return jax.shard_map(
        on_device,
        mesh=mesh,
        in_specs=(
            P("dp", "tensor"),
            P("tensor", None),
            P("tensor", None),
            P("dp", "tensor"),
            P("dp", None, "tensor", None),
            P(None, "tensor", None),
        ),
        out_specs=(P("dp", "tensor"), P("dp", None, "tensor", None), P(None, "tensor", None)),
        check_vma=False,
    )
```

profile of v0, /device:TPU:1, one launch (start us, length us, event | category | flops | bytes accessed | tf_op | source)
XLA Modules:
  0.0 546.6 jit_solution(7963657524135838168)
XLA Ops:
  7.2 0.7 all-gather.2.cloned.1.call-update
  8.0 0.9 copy.11
  8.9 0.1 reshape.41
  9.0 53.5 %all-gather.2.cloned.1.call-done = bf16[384,4096]{1,0:T(8,128)(2,1)} async-done(((bf16[384,512]{1,0:T(8,128)(2,1)}), bf16[384,4096]{1,0:T(8,128)(2,1)}) %all-gather.2.cloned.1.call-update) | async-done | bytes 3145744 | tf_op jit(solution)/shard_map/all_gather | solution.py:14
  62.5 3.1 fusion.20
  65.6 0.7 fusion.17
  66.3 0.4 copy-done.4
  66.7 1.1 fusion.3
  67.8 0.7 fusion.22
  68.5 0.6 copy-done.3
  69.1 0.5 maximum_multiply_fusion
  69.7 0.3 convert_add_fusion
  69.9 2.6 convolution_bitcast_fusion
  72.5 0.2 all-reduce.3.cloned.1.call-start
  72.8 1.0 fusion.21
  73.8 0.1 copy-done.5
  73.9 2.7 add_convert_fusion
  76.6 191.3 %all-reduce.5.cloned.1.call-done = f32[64,4096]{1,0:T(8,128)} async-done(((f32[64,4096]{1,0:T(8,128)}), f32[64,4096]{1,0:T(8,128)}) %all-reduce.5.cloned.1.call-update) | async-done | bytes 1048592 | tf_op jit(solution)/shard_map/psum | solution.py:47
  267.9 2.7 fusion.6
  270.6 0.1 copy.12
  270.7 5.8 %cholesky.16 = f32[64,64]{1,0:T(8,128)S(1)} custom-call(f32[64,64]{1,0:T(8,128)S(1)} %fusion.14), custom_call_target="Cholesky" | custom-call | tf_op jit(solution)/shard_map/jit(cholesky)/cholesky | solution.py:49
  276.5 0.6 compare_reduce_fusion
  277.2 0.7 fusion.12
  277.8 4.9 custom-call.7
  282.7 2.3 fusion.4
  285.1 1.0 copy-done.2
  286.0 2.7 fusion.23
  288.7 244.3 %psum.23 = f32[160,64]{0,1:T(8,128)S(1)} all-reduce(f32[160,64]{0,1:T(8,128)S(1)} %fusion.23), channel_id=1, replica_groups=mesh['dp'=64,'tensor'=8] {'dp'}, use_global_device_ids=true, to_apply=%region_4.5 | all-reduce | flops 10240 | bytes 81920 | tf_op jit(solution)/shard_map/psum | solution.py:54
  533.0 0.1 reshape.43
  533.1 0.6 copy.13
  533.7 4.6 fusion
  538.3 1.8 convert_convert_fusion
  (20 shorter events, 0.2 us)
Async XLA Ops:
  7.2 55.3 %copy-start = (bf16[80,4096]{1,0:T(8,128)(2,1)S(1)}, bf16[80,4096]{1,0:T(8,128)(2,1)}, u32[]{:S(2)}) copy-start(bf16[80,4096]{1,0:T(8,128)(2,1)} %param.7) | copy-start | bytes 1966084
  7.2 55.3 %all-gather.2.cloned.1.call-start = ((), (), s32[]{:S(2)}) async-start(), calls=%async_computation | async-start | bytes 3538944 | tf_op jit(solution)/shard_map/all_gather | solution.py:14
  7.9 57.7 %copy-start.6 = (bf16[384,80]{0,1:T(8,128)(2,1)S(1)}, bf16[384,80]{0,1:T(8,128)(2,1)}, u32[]{:S(2)}) copy-start(bf16[384,80]{0,1:T(8,128)(2,1)} %param.9) | copy-start | bytes 184324
  7.9 260.0 %all-reduce.5.cloned.1.call-start = ((), (), s32[]{:S(2)}) async-start(), calls=%async_computation.2 | async-start | bytes 2097152 | tf_op jit(solution)/shard_map/psum | solution.py:47
  62.5 3.1 copy-start.1
  65.6 1.1 copy-start.4
  67.8 1.3 copy-start.3
  72.5 1.3 copy-start.7
  72.5 465.8 %all-reduce.3.cloned.1.call-start = ((), (), s32[]{:S(2)}) async-start(), calls=%async_computation.1 | async-start | bytes 6291456 | tf_op jit(solution)/shard_map/psum | solution.py:24
  72.8 1.1 copy-start.5
  285.0 1.0 copy-start.2
Sparse Core Ops, SparseCore 0:
  10.1 52.3 all-gather.1
  72.7 195.1 all-reduce.4
  270.4 94.6 all-reduce.2
where the time goes:
time: 551 us; the launch traced here: 547 us
  waiting for transfers between devices  246 us (45%)
  blocking collectives  244 us (44%)
  matrix products  24.1 us (4%)
  other arithmetic  14.7 us (3%)
  between operations  13.9 us (3%)
    psum x1, blocking collectives, on_device(): q_group = lax.psum(q_local, 'dp') / data_ways  244 us
    psum x1, waiting for transfers between devices, on_device(): p_mean = lax.psum(p_local, 'dp') / data_ways  191 us
    all_gather x1, waiting for transfers between devices, on_device(): whole = lax.all_gather(tokens, 'tensor', axis=1, tiled=True)  53.5 us
  transfers between devices with their start and end apart: 3, of which 2 were waited for; matrix products, arithmetic and copies ran while one was open for 5% of the time, Pallas kernels for 0%

commit v1 on v0

v1 whole, which is shorter than its diff:
```python
import math

import jax
import jax.numpy as jnp
from jax import lax
from jax.sharding import Mesh, PartitionSpec as P

HIGH_PRECISION = lax.Precision.HIGHEST
LANES = 128


def mean_over_workers(local, workers):
    chips = ("x", "z")
    n_chips = lax.axis_size(chips)
    rows, width = local.shape[0] // 2, local.shape[1]
    piece = width // n_chips
    core = lax.axis_index("core")
    halves = local.reshape(2, rows, width)
    mine = lax.dynamic_index_in_dim(halves, core, 0, keepdims=False)
    other = lax.dynamic_index_in_dim(halves, 1 - core, 0, keepdims=False)
    got = lax.ppermute(other.astype(jnp.bfloat16), "core", [(0, 1), (1, 0)])
    pair = (mine.astype(jnp.float32) + got.astype(jnp.float32)).astype(jnp.bfloat16)
    pieces = pair.reshape(rows, n_chips, piece).transpose(1, 0, 2)
    pieces = lax.all_to_all(pieces, chips, 0, 0, tiled=True)
    total = jnp.sum(pieces.astype(jnp.float32), 0) * (1.0 / workers)
    copies = jnp.broadcast_to(total.astype(jnp.bfloat16)[None], (n_chips, rows, piece))
    gathered = lax.all_to_all(copies, chips, 0, 0, tiled=True)
    half = gathered.transpose(1, 0, 2).reshape(rows, width)
    return lax.all_gather(half, "core", axis=0, tiled=True).astype(jnp.float32)


def on_device(tokens, w_gate, w_up, d_hidden, error_fb, q_prev):
    contract_last = (((1,), (1,)), ((), ()))
    contract_first = (((0,), (0,)), ((), ()))
    whole = lax.all_gather(tokens, "tensor", axis=1, tiled=True)
    gate_pre = lax.dot_general(whole, w_gate, contract_last, preferred_element_type=jnp.float32)
    up_pre = lax.dot_general(whole, w_up, contract_last, preferred_element_type=jnp.float32)
    squash = jax.nn.sigmoid(gate_pre)
    upstream = d_hidden.astype(jnp.float32)
    d_gate = (upstream * up_pre * squash * (1.0 + gate_pre * (1.0 - squash))).astype(jnp.bfloat16)
    d_up = (upstream * gate_pre * squash).astype(jnp.bfloat16)
    act_terms = jnp.dot(d_gate, w_gate, preferred_element_type=jnp.float32) + jnp.dot(
        d_up, w_up, preferred_element_type=jnp.float32
    )
    d_tokens = lax.psum_scatter(act_terms.astype(jnp.bfloat16), "tensor", scatter_dimension=1, tiled=True)
    grads = jnp.concatenate(
        [
            lax.dot_general(d_gate, whole, contract_first, preferred_element_type=jnp.float32),
            lax.dot_general(d_up, whole, contract_first, preferred_element_type=jnp.float32),
        ],
        0,
    )
    grad_scale = 1.0 / math.sqrt(whole.shape[0])
    merged = grads * grad_scale + error_fb.reshape(grads.shape).astype(jnp.float32)
    q_matrix = q_prev.reshape(grads.shape[0], q_prev.shape[2])
    mean = mean_over_workers(merged, lax.axis_size(("x", "z", "core")))
    p_mean = lax.dot_general(
        q_matrix, mean, contract_first, precision=HIGH_PRECISION, preferred_element_type=jnp.float32
    )
    gram_matrix = jnp.dot(p_mean, p_mean.T, precision=HIGH_PRECISION)
    lower_factor = jnp.linalg.cholesky(gram_matrix)
    p_orth = jax.scipy.linalg.solve_triangular(lower_factor, p_mean, lower=True)
    q_group = lax.dot_general(
        mean, p_orth, contract_last, precision=HIGH_PRECISION, preferred_element_type=jnp.float32
    )
    approximation = jnp.dot(q_group, p_orth, precision=HIGH_PRECISION)
    new_error = (merged - approximation).astype(jnp.bfloat16).reshape(error_fb.shape)
    return (d_tokens, new_error, q_group.reshape(q_prev.shape))


def solution(mesh):
    chips_apart = Mesh(mesh.devices.reshape(4, 8, 2, 8), ("x", "z", "core", "tensor"))
    dp = ("x", "z", "core")
    return jax.shard_map(
        on_device,
        mesh=chips_apart,
        in_specs=(
            P(dp, "tensor"),
            P("tensor", None),
            P("tensor", None),
            P(dp, "tensor"),
            P(dp, None, "tensor", None),
            P(None, "tensor", None),
        ),
        out_specs=(P(dp, "tensor"), P(dp, None, "tensor", None), P(None, "tensor", None)),
        check_vma=False,
    )
```

time: 551 us -> 207 us (0.38)
  blocking collectives: 244 us -> 51.1 us
  waiting for transfers between devices: 246 us -> 93.6 us
    psum x1 -> x0, blocking collectives: 244 us -> none  [on_device(): q_group = lax.psum(q_local, 'dp') / data_ways]
    psum x2 -> x0, waiting for transfers between devices: 191 us -> none  [the longest x1 191 us: on_device(): p_mean = lax.psum(p_local, 'dp') / data_ways]
    all_to_all x0 -> x2, blocking collectives: none -> 51.1 us  [the longest x1 26.6 us: mean_over_workers(): pieces = lax.all_to_all(pieces, chips, 0, 0, tiled=True)]
    reduce_scatter x0 -> x1, waiting for transfers between devices: none -> 24.3 us  [on_device(): lax.psum_scatter(act_terms.astype(jnp.bfloat16), 'tensor', scatter_dimens...]
    all_gather x0 -> x1, waiting for transfers between devices: none -> 12 us  [mean_over_workers(): return lax.all_gather(half, 'core', axis=0, tiled=True).astype(jnp.float32)]
  transfers between devices with their start and end apart: 3 -> 4, of which waited for: 2 -> 4; matrix products, arithmetic and copies ran while one was open for 5% -> 14% of each run, Pallas kernels for 0% -> 0%
where the time goes in v1:
time: 207 us; the launch traced here: 205 us
  waiting for transfers between devices  93.6 us (45%)
  blocking collectives  51.1 us (25%)
  matrix products  20.8 us (10%)
  other arithmetic  15.8 us (8%)
  between operations  13.9 us (7%)
  local copies, waits for them, and re-layouts  6 us (3%)
  starting transfers between devices  3.46 us (2%)
    all_gather x1, waiting for transfers between devices, on_device(): whole = lax.all_gather(tokens, 'tensor', axis=1, tiled=True)  54.5 us
    all_to_all x1, blocking collectives, mean_over_workers(): pieces = lax.all_to_all(pieces, chips, 0, 0, tiled=True)  26.6 us
    all_to_all x1, blocking collectives, mean_over_workers(): gathered = lax.all_to_all(copies, chips, 0, 0, tiled=True)  24.5 us
    reduce_scatter x1, waiting for transfers between devices, on_device(): lax.psum_scatter(act_terms.astype(jnp.bfloat16), 'tensor', scatter_dimens...  24.3 us
    all_gather x1, waiting for transfers between devices, mean_over_workers(): return lax.all_gather(half, 'core', axis=0, tiled=True).astype(jnp.float32)  12 us
    another operation x3, other arithmetic, on_device(): lower_factor = jnp.linalg.cholesky(gram_matrix)  6.52 us
    another operation x2, other arithmetic, on_device(): p_orth = jax.scipy.linalg.solve_triangular(lower_factor, p_mean, lower=True)  5.55 us
    dot_general x1, matrix products, on_device(): approximation = jnp.dot(q_group, p_orth, precision=HIGH_PRECISION)  4.58 us
  transfers between devices with their start and end apart: 4, of which 4 were waited for; matrix products, arithmetic and copies ran while one was open for 14% of the time, Pallas kernels for 0%

profile of v1, /device:TPU:1, one launch (start us, length us, event | category | flops | bytes accessed | tf_op | source)
XLA Modules:
  0.0 204.6 jit_solution(2318908216291393326)
XLA Ops:
  7.2 0.7 all-gather.3.cloned.1.call-update
  8.0 54.5 %all-gather.3.cloned.1.call-done = bf16[384,4096]{1,0:T(8,128)(2,1)} async-done(((bf16[384,512]{1,0:T(8,128)(2,1)}), bf16[384,4096]{1,0:T(8,128)(2,1)}) %all-gather.3.cloned.1.call-update) | async-done | bytes 3145744 | tf_op jit(solution)/shard_map/all_gather | solution.py:35
  62.5 3.1 %fusion.16 = f32[384,80]{0,1:T(8,128)S(1)} fusion(bf16[384,4096]{1,0:T(8,128)(2,1)} %all-gather.3.cloned.1.call-done, bf16[80,4096]{1,0:T(8,128)(2,1)S(1)} %copy-done), kind=kOutput, calls=%fused_computation.33 | convolution fusion | flops 251658240 | bytes 3923968 | tf_op jit(solution)/shard_map/dot_general | solution.py:36
  65.6 0.7 fusion.13
  66.4 0.4 copy-done.5
  66.7 1.1 fusion.4
  67.8 0.7 fusion.18
  68.5 0.6 copy-done.4
  69.1 2.1 %maximum_multiply_fusion = (f32[160,4096]{1,0:T(8,128)S(1)}, f32[160,4096]{1,0:T(8,128)}) fusion(f32[80,4096]{1,0:T(8,128)S(1)} %fusion.13, f32[80,4096]{1,0:T(8,128)S(1)} %fusion.18, bf16[1,2,80,4096]{3,2,1,0:T(8,128)(2,1)S(1)} %copy-done.4), kind=kLoop, calls=%fused_computation.3 | loop fusion | flops 2621440 | bytes 9175040 | tf_op jit(solution)/shard_map/mul | solution.py:54
  71.5 0.9 fusion.5
  72.4 3.2 %collective-permute-start = (bf16[80,4096]{1,0:T(8,128)(2,1)}, bf16[80,4096]{1,0:T(8,128)(2,1)}, u32[]{:S(2)}, u32[]{:S(2)}) collective-permute-start(bf16[80,4096]{1,0:T(8,128)(2,1)} %fusion.5), channel_id=1, source_target_pairs={{0,8},{8,0},{1,9},{9,1},{2,10},{10,2},{3,11},{11,3},{4,12},{12,4},... | collective-permute-start | bytes 1966088 | tf_op jit(solution)/shard_map/ppermute | solution.py:21
  75.6 2.0 collective-permute-done
  77.6 1.2 fusion.6
  79.2 26.6 %all_to_all.10 = bf16[32,80,128]{2,1,0:T(8,128)(2,1)S(1)} all-to-all(bf16[32,80,128]{2,1,0:T(8,128)(2,1)S(1)} %copy.18), channel_id=1, replica_groups=mesh['x'=4,'z'=8,'core'=2,'tensor'=8] {'x','z'}, dimensions={0} | all-to-all | bytes 1310720 | tf_op jit(solution)/shard_map/all_to_all | solution.py:24
  106.0 24.5 %all_to_all.11 = bf16[32,80,128]{2,1,0:T(8,128)(2,1)S(1)} all-to-all(bf16[32,80,128]{2,1,0:T(8,128)(2,1)S(1)} %broadcast_in_dim.3), channel_id=1, replica_groups=mesh['x'=4,'z'=8,'core'=2,'tensor'=8] {'x','z'}, dimensions={0} | all-to-all | bytes 1310720 | tf_op jit(solution)/shard_map/all_to_all | solution.py:27
  130.6 0.9 copy_bitcast_fusion
  131.7 1.0 fusion.17
  132.7 2.7 %add_convert_fusion = bf16[384,4096]{1,0:T(8,128)(2,1)} fusion(f32[384,4096]{1,0:T(8,128)S(1)} %fusion.17, bf16[80,4096]{1,0:T(8,128)(2,1)S(1)} %copy-done.6, f32[384,80]{0,1:T(8,128)S(1)} %fusion.16, bf16[384,80]{0,1:T(8,128)(2,1)S(1)} %copy-done.7), kind=kOutput, calls=%fused_computation | convolution fusion | flops 255019008 | bytes 10276864 | tf_op jit(solution)/shard_map/dot_general | solution.py:42
  135.4 0.8 copy-done.8
  136.4 12.0 %all-gather.5.cloned.1.call-done = bf16[160,4096]{1,0:T(8,128)(2,1)} async-done(((bf16[80,4096]{1,0:T(8,128)(2,1)}), bf16[160,4096]{1,0:T(8,128)(2,1)}) %all-gather.5.cloned.1.call-update) | async-done | bytes 1310736 | tf_op jit(solution)/shard_map/all_gather | solution.py:29
  148.4 2.0 fusion.19
  150.3 1.0 fusion.20
  151.4 5.8 %cholesky.16 = f32[64,64]{1,0:T(8,128)S(1)} custom-call(f32[64,64]{1,0:T(8,128)S(1)} %fusion.12), custom_call_target="Cholesky" | custom-call | tf_op jit(solution)/shard_map/jit(cholesky)/cholesky | solution.py:61
  157.3 0.6 compare_reduce_fusion
  157.9 0.7 fusion.9
  158.6 4.9 %custom-call.7 = f32[1,64,64]{1,2,0:T(8,128)S(1)} custom-call(f32[1,64,64]{2,1,0:T(8,128)S(1)} %fusion.9), custom_call_target="InvertDiagBlocksLowerTriangular" | custom-call | tf_op jit(solution)/shard_map/jit(_solve_triangular)/triangular_solve | solution.py:62
  163.5 1.0 fusion.10
  164.6 1.0 copy-done.3
  165.5 2.9 %fusion.21 = f32[160,64]{0,1:T(8,128)S(1)} fusion(bf16[160,4096]{1,0:T(8,128)(2,1)} %all-gather.5.cloned.1.call-done, f32[64,4096]{1,0:T(8,128)S(1)} %fusion.10), kind=kOutput, calls=%fused_computation.38 | convolution fusion | flops 503316480 | bytes 2400256 | tf_op jit(solution)/shard_map/dot_general | solution.py:63
  168.6 0.6 copy.22
  169.2 4.6 %fusion = bf16[160,4096]{1,0:T(8,128)(2,1)} fusion(f32[160,4096]{1,0:T(8,128)S(1)} %copy-done.2, f32[160,64]{0,1:T(8,128)S(1)} %fusion.21, f32[64,4096]{1,0:T(8,128)} %copy-done.3), kind=kOutput, calls=%fused_computation.2 | convolution fusion | flops 504627200 | bytes 5021696 | tf_op jit(solution)/shard_map/dot_general | solution.py:66
  173.8 24.3 %reduce-scatter.2.cloned.1.call-done = bf16[384,512]{1,0:T(8,128)(2,1)} async-done(((bf16[384,4096]{1,0:T(8,128)(2,1)}), bf16[384,512]{1,0:T(8,128)(2,1)}) %reduce-scatter.2.cloned.1.call-update) | async-done | bytes 393232 | tf_op jit(solution)/shard_map/reduce_scatter | solution.py:45
  (31 shorter events, 1.6 us)
Async XLA Ops:
  7.2 55.3 %copy-start = (bf16[80,4096]{1,0:T(8,128)(2,1)S(1)}, bf16[80,4096]{1,0:T(8,128)(2,1)}, u32[]{:S(2)}) copy-start(bf16[80,4096]{1,0:T(8,128)(2,1)} %param.7) | copy-start | bytes 1966084
  7.2 58.4 %copy-start.7 = (bf16[384,80]{0,1:T(8,128)(2,1)S(1)}, bf16[384,80]{0,1:T(8,128)(2,1)}, u32[]{:S(2)}) copy-start(bf16[384,80]{0,1:T(8,128)(2,1)} %param.9) | copy-start | bytes 184324
  7.2 55.3 %all-gather.3.cloned.1.call-start = ((), (), s32[]{:S(2)}) async-start(), calls=%async_computation.3 | async-start | bytes 3538944 | tf_op jit(solution)/shard_map/all_gather | solution.py:35
  7.9 140.4 %all-gather.5.cloned.1.call-start = ((), (), s32[]{:S(2)}) async-start(), calls=%async_computation.5 | async-start | bytes 1966080 | tf_op jit(solution)/shard_map/all_gather | solution.py:29
  62.5 3.1 %copy-start.1 = (bf16[384,4096]{1,0:T(8,128)(2,1)S(1)}, bf16[384,4096]{1,0:T(8,128)(2,1)}, u32[]{:S(2)}) copy-start(bf16[384,4096]{1,0:T(8,128)(2,1)} %all-gather.3.cloned.1.call-done) | copy-start | bytes 9437188
  65.6 1.1 copy-start.5
  67.8 1.3 copy-start.4
  72.4 5.2 %collective-permute-start = (bf16[80,4096]{1,0:T(8,128)(2,1)}, bf16[80,4096]{1,0:T(8,128)(2,1)}, u32[]{:S(2)}, u32[]{:S(2)}) collective-permute-start(bf16[80,4096]{1,0:T(8,128)(2,1)} %fusion.5), channel_id=1, source_target_pairs={{0,8},{8,0},{1,9},{9,1},{2,10},{10,2},{3,11},{11,3},{4,12},{12,4},... | collective-permute-start | bytes 1966088 | tf_op jit(solution)/shard_map/ppermute | solution.py:21
  131.5 1.2 copy-start.6
  131.5 66.6 %reduce-scatter.2.cloned.1.call-start = ((), (), s32[]{:S(2)}) async-start(), calls=%async_computation.4 | async-start | bytes 3538944 | tf_op jit(solution)/shard_map/reduce_scatter | solution.py:45
  135.4 0.8 copy-start.8
  164.6 1.0 copy-start.3
  165.5 3.7 %copy-start.2 = (f32[160,4096]{1,0:T(8,128)S(1)}, f32[160,4096]{1,0:T(8,128)}, u32[]{:S(2)}) copy-start(f32[160,4096]{1,0:T(8,128)} %get-tuple-element.16) | copy-start | bytes 7864324
Sparse Core Ops, SparseCore 0:
  10.1 52.3 all-gather.2
  131.6 16.7 all-gather.4
  151.8 46.2 reduce-scatter.1

commit v2 on v1

v2 whole, which is shorter than its diff:
```python
import functools
import math

import jax
import jax.numpy as jnp
from jax import lax
from jax.experimental import pallas as pl
from jax.experimental.pallas import tpu as pltpu
from jax.sharding import Mesh, PartitionSpec as P

HIGH_PRECISION = lax.Precision.HIGHEST
CHIPS = ("x", "z")
SWAP = ((0, 1), (1, 0))
VMEM_BYTES = 50 * 1024 * 1024


def three_parts(value):
    high = value.astype(jnp.bfloat16)
    rest = value - high.astype(jnp.float32)
    middle = rest.astype(jnp.bfloat16)
    low = (rest - middle.astype(jnp.float32)).astype(jnp.bfloat16)
    return high, middle, low


def inverse_cholesky(gram):
    n = gram.shape[0]
    row_ids = lax.broadcasted_iota(jnp.int32, (n, n), 0)
    col_ids = lax.broadcasted_iota(jnp.int32, (n, n), 1)
    eye = jnp.where(row_ids == col_ids, 1.0, 0.0)
    work = jnp.concatenate([gram, eye], 1)
    blocks = [work[8 * k : 8 * k + 8] for k in range(n // 8)]
    below = lax.broadcasted_iota(jnp.int32, (8, 2 * n), 0)
    for j in range(n - 1):
        k, i = divmod(j, 8)
        row = blocks[k][i : i + 1]
        scaled = row * (1.0 / row[:, j : j + 1])
        for b in range(k, n // 8):
            factor = jnp.broadcast_to(blocks[b][:, j : j + 1], (8, 2 * n))
            if b == k:
                factor = jnp.where(below > i, factor, 0.0)
            blocks[b] = blocks[b] - factor * scaled
    work = jnp.concatenate(blocks, 0)
    pivots = jnp.sum(jnp.where(row_ids == col_ids, work[:, :n], 0.0), 1, keepdims=True)
    return work[:, n:] * lax.rsqrt(pivots)


def finish_kernel(core_ref, own_ref, other_ref, q_ref, merged_ref, new_ref, q_next_ref, stack_ref):
    chunks, rows, lanes = own_ref.shape
    units, rank = 2 * rows, q_ref.shape[1]
    first = core_ref[0] == 0
    for j in range(chunks):
        at = slice(j * lanes, (j + 1) * lanes)
        stack_ref[0:rows, at] = jnp.where(first, own_ref[j], other_ref[j])
        stack_ref[rows:units, at] = jnp.where(first, other_ref[j], own_ref[j])
    q_gate = jnp.concatenate(three_parts(q_ref[0]), 0)
    q_up = jnp.concatenate(three_parts(q_ref[1]), 0)
    width = chunks * lanes
    step = 1024
    for f in range(0, width, step):
        p_parts = jnp.dot(q_gate, stack_ref[0:rows, f : f + step], preferred_element_type=jnp.float32)
        p_parts += jnp.dot(q_up, stack_ref[rows:units, f : f + step], preferred_element_type=jnp.float32)
        p_mean = p_parts[0:rank] + p_parts[rank : 2 * rank] + p_parts[2 * rank :]
        for k, part in enumerate(three_parts(p_mean)):
            stack_ref[units + k * rank : units + (k + 1) * rank, f : f + step] = part
    products = lax.dot_general(
        stack_ref[...], stack_ref[units:, :], (((1,), (1,)), ((), ())), preferred_element_type=jnp.float32
    )
    products = products[:, 0:rank] + products[:, rank : 2 * rank] + products[:, 2 * rank :]
    gram = products[units : units + rank] + products[units + rank : units + 2 * rank] + products[units + 2 * rank :]
    inverse = inverse_cholesky(gram)
    for k in range(2):
        q_next_ref[k] = lax.dot_general(
            inverse, products[k * rows : (k + 1) * rows], (((1,), (1,)), ((), ())),
            precision=HIGH_PRECISION, preferred_element_type=jnp.float32,
        )
    gram_inverse = jnp.dot(inverse.T, inverse, precision=HIGH_PRECISION, preferred_element_type=jnp.float32)
    weights = jnp.dot(
        products[0:units], gram_inverse, precision=HIGH_PRECISION, preferred_element_type=jnp.float32
    )
    high, middle, _ = three_parts(weights)
    factors = jnp.concatenate([high, high, middle], 1)
    for f in range(0, width, step):
        p_high = stack_ref[units : units + rank, f : f + step]
        p_middle = stack_ref[units + rank : units + 2 * rank, f : f + step]
        basis = jnp.concatenate([p_high, p_middle, p_high], 0)
        approximation = jnp.dot(factors, basis, preferred_element_type=jnp.float32)
        fresh = (merged_ref[:, f : f + step] - approximation).astype(jnp.bfloat16)
        new_ref[0, :, f : f + step] = fresh[0:rows]
        new_ref[1, :, f : f + step] = fresh[rows:]


def finish(core, own, other, q_prev, merged):
    rows = own.shape[1]
    width = own.shape[0] * own.shape[2]
    rank = q_prev.shape[2]
    vmem = pl.BlockSpec(memory_space=pltpu.VMEM)
    return pl.pallas_call(
        finish_kernel,
        out_shape=(
            jax.ShapeDtypeStruct((2, rows, width), jnp.bfloat16),
            jax.ShapeDtypeStruct((2, rank, rows), jnp.float32),
        ),
        in_specs=[pl.BlockSpec(memory_space=pltpu.SMEM), vmem, vmem, vmem, vmem],
        out_specs=(vmem, vmem),
        scratch_shapes=[pltpu.VMEM((2 * rows + 3 * rank, width), jnp.bfloat16)],
        compiler_params=pltpu.CompilerParams(vmem_limit_bytes=VMEM_BYTES),
        name="finish",
    )(core.reshape(1), own, other, q_prev.transpose(0, 2, 1), merged)


def gradient_kernel(core_ref, tokens_hbm, gate_ref, up_ref, cot_ref, error_ref, d_ref, send_ref, keep_ref, merged_ref, tokens_ref, sems, *, scale):
    parts = sems.shape[0]
    rows, width = gate_ref.shape
    step = width // parts
    chunks, _, lanes = send_ref.shape

    def load(k):
        at = pl.ds(k * step, step)
        return pltpu.make_async_copy(tokens_hbm.at[:, at], tokens_ref.at[:, at], sems.at[k])

    for k in range(parts):
        load(k).start()
    pre = jnp.zeros((2 * rows, tokens_ref.shape[0]), jnp.float32)
    for k in range(parts):
        load(k).wait()
        at = slice(k * step, (k + 1) * step)
        weights = jnp.concatenate([gate_ref[:, at], up_ref[:, at]], 0)
        pre += lax.dot_general(
            weights, tokens_ref[:, at], (((1,), (1,)), ((), ())), preferred_element_type=jnp.float32
        )
    gate_pre, up_pre = pre[0:rows], pre[rows:]
    squash = jax.nn.sigmoid(gate_pre)
    upstream = cot_ref[...].astype(jnp.float32)
    d_gate = (upstream * up_pre * squash * (1.0 + gate_pre * (1.0 - squash))).astype(jnp.bfloat16)
    d_up = (upstream * gate_pre * squash).astype(jnp.bfloat16)
    d_both = jnp.concatenate([d_gate, d_up], 0)
    d_ref[...] = d_both
    first = core_ref[0] == 0
    step = 512
    for f in range(0, width, step):
        at = slice(f, f + step)
        grads = jnp.dot(d_both, tokens_ref[:, at], preferred_element_type=jnp.float32) * scale
        gate_half = grads[0:rows] + error_ref[0, :, at].astype(jnp.float32)
        up_half = grads[rows:] + error_ref[1, :, at].astype(jnp.float32)
        merged_ref[0:rows, at] = gate_half
        merged_ref[rows:, at] = up_half
        keep = jnp.where(first, gate_half, up_half)
        send = jnp.where(first, up_half, gate_half).astype(jnp.bfloat16)
        for i in range(step // lanes):
            part = slice(i * lanes, (i + 1) * lanes)
            keep_ref[f // lanes + i] = keep[:, part]
            send_ref[f // lanes + i] = send[:, part]


def gradients(core, whole, w_gate, w_up, cot, error_fb, n_chips):
    count, width = whole.shape
    rows = w_gate.shape[0]
    lanes = width // n_chips
    vmem = pl.BlockSpec(memory_space=pltpu.VMEM)
    return pl.pallas_call(
        functools.partial(gradient_kernel, scale=1.0 / math.sqrt(count)),
        out_shape=(
            jax.ShapeDtypeStruct((2 * rows, count), jnp.bfloat16),
            jax.ShapeDtypeStruct((n_chips, rows, lanes), jnp.bfloat16),
            jax.ShapeDtypeStruct((n_chips, rows, lanes), jnp.float32),
            jax.ShapeDtypeStruct((2 * rows, width), jnp.float32),
        ),
        in_specs=[pl.BlockSpec(memory_space=pltpu.SMEM), pl.BlockSpec(memory_space=pl.ANY)] + [vmem] * 4,
        out_specs=(vmem,) * 4,
        scratch_shapes=[pltpu.VMEM((count, width), jnp.bfloat16), pltpu.SemaphoreType.DMA((8,))],
        compiler_params=pltpu.CompilerParams(vmem_limit_bytes=VMEM_BYTES),
        name="gradients",
    )(core.reshape(1), whole, w_gate, w_up, cot.T, error_fb.reshape(2, rows, width))


def act_kernel(d_ref, gate_ref, up_ref, act_ref):
    d_both = d_ref[...].T
    step = 1024
    for f in range(0, act_ref.shape[1], step):
        at = slice(f, f + step)
        weights = jnp.concatenate([gate_ref[:, at], up_ref[:, at]], 0)
        act_ref[:, at] = jnp.dot(d_both, weights, preferred_element_type=jnp.float32).astype(jnp.bfloat16)


def act_terms(d_both, w_gate, w_up):
    vmem = pl.BlockSpec(memory_space=pltpu.VMEM)
    return pl.pallas_call(
        act_kernel,
        out_shape=jax.ShapeDtypeStruct((d_both.shape[1], w_gate.shape[1]), jnp.bfloat16),
        in_specs=[vmem] * 3,
        out_specs=vmem,
        compiler_params=pltpu.CompilerParams(vmem_limit_bytes=VMEM_BYTES),
        name="act_terms",
    )(d_both, w_gate, w_up)


def mean_kernel(pieces_ref, copies_ref, *, scale):
    total = pieces_ref[0].astype(jnp.float32)
    for k in range(1, pieces_ref.shape[0]):
        total += pieces_ref[k].astype(jnp.float32)
    mean = (total * scale).astype(jnp.bfloat16)
    for k in range(copies_ref.shape[0]):
        copies_ref[k] = mean


def mean_copies(pieces, workers):
    vmem = pl.BlockSpec(memory_space=pltpu.VMEM)
    return pl.pallas_call(
        functools.partial(mean_kernel, scale=1.0 / workers),
        out_shape=jax.ShapeDtypeStruct(pieces.shape, jnp.bfloat16),
        in_specs=[vmem],
        out_specs=vmem,
        compiler_params=pltpu.CompilerParams(vmem_limit_bytes=VMEM_BYTES),
        name="mean_copies",
    )(pieces)


def on_device(tokens, w_gate, w_up, d_hidden, error_fb, q_prev):
    core = lax.axis_index("core")
    n_chips = lax.axis_size(CHIPS)
    whole = lax.all_gather(tokens, "tensor", axis=1, tiled=True)
    d_both, send, keep, merged = gradients(core, whole, w_gate, w_up, d_hidden, error_fb, n_chips)
    act = act_terms(d_both, w_gate, w_up)
    got = lax.ppermute(send, "core", SWAP)
    pieces = (keep + got.astype(jnp.float32)).astype(jnp.bfloat16)
    pieces, act = lax.optimization_barrier((pieces, act))
    d_tokens = lax.psum_scatter(act, "tensor", scatter_dimension=1, tiled=True)
    pieces = lax.all_to_all(pieces, CHIPS, 0, 0, tiled=True)
    copies = mean_copies(pieces, n_chips * lax.axis_size("core"))
    own_half = lax.all_to_all(copies, CHIPS, 0, 0, tiled=True)
    other_half = lax.ppermute(own_half, "core", SWAP)
    new_error, q_next = finish(core, own_half, other_half, q_prev, merged)
    return (d_tokens, new_error.reshape(error_fb.shape), q_next.transpose(0, 2, 1))


def solution(mesh):
    chips_apart = Mesh(mesh.devices.reshape(4, 8, 2, 8), ("x", "z", "core", "tensor"))
    dp = ("x", "z", "core")
    return jax.shard_map(
        on_device,
        mesh=chips_apart,
        in_specs=(
            P(dp, "tensor"),
            P("tensor", None),
            P("tensor", None),
            P(dp, "tensor"),
            P(dp, None, "tensor", None),
            P(None, "tensor", None),
        ),
        out_specs=(P(dp, "tensor"), P(dp, None, "tensor", None), P(None, "tensor", None)),
        check_vma=False,
    )
```

time: 207 us -> 156 us (0.75)
  waiting for transfers between devices: 93.6 us -> 56.9 us
  matrix products: 20.8 us -> 0 us
  Pallas kernels: 0 us -> 19.9 us
  other arithmetic: 15.8 us -> 0.13 us
  starting transfers between devices: 3.46 us -> 10.1 us
  local copies, waits for them, and re-layouts: 6 us -> 3.02 us
    reduce_scatter x1, waiting for transfers between devices: 24.3 us -> 0.01 us  [on_device(): d_tokens = lax.psum_scatter(act, 'tensor', scatter_dimension=1, tiled=True)]
    pallas_call x0 -> x4, Pallas kernels: none -> 19.9 us  [the longest x1 10.4 us: finish(): pl.pallas_call(finish_kernel, out_shape=(jax.ShapeDtypeStruct((2, rows, w...]
    dot_general x10 -> x0, matrix products: 19.7 us -> none  [the longest x1 4.58 us: on_device(): approximation = jnp.dot(q_group, p_orth, precision=HIGH_PRECISION)]
    another operation x5 -> x0, other arithmetic: 12.1 us -> none  [the longest x3 6.52 us: on_device(): lower_factor = jnp.linalg.cholesky(gram_matrix)]
    all_gather x1 -> x0, waiting for transfers between devices: 12 us -> none  [mean_over_workers(): return lax.all_gather(half, 'core', axis=0, tiled=True).astype(jnp.float32)]
    ppermute x1 -> x2, starting transfers between devices: 3.17 us -> 10 us  [the longest x1 6.86 us: on_device(): other_half = lax.ppermute(own_half, 'core', SWAP)]
    mul x1 -> x0, other arithmetic: 2.07 us -> none  [on_device(): grads * grad_scale + error_fb.reshape(grads.shape).astype(jnp.float32)]
  transfers between devices with their start and end apart: 4 -> 4, of which waited for: 4 -> 2; matrix products, arithmetic and copies ran while one was open for 14% -> 0% of each run, Pallas kernels for 0% -> 8%
where the time goes in v2:
time: 156 us
  waiting for transfers between devices  56.9 us (36%)
  blocking collectives  51.4 us (33%)
  Pallas kernels  19.9 us (13%)
  between operations  14.1 us (9%)
  starting transfers between devices  10.1 us (6%)
  local copies, waits for them, and re-layouts  3.02 us (2%)
    all_gather x1, waiting for transfers between devices, on_device(): whole = lax.all_gather(tokens, 'tensor', axis=1, tiled=True)  54.5 us
    all_to_all x1, blocking collectives, on_device(): pieces = lax.all_to_all(pieces, CHIPS, 0, 0, tiled=True)  27.3 us
    all_to_all x1, blocking collectives, on_device(): own_half = lax.all_to_all(copies, CHIPS, 0, 0, tiled=True)  24 us
    pallas_call x1, Pallas kernels, finish(): pl.pallas_call(finish_kernel, out_shape=(jax.ShapeDtypeStruct((2, rows, w...  10.4 us
    ppermute x1, starting transfers between devices, on_device(): other_half = lax.ppermute(own_half, 'core', SWAP)  6.86 us
    pallas_call x1, Pallas kernels, gradients(): pl.pallas_call(functools.partial(gradient_kernel, scale=1.0 / math.sqrt(c...  6.78 us
    ppermute x1, starting transfers between devices, on_device(): got = lax.ppermute(send, 'core', SWAP)  3.18 us
  transfers between devices with their start and end apart: 4, of which 2 were waited for; matrix products, arithmetic and copies ran while one was open for 0% of the time, Pallas kernels for 8%

profile of v2, /device:TPU:1, one launch (start us, length us, event | category | flops | bytes accessed | tf_op | source)
XLA Modules:
  0.0 155.5 jit_solution(15161131548756107902)
XLA Ops:
  7.2 0.0 all-gather.2.cloned.1.call-start
  7.2 0.7 all-gather.2.cloned.1.call-update
  7.9 0.0 reduce-scatter.2.cloned.1.call-start
  7.9 54.5 %all-gather.2.cloned.1.call-done.tokens_hbm = bf16[384,4096]{1,0:T(8,128)(2,1)} async-done(((bf16[384,512]{1,0:T(8,128)(2,1)}), bf16[384,4096]{1,0:T(8,128)(2,1)}) %all-gather.2.cloned.1.call-update) | async-done | bytes 3145744 | tf_op jit(solution)/shard_map/all_gather | solution.py:221
  62.5 0.0 copy-start.1
  62.5 1.1 copy-done.1
  63.6 0.0 copy-start.3
  63.6 1.1 copy-done.3
  64.6 0.0 copy-start.6
  64.6 0.8 copy-done.6
  65.5 0.0 copy-start.2
  65.5 0.0 copy-start.4
  65.5 6.8 %gradients.1 = (bf16[160,384]{1,0:T(8,128)(2,1)S(1)}, bf16[32,80,128]{2,1,0:T(8,128)(2,1)S(1)}, f32[32,80,128]{2,1,0:T(8,128)S(1)}, f32[160,4096]{1,0:T(8,128)}) custom-call(s32[1]{0:T(128)} %bitcast.core_ref, bf16[384,4096]{1,0:T(8,128)(2,1)} %all-gather.2.cloned.1.call-done.tokens_hbm, bf16[80,4096]{1,0:T(8,128)(2,1)S(1)} %copy-done.1, ...), custom_call_target="tpu_custom_call" | custom-call | tf_op jit(solution)/shard_map/gradients/pallas_call | solution.py:160
  72.3 3.2 %collective-permute-start = (bf16[32,80,128]{2,1,0:T(8,128)(2,1)S(1)}, bf16[32,80,128]{2,1,0:T(8,128)(2,1)S(1)}, u32[]{:S(2)}, u32[]{:S(2)}) collective-permute-start(bf16[32,80,128]{2,1,0:T(8,128)(2,1)S(1)} %get-tuple-element.12), channel_id=1, source_target_pairs={{0,8},{8,0},{1,9},{9,1},{2,10},{10,2},{3,11},{11,3},{4,12},{12,4},... | collective-permute-start | bytes 1966088 | tf_op jit(solution)/shard_map/ppermute | solution.py:224
  75.5 0.0 copy-done.2
  75.5 0.0 copy-done.4
  75.5 2.6 %act_terms.1 = bf16[384,4096]{1,0:T(8,128)(2,1)} custom-call(bf16[160,384]{1,0:T(8,128)(2,1)S(1)} %get-tuple-element.13.d_ref, bf16[80,4096]{1,0:T(8,128)(2,1)S(1)} %copy-done.2, bf16[80,4096]{1,0:T(8,128)(2,1)S(1)} %copy-done.4), custom_call_target="tpu_custom_call" | custom-call | tf_op jit(solution)/shard_map/act_terms/pallas_call | solution.py:187
  78.1 0.0 collective-permute-done
  78.1 0.1 add_convert_fusion
  78.2 0.0 reduce-scatter.2.cloned.1.call-update
  78.3 0.0 copy-start.5
  78.3 27.3 %all_to_all.10.pieces_ref = bf16[32,80,128]{2,1,0:T(8,128)(2,1)S(1)} all-to-all(bf16[32,80,128]{2,1,0:T(8,128)(2,1)S(1)} %add_convert_fusion), channel_id=1, replica_groups=mesh['x'=4,'z'=8,'core'=2,'tensor'=8] {'x','z'}, dimensions={0} | all-to-all | bytes 1310720 | tf_op jit(solution)/shard_map/all_to_all | solution.py:228
  105.6 0.0 copy-start
  105.6 0.1 mean_copies.1
  105.7 24.0 %all_to_all.11.own_ref = bf16[32,80,128]{2,1,0:T(8,128)(2,1)S(1)} all-to-all(bf16[32,80,128]{2,1,0:T(8,128)(2,1)S(1)} %mean_copies.1), channel_id=1, replica_groups=mesh['x'=4,'z'=8,'core'=2,'tensor'=8] {'x','z'}, dimensions={0} | all-to-all | bytes 1310720 | tf_op jit(solution)/shard_map/all_to_all | solution.py:230
  129.8 6.9 %collective-permute-start.1 = (bf16[32,80,128]{2,1,0:T(8,128)(2,1)S(1)}, bf16[32,80,128]{2,1,0:T(8,128)(2,1)S(1)}, u32[]{:S(2)}, u32[]{:S(2)}) collective-permute-start(bf16[32,80,128]{2,1,0:T(8,128)(2,1)S(1)} %all_to_all.11.own_ref), channel_id=1, source_target_pairs={{0,8},{8,0},{1,9},{9,1},{2,10},{10,2},{3,11},{11,3},{4,12},{12,4},... | collective-permute-start | bytes 1966088 | tf_op jit(solution)/shard_map/ppermute | solution.py:231
  136.6 1.7 %collective-permute-done.1.other_ref = bf16[32,80,128]{2,1,0:T(8,128)(2,1)S(1)} collective-permute-done((bf16[32,80,128]{2,1,0:T(8,128)(2,1)S(1)}, bf16[32,80,128]{2,1,0:T(8,128)(2,1)S(1)}, u32[]{:S(2)}, u32[]{:S(2)}) %collective-permute-start.1) | collective-permute-done | bytes 655392 | tf_op jit(solution)/shard_map/ppermute | solution.py:231
  138.3 0.0 copy-done.5
  138.3 0.0 copy-done
  138.3 10.4 %finish.1 = (bf16[2,80,4096]{2,1,0:T(8,128)(2,1)}, f32[2,64,80]{2,1,0:T(8,128)}) custom-call(s32[1]{0:T(128)} %bitcast.core_ref, bf16[32,80,128]{2,1,0:T(8,128)(2,1)S(1)} %all_to_all.11.own_ref, bf16[32,80,128]{2,1,0:T(8,128)(2,1)S(1)} %collective-permute-done.1.other_ref, f32[2,64,80]{2,1,0:T(8,128)S(1)} %bitcast.6, f32[160,4096]{1,0:T(8,128)S(1)} %copy-done), custom_call_target="tpu_custom_call" | custom-call | tf_op jit(solution)/shard_map/finish/pallas_call | solution.py:97
  148.7 0.0 reduce-scatter.2.cloned.1.call-done
Async XLA Ops:
  7.2 55.3 %all-gather.2.cloned.1.call-start = ((), (), s32[]{:S(2)}) async-start(), calls=%async_computation.3 | async-start | bytes 3538944 | tf_op jit(solution)/shard_map/all_gather | solution.py:221
  7.9 140.8 %reduce-scatter.2.cloned.1.call-start = ((), (), s32[]{:S(2)}) async-start(), calls=%async_computation.4 | async-start | bytes 3538944 | tf_op jit(solution)/shard_map/reduce_scatter | solution.py:227
  62.5 1.1 copy-start.1
  63.6 1.1 copy-start.3
  64.6 0.8 copy-start.6
  65.5 10.0 %copy-start.2 = (bf16[80,4096]{1,0:T(8,128)(2,1)S(1)}, bf16[80,4096]{1,0:T(8,128)(2,1)}, u32[]{:S(2)}) copy-start(bf16[80,4096]{1,0:T(8,128)(2,1)} %gate_ref.3) | copy-start | bytes 1966084
  65.5 10.0 %copy-start.4 = (bf16[80,4096]{1,0:T(8,128)(2,1)S(1)}, bf16[80,4096]{1,0:T(8,128)(2,1)}, u32[]{:S(2)}) copy-start(bf16[80,4096]{1,0:T(8,128)(2,1)} %up_ref.3) | copy-start | bytes 1966084
  72.3 5.9 %collective-permute-start = (bf16[32,80,128]{2,1,0:T(8,128)(2,1)S(1)}, bf16[32,80,128]{2,1,0:T(8,128)(2,1)S(1)}, u32[]{:S(2)}, u32[]{:S(2)}) collective-permute-start(bf16[32,80,128]{2,1,0:T(8,128)(2,1)S(1)} %get-tuple-element.12), channel_id=1, source_target_pairs={{0,8},{8,0},{1,9},{9,1},{2,10},{10,2},{3,11},{11,3},{4,12},{12,4},... | collective-permute-start | bytes 1966088 | tf_op jit(solution)/shard_map/ppermute | solution.py:224
  78.3 60.1 %copy-start.5 = (f32[2,80,64]{1,2,0:T(8,128)S(1)}, f32[2,80,64]{1,2,0:T(8,128)}, u32[]{:S(2)}) copy-start(f32[2,80,64]{1,2,0:T(8,128)} %param.11) | copy-start | bytes 122884
  105.6 32.7 %copy-start = (f32[160,4096]{1,0:T(8,128)S(1)}, f32[160,4096]{1,0:T(8,128)}, u32[]{:S(2)}) copy-start(f32[160,4096]{1,0:T(8,128)} %get-tuple-element.16.merged_ref) | copy-start | bytes 7864324
  129.8 8.6 %collective-permute-start.1 = (bf16[32,80,128]{2,1,0:T(8,128)(2,1)S(1)}, bf16[32,80,128]{2,1,0:T(8,128)(2,1)S(1)}, u32[]{:S(2)}, u32[]{:S(2)}) collective-permute-start(bf16[32,80,128]{2,1,0:T(8,128)(2,1)S(1)} %all_to_all.11.own_ref), channel_id=1, source_target_pairs={{0,8},{8,0},{1,9},{9,1},{2,10},{10,2},{3,11},{11,3},{4,12},{12,4},... | collective-permute-start | bytes 1966088 | tf_op jit(solution)/shard_map/ppermute | solution.py:231
Sparse Core Ops, SparseCore 0:
  10.1 52.3 all-gather.1
  78.4 44.8 reduce-scatter.1

commit v3 on v2

--- a/solution.py
+++ b/solution.py
@@ -11,7 +11,7 @@
 HIGH_PRECISION = lax.Precision.HIGHEST
 CHIPS = ("x", "z")
 SWAP = ((0, 1), (1, 0))
-VMEM_BYTES = 50 * 1024 * 1024
+VMEM_BYTES = 24 * 1024 * 1024
 
 
 def three_parts(value):
@@ -44,10 +44,12 @@
     return work[:, n:] * lax.rsqrt(pivots)
 
 
-def finish_kernel(core_ref, own_ref, other_ref, q_ref, merged_ref, new_ref, q_next_ref, stack_ref):
+def finish_kernel(where_ref, own_ref, other_ref, q_ref, merged_hbm, new_ref, q_next_ref, stack_ref, merged_ref, sem):
+    load = pltpu.make_async_copy(merged_hbm, merged_ref, sem)
+    load.start()
     chunks, rows, lanes = own_ref.shape
     units, rank = 2 * rows, q_ref.shape[1]
-    first = core_ref[0] == 0
+    first = where_ref[0] == 0
     for j in range(chunks):
         at = slice(j * lanes, (j + 1) * lanes)
         stack_ref[0:rows, at] = jnp.where(first, own_ref[j], other_ref[j])
@@ -79,6 +81,7 @@
     )
     high, middle, _ = three_parts(weights)
     factors = jnp.concatenate([high, high, middle], 1)
+    load.wait()
     for f in range(0, width, step):
         p_high = stack_ref[units : units + rank, f : f + step]
         p_middle = stack_ref[units + rank : units + 2 * rank, f : f + step]
@@ -89,7 +92,7 @@
         new_ref[1, :, f : f + step] = fresh[rows:]
 
 
-def finish(core, own, other, q_prev, merged):
+def finish(where, own, other, q_prev, merged):
     rows = own.shape[1]
     width = own.shape[0] * own.shape[2]
     rank = q_prev.shape[2]
@@ -100,34 +103,69 @@
             jax.ShapeDtypeStruct((2, rows, width), jnp.bfloat16),
             jax.ShapeDtypeStruct((2, rank, rows), jnp.float32),
         ),
-        in_specs=[pl.BlockSpec(memory_space=pltpu.SMEM), vmem, vmem, vmem, vmem],
+        in_specs=[pl.BlockSpec(memory_space=pltpu.SMEM), vmem, vmem, vmem, pl.BlockSpec(memory_space=pl.ANY)],
         out_specs=(vmem, vmem),
-        scratch_shapes=[pltpu.VMEM((2 * rows + 3 * rank, width), jnp.bfloat16)],
+        scratch_shapes=[
+            pltpu.VMEM((2 * rows + 3 * rank, width), jnp.bfloat16),
+            pltpu.VMEM((2 * rows, width), jnp.float32),
+            pltpu.SemaphoreType.DMA,
+        ],
         compiler_params=pltpu.CompilerParams(vmem_limit_bytes=VMEM_BYTES),
         name="finish",
-    )(core.reshape(1), own, other, q_prev.transpose(0, 2, 1), merged)
-
-
-def gradient_kernel(core_ref, tokens_hbm, gate_ref, up_ref, cot_ref, error_ref, d_ref, send_ref, keep_ref, merged_ref, tokens_ref, sems, *, scale):
-    parts = sems.shape[0]
-    rows, width = gate_ref.shape
-    step = width // parts
-    chunks, _, lanes = send_ref.shape
-
-    def load(k):
-        at = pl.ds(k * step, step)
-        return pltpu.make_async_copy(tokens_hbm.at[:, at], tokens_ref.at[:, at], sems.at[k])
-
-    for k in range(parts):
-        load(k).start()
-    pre = jnp.zeros((2 * rows, tokens_ref.shape[0]), jnp.float32)
-    for k in range(parts):
-        load(k).wait()
-        at = slice(k * step, (k + 1) * step)
+    )(where, own, other, q_prev.transpose(0, 2, 1), merged)
+
+
+def shard_offset(tensor_index, shift, width, tensor_ways):
+    shard = (tensor_index + shift + tensor_ways) % tensor_ways
+    return pl.multiple_of(shard * width, width)
+
+
+def add_products(pre, where_ref, gate_ref, up_ref, shards, shard_width, tensor_ways):
+    for ref, shift, start in shards:
+        at = shard_offset(where_ref[1], shift, shard_width, tensor_ways) + start
+        at = pl.ds(pl.multiple_of(at, 128), ref.shape[1])
         weights = jnp.concatenate([gate_ref[:, at], up_ref[:, at]], 0)
-        pre += lax.dot_general(
-            weights, tokens_ref[:, at], (((1,), (1,)), ((), ())), preferred_element_type=jnp.float32
-        )
+        pre += lax.dot_general(weights, ref[...], (((1,), (1,)), ((), ())), preferred_element_type=jnp.float32)
+    return pre
+
+
+def early_kernel(where_ref, gate_ref, up_ref, *refs, shifts, tensor_ways):
+    shards = [(ref, shift, 0) for ref, shift in zip(refs[:-1], shifts)]
+    pre_ref = refs[-1]
+    zeros = jnp.zeros(pre_ref.shape, jnp.float32)
+    pre_ref[...] = add_products(zeros, where_ref, gate_ref, up_ref, shards, refs[0].shape[1], tensor_ways)
+
+
+def early_products(where, w_gate, w_up, shards, tensor_ways):
+    vmem = pl.BlockSpec(memory_space=pltpu.VMEM)
+    return pl.pallas_call(
+        functools.partial(early_kernel, shifts=[shift for _, shift in shards], tensor_ways=tensor_ways),
+        out_shape=jax.ShapeDtypeStruct((2 * w_gate.shape[0], shards[0][0].shape[0]), jnp.float32),
+        in_specs=[pl.BlockSpec(memory_space=pltpu.SMEM)] + [vmem] * (2 + len(shards)),
+        out_specs=vmem,
+        compiler_params=pltpu.CompilerParams(vmem_limit_bytes=VMEM_BYTES),
+        name="early_products",
+    )(where, w_gate, w_up, *[shard for shard, _ in shards])
+
+
+def gradient_kernel(where_ref, pre_ref, gate_ref, up_ref, cot_ref, error_ref, *refs, places, early, shard_width, tensor_ways, scale):
+    sources = refs[: len(places)]
+    d_ref, send_ref, keep_ref, merged_ref, tokens_ref, sems = refs[len(places) :]
+    rows = gate_ref.shape[0]
+    lanes = send_ref.shape[2]
+    slots = []
+    column = 0
+    for source, (shift, start) in zip(sources, places):
+        slots.append((tokens_ref.at[:, pl.ds(column, source.shape[1])], shift, start))
+        column += source.shape[1]
+    order = list(range(early, len(places))) + list(range(early))
+    copies = [pltpu.make_async_copy(sources[i], slots[i][0], sems.at[i]) for i in range(len(places))]
+    for i in order:
+        copies[i].start()
+    pre = pre_ref[...]
+    for i in order[: len(places) - early]:
+        copies[i].wait()
+        pre = add_products(pre, where_ref, gate_ref, up_ref, slots[i : i + 1], shard_width, tensor_ways)
     gate_pre, up_pre = pre[0:rows], pre[rows:]
     squash = jax.nn.sigmoid(gate_pre)
     upstream = cot_ref[...].astype(jnp.float32)
@@ -135,42 +173,61 @@
     d_up = (upstream * gate_pre * squash).astype(jnp.bfloat16)
     d_both = jnp.concatenate([d_gate, d_up], 0)
     d_ref[...] = d_both
-    first = core_ref[0] == 0
-    step = 512
-    for f in range(0, width, step):
-        at = slice(f, f + step)
-        grads = jnp.dot(d_both, tokens_ref[:, at], preferred_element_type=jnp.float32) * scale
-        gate_half = grads[0:rows] + error_ref[0, :, at].astype(jnp.float32)
-        up_half = grads[rows:] + error_ref[1, :, at].astype(jnp.float32)
-        merged_ref[0:rows, at] = gate_half
-        merged_ref[rows:, at] = up_half
+    first = where_ref[0] == 0
+    for i in order:
+        if i < early:
+            copies[i].wait()
+        ref, shift, start = slots[i]
+        size = ref.shape[1]
+        at = pl.multiple_of(shard_offset(where_ref[1], shift, shard_width, tensor_ways) + start, 128)
+        grads = jnp.dot(d_both, ref[...], preferred_element_type=jnp.float32) * scale
+        gate_half = grads[0:rows] + error_ref[0, :, pl.ds(at, size)].astype(jnp.float32)
+        up_half = grads[rows:] + error_ref[1, :, pl.ds(at, size)].astype(jnp.float32)
+        merged_ref[0:rows, pl.ds(at, size)] = gate_half
+        merged_ref[rows:, pl.ds(at, size)] = up_half
+        gate_half = gate_half.astype(jnp.bfloat16)
+        up_half = up_half.astype(jnp.bfloat16)
         keep = jnp.where(first, gate_half, up_half)
-        send = jnp.where(first, up_half, gate_half).astype(jnp.bfloat16)
-        for i in range(step // lanes):
-            part = slice(i * lanes, (i + 1) * lanes)
-            keep_ref[f // lanes + i] = keep[:, part]
-            send_ref[f // lanes + i] = send[:, part]
-
-
-def gradients(core, whole, w_gate, w_up, cot, error_fb, n_chips):
-    count, width = whole.shape
-    rows = w_gate.shape[0]
+        send = jnp.where(first, up_half, gate_half)
+        chunk = at // lanes
+        for k in range(size // lanes):
+            part = slice(k * lanes, (k + 1) * lanes)
+            keep_ref[chunk + k] = keep[:, part]
+            send_ref[chunk + k] = send[:, part]
+
+
+def gradients(where, pre, shards, early, w_gate, w_up, cot, error_fb, n_chips, tensor_ways):
+    rows, width = w_gate.shape
+    count = pre.shape[1]
     lanes = width // n_chips
     vmem = pl.BlockSpec(memory_space=pltpu.VMEM)
-    return pl.pallas_call(
-        functools.partial(gradient_kernel, scale=1.0 / math.sqrt(count)),
+    here = pl.BlockSpec(memory_space=pl.ANY)
+    whole_width = shards[0][0].shape[1]
+    operands = [
+        pltpu.with_memory_space_constraint(shard, pltpu.HBM) if shard.shape[1] == whole_width else shard
+        for shard, _, _ in shards
+    ]
+    return pl.pallas_call(
+        functools.partial(
+            gradient_kernel,
+            places=[(shift, start) for _, shift, start in shards],
+            early=early,
+            shard_width=width // tensor_ways,
+            tensor_ways=tensor_ways,
+            scale=1.0 / math.sqrt(count),
+        ),
         out_shape=(
             jax.ShapeDtypeStruct((2 * rows, count), jnp.bfloat16),
             jax.ShapeDtypeStruct((n_chips, rows, lanes), jnp.bfloat16),
-            jax.ShapeDtypeStruct((n_chips, rows, lanes), jnp.float32),
+            jax.ShapeDtypeStruct((n_chips, rows, lanes), jnp.bfloat16),
             jax.ShapeDtypeStruct((2 * rows, width), jnp.float32),
         ),
-        in_specs=[pl.BlockSpec(memory_space=pltpu.SMEM), pl.BlockSpec(memory_space=pl.ANY)] + [vmem] * 4,
+        in_specs=[pl.BlockSpec(memory_space=pltpu.SMEM)] + [vmem] * 5 + [here] * len(shards),
         out_specs=(vmem,) * 4,
-        scratch_shapes=[pltpu.VMEM((count, width), jnp.bfloat16), pltpu.SemaphoreType.DMA((8,))],
+        scratch_shapes=[pltpu.VMEM((count, width), jnp.bfloat16), pltpu.SemaphoreType.DMA((len(shards),))],
         compiler_params=pltpu.CompilerParams(vmem_limit_bytes=VMEM_BYTES),
         name="gradients",
-    )(core.reshape(1), whole, w_gate, w_up, cot.T, error_fb.reshape(2, rows, width))
+    )(where, pre, w_gate, w_up, cot.T, error_fb.reshape(2, rows, width), *operands)
 
 
 def act_kernel(d_ref, gate_ref, up_ref, act_ref):
@@ -215,21 +272,41 @@
     )(pieces)
 
 
+def ring(value, step):
+    ways = lax.axis_size("tensor")
+    return lax.ppermute(value, "tensor", [(i, (i + step) % ways) for i in range(ways)])
+
+
 def on_device(tokens, w_gate, w_up, d_hidden, error_fb, q_prev):
     core = lax.axis_index("core")
     n_chips = lax.axis_size(CHIPS)
-    whole = lax.all_gather(tokens, "tensor", axis=1, tiled=True)
-    d_both, send, keep, merged = gradients(core, whole, w_gate, w_up, d_hidden, error_fb, n_chips)
+    ways = lax.axis_size("tensor")
+    where = jnp.stack([core, lax.axis_index("tensor")])
+    share = w_gate.shape[1] // ways
+
+    shards = [(tokens, 0, 0)]
+    ahead = behind = tokens
+    for k in range(1, ways // 2):
+        ahead, behind = ring(ahead, 1), ring(behind, -1)
+        shards += [(ahead, -k, 0), (behind, k, 0)]
+    early = 5
+    pre = early_products(where, w_gate, w_up, [shard[:2] for shard in shards[:early]], ways)
+    middle = share // 2
+    ahead, behind, pre = lax.optimization_barrier((ahead[:, :middle], behind[:, middle:], pre))
+    shards += [(ring(ahead, 1), ways // 2, 0), (ring(behind, -1), ways // 2, middle)]
+    d_both, send, keep, merged = gradients(
+        where, pre, shards, early, w_gate, w_up, d_hidden, error_fb, n_chips, ways
+    )
     act = act_terms(d_both, w_gate, w_up)
     got = lax.ppermute(send, "core", SWAP)
-    pieces = (keep + got.astype(jnp.float32)).astype(jnp.bfloat16)
+    pieces = (keep.astype(jnp.float32) + got.astype(jnp.float32)).astype(jnp.bfloat16)
     pieces, act = lax.optimization_barrier((pieces, act))
     d_tokens = lax.psum_scatter(act, "tensor", scatter_dimension=1, tiled=True)
     pieces = lax.all_to_all(pieces, CHIPS, 0, 0, tiled=True)
     copies = mean_copies(pieces, n_chips * lax.axis_size("core"))
     own_half = lax.all_to_all(copies, CHIPS, 0, 0, tiled=True)
     other_half = lax.ppermute(own_half, "core", SWAP)
-    new_error, q_next = finish(core, own_half, other_half, q_prev, merged)
+    new_error, q_next = finish(where, own_half, other_half, q_prev, merged)
     return (d_tokens, new_error.reshape(error_fb.shape), q_next.transpose(0, 2, 1))
 
 

time: 156 us -> 158 us (1.013)
  waiting for transfers between devices: 56.9 us -> 14.7 us
  starting transfers between devices: 10.1 us -> 44.4 us
  blocking collectives: 51.4 us -> 57 us
  other arithmetic: 0.13 us -> 2.17 us
    all_gather x1 -> x0, waiting for transfers between devices: 54.5 us -> none  [on_device(): whole = lax.all_gather(tokens, 'tensor', axis=1, tiled=True)]
    ppermute x0 -> x8, starting transfers between devices: none -> 29.3 us  [ring(): lax.ppermute(value, 'tensor', [(i, (i + step) % ways) for i in range(ways)])]
    ppermute x0 -> x8, waiting for transfers between devices: none -> 12.9 us  [ring(): lax.ppermute(value, 'tensor', [(i, (i + step) % ways) for i in range(ways)])]
    all_to_all x1, blocking collectives: 27.3 us -> 33.2 us  [on_device(): pieces = lax.all_to_all(pieces, CHIPS, 0, 0, tiled=True)]
    ppermute x1, starting transfers between devices: 3.18 us -> 8.28 us  [on_device(): got = lax.ppermute(send, 'core', SWAP)]
    convert_element_type x1, other arithmetic: 0.13 us -> 2.09 us  [on_device(): (keep.astype(jnp.float32) + got.astype(jnp.float32)).astype(jnp.bfloat16)]
    unnamed x14 -> x30, local copies, waits for them, and re-layouts: 3.02 us -> 4.28 us
    pallas_call x1 -> x2, Pallas kernels: 6.78 us -> 6.3 us  [the longest x1 5.01 us: gradients(): pl.pallas_call(functools.partial(gradient_kernel, places=[(shift, start)...]
  transfers between devices with their start and end apart: 4 -> 11, of which waited for: 2 -> 6; matrix products, arithmetic and copies ran while one was open for 0% -> 0% of each run, Pallas kernels for 8% -> 10%
where the time goes in v3:
time: 158 us; the launch traced here: 157 us
  blocking collectives  57 us (36%)
  starting transfers between devices  44.4 us (28%)
  Pallas kernels  20.2 us (13%)
  waiting for transfers between devices  14.7 us (9%)
  between operations  14.3 us (9%)
  local copies, waits for them, and re-layouts  4.31 us (3%)
  other arithmetic  2.17 us (1%)
    all_to_all x1, blocking collectives, on_device(): pieces = lax.all_to_all(pieces, CHIPS, 0, 0, tiled=True)  33.2 us
    ppermute x8, starting transfers between devices, ring(): lax.ppermute(value, 'tensor', [(i, (i + step) % ways) for i in range(ways)])  29.3 us
    all_to_all x1, blocking collectives, on_device(): own_half = lax.all_to_all(copies, CHIPS, 0, 0, tiled=True)  23.8 us
    ppermute x8, waiting for transfers between devices, ring(): lax.ppermute(value, 'tensor', [(i, (i + step) % ways) for i in range(ways)])  12.9 us
    pallas_call x1, Pallas kernels, finish(): pl.pallas_call(finish_kernel, out_shape=(jax.ShapeDtypeStruct((2, rows, w...  11.1 us
    ppermute x1, starting transfers between devices, on_device(): got = lax.ppermute(send, 'core', SWAP)  8.28 us
    ppermute x1, starting transfers between devices, on_device(): other_half = lax.ppermute(own_half, 'core', SWAP)  6.86 us
    pallas_call x1, Pallas kernels, gradients(): pl.pallas_call(functools.partial(gradient_kernel, places=[(shift, start)...  5.01 us
  transfers between devices with their start and end apart: 11, of which 6 were waited for; matrix products, arithmetic and copies ran while one was open for 0% of the time, Pallas kernels for 10%

profile of v3, /device:TPU:1, one launch (start us, length us, event | category | flops | bytes accessed | tf_op | source)
XLA Modules:
  0.0 157.1 jit_solution(7602573883376926640)
XLA Ops:
  7.2 0.0 reduce-scatter.2.cloned.1.call-start
  7.2 5.9 %collective-permute-start.3 = (bf16[384,512]{1,0:T(8,128)(2,1)}, bf16[384,512]{1,0:T(8,128)(2,1)S(1)}, u32[]{:S(2)}, u32[]{:S(2)}) collective-permute-start(bf16[384,512]{1,0:T(8,128)(2,1)} %refs_0_.3), channel_id=1, source_target_pairs={{0,7},{1,0},{2,1},{3,2},{4,3},{5,4},{6,5},{7,6},{8,15},{9,8},{10,9... | collective-permute-start | bytes 1179656 | tf_op jit(solution)/shard_map/ppermute | solution.py:277
  13.1 1.9 %collective-permute-start = (bf16[384,512]{1,0:T(8,128)(2,1)}, bf16[384,512]{1,0:T(8,128)(2,1)S(1)}, u32[]{:S(2)}, u32[]{:S(2)}) collective-permute-start(bf16[384,512]{1,0:T(8,128)(2,1)} %refs_0_.3), channel_id=1, source_target_pairs={{0,1},{1,2},{2,3},{3,4},{4,5},{5,6},{6,7},{7,0},{8,9},{9,10},{10,1... | collective-permute-start | bytes 1179656 | tf_op jit(solution)/shard_map/ppermute | solution.py:277
  15.1 4.2 %collective-permute-done.3.refs_2_ = bf16[384,512]{1,0:T(8,128)(2,1)S(1)} collective-permute-done((bf16[384,512]{1,0:T(8,128)(2,1)}, bf16[384,512]{1,0:T(8,128)(2,1)S(1)}, u32[]{:S(2)}, u32[]{:S(2)}) %collective-permute-start.3) | collective-permute-done | bytes 393248 | tf_op jit(solution)/shard_map/ppermute | solution.py:277
  19.3 5.2 %collective-permute-start.4 = (bf16[384,512]{1,0:T(8,128)(2,1)S(1)}, bf16[384,512]{1,0:T(8,128)(2,1)S(1)}, u32[]{:S(2)}, u32[]{:S(2)}) collective-permute-start(bf16[384,512]{1,0:T(8,128)(2,1)S(1)} %collective-permute-done.3.refs_2_), channel_id=1, source_target_pairs={{0,7},{1,0},{2,1},{3,2},{4,3},{5,4},{6,5},{7,6},{8,15},{9,8},{10,9... | collective-permute-start | bytes 1179656 | tf_op jit(solution)/shard_map/ppermute | solution.py:277
  24.5 1.9 %collective-permute-start.1 = (bf16[384,512]{1,0:T(8,128)(2,1)S(1)}, bf16[384,512]{1,0:T(8,128)(2,1)S(1)}, u32[]{:S(2)}, u32[]{:S(2)}) collective-permute-start(bf16[384,512]{1,0:T(8,128)(2,1)S(1)} %collective-permute-done.refs_1_), channel_id=1, source_target_pairs={{0,1},{1,2},{2,3},{3,4},{4,5},{5,6},{6,7},{7,0},{8,9},{9,10},{10,1... | collective-permute-start | bytes 1179656 | tf_op jit(solution)/shard_map/ppermute | solution.py:277
  26.4 2.7 %collective-permute-done.4.refs_4_ = bf16[384,512]{1,0:T(8,128)(2,1)S(1)} collective-permute-done((bf16[384,512]{1,0:T(8,128)(2,1)S(1)}, bf16[384,512]{1,0:T(8,128)(2,1)S(1)}, u32[]{:S(2)}, u32[]{:S(2)}) %collective-permute-start.4) | collective-permute-done | bytes 393248 | tf_op jit(solution)/shard_map/ppermute | solution.py:277
  29.2 5.9 %collective-permute-start.5 = (bf16[384,512]{1,0:T(8,128)(2,1)S(1)}, bf16[384,512]{1,0:T(8,128)(2,1)S(1)}, u32[]{:S(2)}, u32[]{:S(2)}) collective-permute-start(bf16[384,512]{1,0:T(8,128)(2,1)S(1)} %collective-permute-done.4.refs_4_), channel_id=1, source_target_pairs={{0,7},{1,0},{2,1},{3,2},{4,3},{5,4},{6,5},{7,6},{8,15},{9,8},{10,9... | collective-permute-start | bytes 1179656 | tf_op jit(solution)/shard_map/ppermute | solution.py:277
  35.1 1.9 %collective-permute-start.2 = (bf16[384,512]{1,0:T(8,128)(2,1)S(1)}, bf16[384,512]{1,0:T(8,128)(2,1)S(1)}, u32[]{:S(2)}, u32[]{:S(2)}) collective-permute-start(bf16[384,512]{1,0:T(8,128)(2,1)S(1)} %collective-permute-done.1.refs_3_), channel_id=1, source_target_pairs={{0,1},{1,2},{2,3},{3,4},{4,5},{5,6},{6,7},{7,0},{8,9},{9,10},{10,1... | collective-permute-start | bytes 1179656 | tf_op jit(solution)/shard_map/ppermute | solution.py:277
  37.0 0.1 pad_add_fusion.where_ref
  37.1 1.1 copy-done
  38.2 1.1 copy-done.2
  39.2 1.0 copy-done.4
  40.2 1.3 early_products.1.pre_ref
  41.6 3.2 %collective-permute-done.2.refs_5_ = bf16[384,512]{1,0:T(8,128)(2,1)S(1)} collective-permute-done((bf16[384,512]{1,0:T(8,128)(2,1)S(1)}, bf16[384,512]{1,0:T(8,128)(2,1)S(1)}, u32[]{:S(2)}, u32[]{:S(2)}) %collective-permute-start.2) | collective-permute-done | bytes 393248 | tf_op jit(solution)/shard_map/ppermute | solution.py:277
  44.8 2.2 %collective-permute-start.6 = (bf16[384,256]{1,0:T(8,128)(2,1)S(1)}, bf16[384,256]{1,0:T(8,128)(2,1)S(1)}, u32[]{:S(2)}, u32[]{:S(2)}) collective-permute-start(bf16[384,256]{1,0:T(8,128)(2,1)S(1)} %slice.8), channel_id=1, source_target_pairs={{0,1},{1,2},{2,3},{3,4},{4,5},{5,6},{6,7},{7,0},{8,9},{9,10},{10,1... | collective-permute-start | bytes 589832 | tf_op jit(solution)/shard_map/ppermute | solution.py:277
  47.0 4.3 %collective-permute-start.7 = (bf16[384,256]{1,0:T(8,128)(2,1)S(1)}, bf16[384,256]{1,0:T(8,128)(2,1)S(1)}, u32[]{:S(2)}, u32[]{:S(2)}) collective-permute-start(bf16[384,256]{1,0:T(8,128)(2,1)S(1)} %slice.9), channel_id=1, source_target_pairs={{0,7},{1,0},{2,1},{3,2},{4,3},{5,4},{6,5},{7,6},{8,15},{9,8},{10,9... | collective-permute-start | bytes 589832 | tf_op jit(solution)/shard_map/ppermute | solution.py:277
  51.3 1.1 collective-permute-done.6.refs_7_
  52.4 1.7 %collective-permute-done.7.refs_8_ = bf16[384,256]{1,0:T(8,128)(2,1)S(1)} collective-permute-done((bf16[384,256]{1,0:T(8,128)(2,1)S(1)}, bf16[384,256]{1,0:T(8,128)(2,1)S(1)}, u32[]{:S(2)}, u32[]{:S(2)}) %collective-permute-start.7) | collective-permute-done | bytes 196640 | tf_op jit(solution)/shard_map/ppermute | solution.py:277
  54.2 5.0 %gradients.1 = (bf16[160,384]{1,0:T(8,128)(2,1)S(1)}, bf16[32,80,128]{2,1,0:T(8,128)(2,1)}, bf16[32,80,128]{2,1,0:T(8,128)(2,1)S(1)}, f32[160,4096]{1,0:T(8,128)S(1)}) custom-call(s32[2]{0:T(128)S(1)} %pad_add_fusion.where_ref, f32[160,384]{1,0:T(8,128)S(1)} %early_products.1.pre_ref, bf16[80,4096]{1,0:T(8,128)(2,1)S(1)} %copy-done, ...), custom_call_target="tpu_custom_call" | custom-call | tf_op jit(solution)/shard_map/gradients/pallas_call | solution.py:210
  59.2 8.3 %collective-permute-start.8 = (bf16[32,80,128]{2,1,0:T(8,128)(2,1)}, bf16[32,80,128]{2,1,0:T(8,128)(2,1)}, u32[]{:S(2)}, u32[]{:S(2)}) collective-permute-start(bf16[32,80,128]{2,1,0:T(8,128)(2,1)} %get-tuple-element.18), channel_id=1, source_target_pairs={{0,8},{8,0},{1,9},{9,1},{2,10},{10,2},{3,11},{11,3},{4,12},{12,4},... | collective-permute-start | bytes 1966088 | tf_op jit(solution)/shard_map/ppermute | solution.py:301
  67.5 2.6 %act_terms.1 = bf16[384,4096]{1,0:T(8,128)(2,1)} custom-call(bf16[160,384]{1,0:T(8,128)(2,1)S(1)} %get-tuple-element.19.d_ref, bf16[80,4096]{1,0:T(8,128)(2,1)S(1)} %copy-done.1, bf16[80,4096]{1,0:T(8,128)(2,1)S(1)} %copy-done.3), custom_call_target="tpu_custom_call" | custom-call | tf_op jit(solution)/shard_map/act_terms/pallas_call | solution.py:244
  70.2 2.1 %add_convert_fusion = bf16[32,80,128]{2,1,0:T(8,128)(2,1)} fusion(bf16[32,80,128]{2,1,0:T(8,128)(2,1)} %collective-permute-done.8, bf16[32,80,128]{2,1,0:T(8,128)(2,1)S(1)} %get-tuple-element.17), kind=kLoop, calls=%fused_computation | loop fusion | flops 1310720 | bytes 1966080 | tf_op jit(solution)/shard_map/convert_element_type | solution.py:302
  72.3 0.0 reduce-scatter.2.cloned.1.call-update
  72.3 1.1 copy-done.12
  73.3 33.2 %all_to_all.10.pieces_ref = bf16[32,80,128]{2,1,0:T(8,128)(2,1)S(1)} all-to-all(bf16[32,80,128]{2,1,0:T(8,128)(2,1)S(1)} %copy-done.12), channel_id=1, replica_groups=mesh['x'=4,'z'=8,'core'=2,'tensor'=8] {'x','z'}, dimensions={0} | all-to-all | bytes 1310720 | tf_op jit(solution)/shard_map/all_to_all | solution.py:305
  106.5 0.1 mean_copies.1
  106.7 23.8 %all_to_all.11.own_ref = bf16[32,80,128]{2,1,0:T(8,128)(2,1)S(1)} all-to-all(bf16[32,80,128]{2,1,0:T(8,128)(2,1)S(1)} %mean_copies.1), channel_id=1, replica_groups=mesh['x'=4,'z'=8,'core'=2,'tensor'=8] {'x','z'}, dimensions={0} | all-to-all | bytes 1310720 | tf_op jit(solution)/shard_map/all_to_all | solution.py:307
  130.5 6.9 %collective-permute-start.9 = (bf16[32,80,128]{2,1,0:T(8,128)(2,1)S(1)}, bf16[32,80,128]{2,1,0:T(8,128)(2,1)S(1)}, u32[]{:S(2)}, u32[]{:S(2)}) collective-permute-start(bf16[32,80,128]{2,1,0:T(8,128)(2,1)S(1)} %all_to_all.11.own_ref), channel_id=1, source_target_pairs={{0,8},{8,0},{1,9},{9,1},{2,10},{10,2},{3,11},{11,3},{4,12},{12,4},... | collective-permute-start | bytes 1966088 | tf_op jit(solution)/shard_map/ppermute | solution.py:308
  137.4 1.7 %collective-permute-done.9.other_ref = bf16[32,80,128]{2,1,0:T(8,128)(2,1)S(1)} collective-permute-done((bf16[32,80,128]{2,1,0:T(8,128)(2,1)S(1)}, bf16[32,80,128]{2,1,0:T(8,128)(2,1)S(1)}, u32[]{:S(2)}, u32[]{:S(2)}) %collective-permute-start.9) | collective-permute-done | bytes 655392 | tf_op jit(solution)/shard_map/ppermute | solution.py:308
  139.1 11.1 %finish.1 = (bf16[2,80,4096]{2,1,0:T(8,128)(2,1)}, f32[2,64,80]{2,1,0:T(8,128)}) custom-call(s32[2]{0:T(128)S(1)} %pad_add_fusion.where_ref, bf16[32,80,128]{2,1,0:T(8,128)(2,1)S(1)} %all_to_all.11.own_ref, bf16[32,80,128]{2,1,0:T(8,128)(2,1)S(1)} %collective-permute-done.9.other_ref, f32[2,64,80]{2,1,0:T(8,128)S(1)} %bitcast.8, ...), custom_call_target="tpu_custom_call" | custom-call | tf_op jit(solution)/shard_map/finish/pallas_call | solution.py:100
  150.2 0.0 reduce-scatter.2.cloned.1.call-done
  (32 shorter events, 0.1 us)
Async XLA Ops:
  7.2 143.0 %reduce-scatter.2.cloned.1.call-start = ((), (), s32[]{:S(2)}) async-start(), calls=%async_computation.3 | async-start | bytes 3538944 | tf_op jit(solution)/shard_map/reduce_scatter | solution.py:304
  7.2 12.0 %collective-permute-start.3 = (bf16[384,512]{1,0:T(8,128)(2,1)}, bf16[384,512]{1,0:T(8,128)(2,1)S(1)}, u32[]{:S(2)}, u32[]{:S(2)}) collective-permute-start(bf16[384,512]{1,0:T(8,128)(2,1)} %refs_0_.3), channel_id=1, source_target_pairs={{0,7},{1,0},{2,1},{3,2},{4,3},{5,4},{6,5},{7,6},{8,15},{9,8},{10,9... | collective-permute-start | bytes 1179656 | tf_op jit(solution)/shard_map/ppermute | solution.py:277
  13.1 11.3 %collective-permute-start = (bf16[384,512]{1,0:T(8,128)(2,1)}, bf16[384,512]{1,0:T(8,128)(2,1)S(1)}, u32[]{:S(2)}, u32[]{:S(2)}) collective-permute-start(bf16[384,512]{1,0:T(8,128)(2,1)} %refs_0_.3), channel_id=1, source_target_pairs={{0,1},{1,2},{2,3},{3,4},{4,5},{5,6},{6,7},{7,0},{8,9},{9,10},{10,1... | collective-permute-start | bytes 1179656 | tf_op jit(solution)/shard_map/ppermute | solution.py:277
  19.3 22.3 %copy-start.5 = (bf16[384,512]{1,0:T(8,128)(2,1)}, bf16[384,512]{1,0:T(8,128)(2,1)S(1)}, u32[]{:S(2)}) copy-start(bf16[384,512]{1,0:T(8,128)(2,1)S(1)} %collective-permute-done.3.refs_2_) | copy-start | bytes 1179652
  19.3 9.9 %collective-permute-start.4 = (bf16[384,512]{1,0:T(8,128)(2,1)S(1)}, bf16[384,512]{1,0:T(8,128)(2,1)S(1)}, u32[]{:S(2)}, u32[]{:S(2)}) collective-permute-start(bf16[384,512]{1,0:T(8,128)(2,1)S(1)} %collective-permute-done.3.refs_2_), channel_id=1, source_target_pairs={{0,7},{1,0},{2,1},{3,2},{4,3},{5,4},{6,5},{7,6},{8,15},{9,8},{10,9... | collective-permute-start | bytes 1179656 | tf_op jit(solution)/shard_map/ppermute | solution.py:277
  24.5 17.1 %copy-start.6 = (bf16[384,512]{1,0:T(8,128)(2,1)}, bf16[384,512]{1,0:T(8,128)(2,1)S(1)}, u32[]{:S(2)}) copy-start(bf16[384,512]{1,0:T(8,128)(2,1)S(1)} %collective-permute-done.refs_1_) | copy-start | bytes 1179652
  24.5 10.6 %collective-permute-start.1 = (bf16[384,512]{1,0:T(8,128)(2,1)S(1)}, bf16[384,512]{1,0:T(8,128)(2,1)S(1)}, u32[]{:S(2)}, u32[]{:S(2)}) collective-permute-start(bf16[384,512]{1,0:T(8,128)(2,1)S(1)} %collective-permute-done.refs_1_), channel_id=1, source_target_pairs={{0,1},{1,2},{2,3},{3,4},{4,5},{5,6},{6,7},{7,0},{8,9},{9,10},{10,1... | collective-permute-start | bytes 1179656 | tf_op jit(solution)/shard_map/ppermute | solution.py:277
  29.2 12.4 %copy-start.7 = (bf16[384,512]{1,0:T(8,128)(2,1)}, bf16[384,512]{1,0:T(8,128)(2,1)S(1)}, u32[]{:S(2)}) copy-start(bf16[384,512]{1,0:T(8,128)(2,1)S(1)} %collective-permute-done.4.refs_4_) | copy-start | bytes 1179652
  29.2 12.4 %collective-permute-start.5 = (bf16[384,512]{1,0:T(8,128)(2,1)S(1)}, bf16[384,512]{1,0:T(8,128)(2,1)S(1)}, u32[]{:S(2)}, u32[]{:S(2)}) collective-permute-start(bf16[384,512]{1,0:T(8,128)(2,1)S(1)} %collective-permute-done.4.refs_4_), channel_id=1, source_target_pairs={{0,7},{1,0},{2,1},{3,2},{4,3},{5,4},{6,5},{7,6},{8,15},{9,8},{10,9... | collective-permute-start | bytes 1179656 | tf_op jit(solution)/shard_map/ppermute | solution.py:277
  35.0 6.5 %copy-start.8 = (bf16[384,512]{1,0:T(8,128)(2,1)}, bf16[384,512]{1,0:T(8,128)(2,1)S(1)}, u32[]{:S(2)}) copy-start(bf16[384,512]{1,0:T(8,128)(2,1)S(1)} %collective-permute-done.1.refs_3_) | copy-start | bytes 1179652
  35.1 9.7 %collective-permute-start.2 = (bf16[384,512]{1,0:T(8,128)(2,1)S(1)}, bf16[384,512]{1,0:T(8,128)(2,1)S(1)}, u32[]{:S(2)}, u32[]{:S(2)}) collective-permute-start(bf16[384,512]{1,0:T(8,128)(2,1)S(1)} %collective-permute-done.1.refs_3_), channel_id=1, source_target_pairs={{0,1},{1,2},{2,3},{3,4},{4,5},{5,6},{6,7},{7,0},{8,9},{9,10},{10,1... | collective-permute-start | bytes 1179656 | tf_op jit(solution)/shard_map/ppermute | solution.py:277
  37.1 1.1 copy-start
  38.2 1.1 copy-start.2
  39.2 1.0 copy-start.4
  40.2 13.9 %copy-start.9 = (bf16[1,2,80,4096]{3,2,1,0:T(8,128)(2,1)S(1)}, bf16[1,2,80,4096]{3,2,1,0:T(8,128)(2,1)}, u32[]{:S(2)}) copy-start(bf16[1,2,80,4096]{3,2,1,0:T(8,128)(2,1)} %param.10) | copy-start | bytes 3932164
  40.2 13.9 %copy-start.11 = (bf16[384,80]{0,1:T(8,128)(2,1)S(1)}, bf16[384,80]{0,1:T(8,128)(2,1)}, u32[]{:S(2)}) copy-start(bf16[384,80]{0,1:T(8,128)(2,1)} %param.9) | copy-start | bytes 184324
  41.6 12.6 %copy-start.13 = (bf16[384,512]{1,0:T(8,128)(2,1)}, bf16[384,512]{1,0:T(8,128)(2,1)S(1)}, u32[]{:S(2)}) copy-start(bf16[384,512]{1,0:T(8,128)(2,1)S(1)} %collective-permute-done.5.refs_6_) | copy-start | bytes 1179652
  44.8 9.4 %copy-start.14 = (bf16[384,512]{1,0:T(8,128)(2,1)}, bf16[384,512]{1,0:T(8,128)(2,1)S(1)}, u32[]{:S(2)}) copy-start(bf16[384,512]{1,0:T(8,128)(2,1)S(1)} %collective-permute-done.2.refs_5_) | copy-start | bytes 1179652
  44.8 7.6 %collective-permute-start.6 = (bf16[384,256]{1,0:T(8,128)(2,1)S(1)}, bf16[384,256]{1,0:T(8,128)(2,1)S(1)}, u32[]{:S(2)}, u32[]{:S(2)}) collective-permute-start(bf16[384,256]{1,0:T(8,128)(2,1)S(1)} %slice.8), channel_id=1, source_target_pairs={{0,1},{1,2},{2,3},{3,4},{4,5},{5,6},{6,7},{7,0},{8,9},{9,10},{10,1... | collective-permute-start | bytes 589832 | tf_op jit(solution)/shard_map/ppermute | solution.py:277
  47.0 7.2 %collective-permute-start.7 = (bf16[384,256]{1,0:T(8,128)(2,1)S(1)}, bf16[384,256]{1,0:T(8,128)(2,1)S(1)}, u32[]{:S(2)}, u32[]{:S(2)}) collective-permute-start(bf16[384,256]{1,0:T(8,128)(2,1)S(1)} %slice.9), channel_id=1, source_target_pairs={{0,7},{1,0},{2,1},{3,2},{4,3},{5,4},{6,5},{7,6},{8,15},{9,8},{10,9... | collective-permute-start | bytes 589832 | tf_op jit(solution)/shard_map/ppermute | solution.py:277
  54.2 13.3 %copy-start.1 = (bf16[80,4096]{1,0:T(8,128)(2,1)S(1)}, bf16[80,4096]{1,0:T(8,128)(2,1)}, u32[]{:S(2)}) copy-start(bf16[80,4096]{1,0:T(8,128)(2,1)} %gate_ref.5) | copy-start | bytes 1966084
  54.2 13.3 %copy-start.3 = (bf16[80,4096]{1,0:T(8,128)(2,1)S(1)}, bf16[80,4096]{1,0:T(8,128)(2,1)}, u32[]{:S(2)}) copy-start(bf16[80,4096]{1,0:T(8,128)(2,1)} %up_ref.5) | copy-start | bytes 1966084
  59.2 10.9 %collective-permute-start.8 = (bf16[32,80,128]{2,1,0:T(8,128)(2,1)}, bf16[32,80,128]{2,1,0:T(8,128)(2,1)}, u32[]{:S(2)}, u32[]{:S(2)}) collective-permute-start(bf16[32,80,128]{2,1,0:T(8,128)(2,1)} %get-tuple-element.18), channel_id=1, source_target_pairs={{0,8},{8,0},{1,9},{9,1},{2,10},{10,2},{3,11},{11,3},{4,12},{12,4},... | collective-permute-start | bytes 1966088 | tf_op jit(solution)/shard_map/ppermute | solution.py:301
  72.3 1.1 copy-start.12
  106.5 32.5 %copy-start.10 = (f32[2,80,64]{1,2,0:T(8,128)S(1)}, f32[2,80,64]{1,2,0:T(8,128)}, u32[]{:S(2)}) copy-start(f32[2,80,64]{1,2,0:T(8,128)} %param.11) | copy-start | bytes 122884
  130.5 8.6 %collective-permute-start.9 = (bf16[32,80,128]{2,1,0:T(8,128)(2,1)S(1)}, bf16[32,80,128]{2,1,0:T(8,128)(2,1)S(1)}, u32[]{:S(2)}, u32[]{:S(2)}) collective-permute-start(bf16[32,80,128]{2,1,0:T(8,128)(2,1)S(1)} %all_to_all.11.own_ref), channel_id=1, source_target_pairs={{0,8},{8,0},{1,9},{9,1},{2,10},{10,2},{3,11},{11,3},{4,12},{12,4},... | collective-permute-start | bytes 1966088 | tf_op jit(solution)/shard_map/ppermute | solution.py:308
Sparse Core Ops, SparseCore 0:
  72.4 51.4 reduce-scatter.1

commit v4 on v3

--- a/solution.py
+++ b/solution.py
@@ -26,41 +26,47 @@
     n = gram.shape[0]
     row_ids = lax.broadcasted_iota(jnp.int32, (n, n), 0)
     col_ids = lax.broadcasted_iota(jnp.int32, (n, n), 1)
-    eye = jnp.where(row_ids == col_ids, 1.0, 0.0)
-    work = jnp.concatenate([gram, eye], 1)
+    work = jnp.concatenate([gram, jnp.where(row_ids == col_ids, 1.0, 0.0)], 1)
     blocks = [work[8 * k : 8 * k + 8] for k in range(n // 8)]
     below = lax.broadcasted_iota(jnp.int32, (8, 2 * n), 0)
-    for j in range(n - 1):
+    for j in range(0, n - 2, 2):
         k, i = divmod(j, 8)
-        row = blocks[k][i : i + 1]
-        scaled = row * (1.0 / row[:, j : j + 1])
-        for b in range(k, n // 8):
-            factor = jnp.broadcast_to(blocks[b][:, j : j + 1], (8, 2 * n))
-            if b == k:
-                factor = jnp.where(below > i, factor, 0.0)
-            blocks[b] = blocks[b] - factor * scaled
+        upper, lower = blocks[k][i : i + 1], blocks[k][i + 1 : i + 2]
+        a, b, c = upper[:, j : j + 1], upper[:, j + 1 : j + 2], lower[:, j + 1 : j + 2]
+        shrink = 1.0 / (a * c - b * b)
+        first = (c * upper - b * lower) * shrink
+        second = (a * lower - b * upper) * shrink
+        for m in range(k, n // 8):
+            left = jnp.broadcast_to(blocks[m][:, j : j + 1], (8, 2 * n))
+            right = jnp.broadcast_to(blocks[m][:, j + 1 : j + 2], (8, 2 * n))
+            change = left * first + right * second
+            if m == k:
+                change = jnp.where(below > i + 1, change, 0.0)
+            blocks[m] = blocks[m] - change
     work = jnp.concatenate(blocks, 0)
-    pivots = jnp.sum(jnp.where(row_ids == col_ids, work[:, :n], 0.0), 1, keepdims=True)
-    return work[:, n:] * lax.rsqrt(pivots)
+    pivots, rows = work[:, :n], work[:, n:]
+    odd = (row_ids[:, 0:1] & 1) == 1
+    diagonal = jnp.sum(jnp.where(row_ids == col_ids, pivots, 0.0), 1, keepdims=True)
+    beside = jnp.sum(jnp.where(row_ids == col_ids + 1, pivots, 0.0), 1, keepdims=True)
+    ratio = jnp.where(odd, beside / pltpu.roll(diagonal, 1, 0), 0.0)
+    return (rows - ratio * pltpu.roll(rows, 1, 0)) * lax.rsqrt(diagonal - ratio * beside)
 
 
 def finish_kernel(where_ref, own_ref, other_ref, q_ref, merged_hbm, new_ref, q_next_ref, stack_ref, merged_ref, sem):
     load = pltpu.make_async_copy(merged_hbm, merged_ref, sem)
     load.start()
     chunks, rows, lanes = own_ref.shape
-    units, rank = 2 * rows, q_ref.shape[1]
+    units, rank = 2 * rows, q_ref.shape[0]
     first = where_ref[0] == 0
     for j in range(chunks):
         at = slice(j * lanes, (j + 1) * lanes)
         stack_ref[0:rows, at] = jnp.where(first, own_ref[j], other_ref[j])
         stack_ref[rows:units, at] = jnp.where(first, other_ref[j], own_ref[j])
-    q_gate = jnp.concatenate(three_parts(q_ref[0]), 0)
-    q_up = jnp.concatenate(three_parts(q_ref[1]), 0)
+    q_parts = jnp.concatenate(three_parts(q_ref[...]), 0)
     width = chunks * lanes
     step = 1024
     for f in range(0, width, step):
-        p_parts = jnp.dot(q_gate, stack_ref[0:rows, f : f + step], preferred_element_type=jnp.float32)
-        p_parts += jnp.dot(q_up, stack_ref[rows:units, f : f + step], preferred_element_type=jnp.float32)
+        p_parts = jnp.dot(q_parts, stack_ref[0:units, f : f + step], preferred_element_type=jnp.float32)
         p_mean = p_parts[0:rank] + p_parts[rank : 2 * rank] + p_parts[2 * rank :]
         for k, part in enumerate(three_parts(p_mean)):
             stack_ref[units + k * rank : units + (k + 1) * rank, f : f + step] = part
@@ -112,34 +118,38 @@
         ],
         compiler_params=pltpu.CompilerParams(vmem_limit_bytes=VMEM_BYTES),
         name="finish",
-    )(where, own, other, q_prev.transpose(0, 2, 1), merged)
-
-
-def shard_offset(tensor_index, shift, width, tensor_ways):
+    )(where, own, other, q_prev.transpose(2, 0, 1).reshape(rank, 2 * rows), pltpu.with_memory_space_constraint(merged, pltpu.HBM))
+
+
+def shard_offset(tensor_index, shift, start, shard_width, tensor_ways):
     shard = (tensor_index + shift + tensor_ways) % tensor_ways
-    return pl.multiple_of(shard * width, width)
+    return pl.multiple_of(shard * shard_width + start, 128)
 
 
 def add_products(pre, where_ref, gate_ref, up_ref, shards, shard_width, tensor_ways):
     for ref, shift, start in shards:
-        at = shard_offset(where_ref[1], shift, shard_width, tensor_ways) + start
-        at = pl.ds(pl.multiple_of(at, 128), ref.shape[1])
+        at = pl.ds(shard_offset(where_ref[1], shift, start, shard_width, tensor_ways), ref.shape[1])
         weights = jnp.concatenate([gate_ref[:, at], up_ref[:, at]], 0)
         pre += lax.dot_general(weights, ref[...], (((1,), (1,)), ((), ())), preferred_element_type=jnp.float32)
     return pre
 
 
-def early_kernel(where_ref, gate_ref, up_ref, *refs, shifts, tensor_ways):
+def early_kernel(where_ref, gate_ref, up_ref, *refs, shifts, shard_width, tensor_ways):
     shards = [(ref, shift, 0) for ref, shift in zip(refs[:-1], shifts)]
     pre_ref = refs[-1]
     zeros = jnp.zeros(pre_ref.shape, jnp.float32)
-    pre_ref[...] = add_products(zeros, where_ref, gate_ref, up_ref, shards, refs[0].shape[1], tensor_ways)
+    pre_ref[...] = add_products(zeros, where_ref, gate_ref, up_ref, shards, shard_width, tensor_ways)
 
 
 def early_products(where, w_gate, w_up, shards, tensor_ways):
     vmem = pl.BlockSpec(memory_space=pltpu.VMEM)
     return pl.pallas_call(
-        functools.partial(early_kernel, shifts=[shift for _, shift in shards], tensor_ways=tensor_ways),
+        functools.partial(
+            early_kernel,
+            shifts=[shift for _, shift in shards],
+            shard_width=w_gate.shape[1] // tensor_ways,
+            tensor_ways=tensor_ways,
+        ),
         out_shape=jax.ShapeDtypeStruct((2 * w_gate.shape[0], shards[0][0].shape[0]), jnp.float32),
         in_specs=[pl.BlockSpec(memory_space=pltpu.SMEM)] + [vmem] * (2 + len(shards)),
         out_specs=vmem,
@@ -150,13 +160,13 @@
 
 def gradient_kernel(where_ref, pre_ref, gate_ref, up_ref, cot_ref, error_ref, *refs, places, early, shard_width, tensor_ways, scale):
     sources = refs[: len(places)]
-    d_ref, send_ref, keep_ref, merged_ref, tokens_ref, sems = refs[len(places) :]
+    d_ref, send_ref, keep_ref, merged_hbm, tokens_ref, send_buf, keep_buf, merged_ref, sems = refs[len(places) :]
     rows = gate_ref.shape[0]
     lanes = send_ref.shape[2]
     slots = []
     column = 0
     for source, (shift, start) in zip(sources, places):
-        slots.append((tokens_ref.at[:, pl.ds(column, source.shape[1])], shift, start))
+        slots.append((tokens_ref.at[:, pl.ds(column, source.shape[1])], shift, start, column))
         column += source.shape[1]
     order = list(range(early, len(places))) + list(range(early))
     copies = [pltpu.make_async_copy(sources[i], slots[i][0], sems.at[i]) for i in range(len(places))]
@@ -165,7 +175,7 @@
     pre = pre_ref[...]
     for i in order[: len(places) - early]:
         copies[i].wait()
-        pre = add_products(pre, where_ref, gate_ref, up_ref, slots[i : i + 1], shard_width, tensor_ways)
+        pre = add_products(pre, where_ref, gate_ref, up_ref, [slots[i][:3]], shard_width, tensor_ways)
     gate_pre, up_pre = pre[0:rows], pre[rows:]
     squash = jax.nn.sigmoid(gate_pre)
     upstream = cot_ref[...].astype(jnp.float32)
@@ -174,26 +184,38 @@
     d_both = jnp.concatenate([d_gate, d_up], 0)
     d_ref[...] = d_both
     first = where_ref[0] == 0
+    out = []
     for i in order:
         if i < early:
             copies[i].wait()
-        ref, shift, start = slots[i]
+        ref, shift, start, column = slots[i]
         size = ref.shape[1]
-        at = pl.multiple_of(shard_offset(where_ref[1], shift, shard_width, tensor_ways) + start, 128)
+        at = shard_offset(where_ref[1], shift, start, shard_width, tensor_ways)
         grads = jnp.dot(d_both, ref[...], preferred_element_type=jnp.float32) * scale
         gate_half = grads[0:rows] + error_ref[0, :, pl.ds(at, size)].astype(jnp.float32)
         up_half = grads[rows:] + error_ref[1, :, pl.ds(at, size)].astype(jnp.float32)
-        merged_ref[0:rows, pl.ds(at, size)] = gate_half
-        merged_ref[rows:, pl.ds(at, size)] = up_half
+        merged_ref[0:rows, column : column + size] = gate_half
+        merged_ref[rows:, column : column + size] = up_half
         gate_half = gate_half.astype(jnp.bfloat16)
         up_half = up_half.astype(jnp.bfloat16)
         keep = jnp.where(first, gate_half, up_half)
         send = jnp.where(first, up_half, gate_half)
-        chunk = at // lanes
-        for k in range(size // lanes):
+        chunk, count = column // lanes, size // lanes
+        for k in range(count):
             part = slice(k * lanes, (k + 1) * lanes)
-            keep_ref[chunk + k] = keep[:, part]
-            send_ref[chunk + k] = send[:, part]
+            keep_buf[chunk + k] = keep[:, part]
+            send_buf[chunk + k] = send[:, part]
+        here, there = pl.ds(chunk, count), pl.ds(at // lanes, count)
+        for source, target in (
+            (send_buf.at[here], send_ref.at[there]),
+            (keep_buf.at[here], keep_ref.at[there]),
+            (merged_ref.at[:, pl.ds(column, size)], merged_hbm.at[:, pl.ds(at, size)]),
+        ):
+            copy = pltpu.make_async_copy(source, target, sems.at[len(places) + len(out)])
+            copy.start()
+            out.append(copy)
+    for copy in out:
+        copy.wait()
 
 
 def gradients(where, pre, shards, early, w_gate, w_up, cot, error_fb, n_chips, tensor_ways):
@@ -202,11 +224,9 @@
     lanes = width // n_chips
     vmem = pl.BlockSpec(memory_space=pltpu.VMEM)
     here = pl.BlockSpec(memory_space=pl.ANY)
-    whole_width = shards[0][0].shape[1]
-    operands = [
-        pltpu.with_memory_space_constraint(shard, pltpu.HBM) if shard.shape[1] == whole_width else shard
-        for shard, _, _ in shards
-    ]
+    last = 2
+    operands = [pltpu.with_memory_space_constraint(shard, pltpu.HBM) for shard, _, _ in shards[:-last]]
+    operands += [shard for shard, _, _ in shards[-last:]]
     return pl.pallas_call(
         functools.partial(
             gradient_kernel,
@@ -218,13 +238,19 @@
         ),
         out_shape=(
             jax.ShapeDtypeStruct((2 * rows, count), jnp.bfloat16),
-            jax.ShapeDtypeStruct((n_chips, rows, lanes), jnp.bfloat16),
-            jax.ShapeDtypeStruct((n_chips, rows, lanes), jnp.bfloat16),
-            jax.ShapeDtypeStruct((2 * rows, width), jnp.float32),
+            pltpu.HBM((n_chips, rows, lanes), jnp.bfloat16),
+            pltpu.HBM((n_chips, rows, lanes), jnp.bfloat16),
+            pltpu.HBM((2 * rows, width), jnp.float32),
         ),
         in_specs=[pl.BlockSpec(memory_space=pltpu.SMEM)] + [vmem] * 5 + [here] * len(shards),
-        out_specs=(vmem,) * 4,
-        scratch_shapes=[pltpu.VMEM((count, width), jnp.bfloat16), pltpu.SemaphoreType.DMA((len(shards),))],
+        out_specs=(vmem, here, here, here),
+        scratch_shapes=[
+            pltpu.VMEM((count, width), jnp.bfloat16),
+            pltpu.VMEM((n_chips, rows, lanes), jnp.bfloat16),
+            pltpu.VMEM((n_chips, rows, lanes), jnp.bfloat16),
+            pltpu.VMEM((2 * rows, width), jnp.float32),
+            pltpu.SemaphoreType.DMA((4 * len(shards),)),
+        ],
         compiler_params=pltpu.CompilerParams(vmem_limit_bytes=VMEM_BYTES),
         name="gradients",
     )(where, pre, w_gate, w_up, cot.T, error_fb.reshape(2, rows, width), *operands)
@@ -249,6 +275,46 @@
         compiler_params=pltpu.CompilerParams(vmem_limit_bytes=VMEM_BYTES),
         name="act_terms",
     )(d_both, w_gate, w_up)
+
+
+def pair_kernel(keep_hbm, got_hbm, sum_ref, keep_ref, got_ref, sems):
+    parts = sems.shape[1]
+    step = sum_ref.shape[0] // parts
+
+    def load(k):
+        at = pl.ds(k * step, step)
+        return (
+            pltpu.make_async_copy(keep_hbm.at[at], keep_ref.at[at], sems.at[0, k]),
+            pltpu.make_async_copy(got_hbm.at[at], got_ref.at[at], sems.at[1, k]),
+        )
+
+    for k in range(parts):
+        for copy in load(k):
+            copy.start()
+    for k in range(parts):
+        for copy in load(k):
+            copy.wait()
+        for i in range(k * step, (k + 1) * step):
+            total = keep_ref[i].astype(jnp.float32) + got_ref[i].astype(jnp.float32)
+            sum_ref[i] = total.astype(jnp.bfloat16)
+
+
+def pair_sum(keep, got):
+    vmem = pl.BlockSpec(memory_space=pltpu.VMEM)
+    here = pl.BlockSpec(memory_space=pl.ANY)
+    return pl.pallas_call(
+        pair_kernel,
+        out_shape=jax.ShapeDtypeStruct(keep.shape, jnp.bfloat16),
+        in_specs=[here] * 2,
+        out_specs=vmem,
+        scratch_shapes=[
+            pltpu.VMEM(keep.shape, jnp.bfloat16),
+            pltpu.VMEM(keep.shape, jnp.bfloat16),
+            pltpu.SemaphoreType.DMA((2, 4)),
+        ],
+        compiler_params=pltpu.CompilerParams(vmem_limit_bytes=VMEM_BYTES),
+        name="pair_sum",
+    )(pltpu.with_memory_space_constraint(keep, pltpu.HBM), got)
 
 
 def mean_kernel(pieces_ref, copies_ref, *, scale):
@@ -299,7 +365,7 @@
     )
     act = act_terms(d_both, w_gate, w_up)
     got = lax.ppermute(send, "core", SWAP)
-    pieces = (keep.astype(jnp.float32) + got.astype(jnp.float32)).astype(jnp.bfloat16)
+    pieces = pair_sum(keep, got)
     pieces, act = lax.optimization_barrier((pieces, act))
     d_tokens = lax.psum_scatter(act, "tensor", scatter_dimension=1, tiled=True)
     pieces = lax.all_to_all(pieces, CHIPS, 0, 0, tiled=True)

time: 158 us -> 155 us (0.981)
  blocking collectives: 57 us -> 54.2 us
  other arithmetic: 2.17 us -> 0.08 us
    all_to_all x1, blocking collectives: 33.2 us -> 30.3 us  [on_device(): pieces = lax.all_to_all(pieces, CHIPS, 0, 0, tiled=True)]
    convert_element_type x1 -> x0, other arithmetic: 2.09 us -> none  [on_device(): (keep.astype(jnp.float32) + got.astype(jnp.float32)).astype(jnp.bfloat16)]
    ppermute x1, starting transfers between devices: 8.28 us -> 6.45 us  [on_device(): got = lax.ppermute(send, 'core', SWAP)]
    pallas_call x0 -> x1, Pallas kernels: none -> 1.7 us  [pair_sum(): pl.pallas_call(pair_kernel, out_shape=jax.ShapeDtypeStruct(keep.shape, jn...]
    ppermute x8, starting transfers between devices: 29.3 us -> 30.9 us  [ring(): lax.ppermute(value, 'tensor', [(i, (i + step) % ways) for i in range(ways)])]
    unnamed x30 -> x28, local copies, waits for them, and re-layouts: 4.28 us -> 3.22 us
  transfers between devices with their start and end apart: 11 -> 11, of which waited for: 6 -> 6; matrix products, arithmetic and copies ran while one was open for 0% -> 0% of each run, Pallas kernels for 10% -> 9%
where the time goes in v4:
time: 155 us; the launch traced here: 154 us
  blocking collectives  54.2 us (35%)
  starting transfers between devices  44.3 us (29%)
  Pallas kernels  21.4 us (14%)
  waiting for transfers between devices  16 us (10%)
  between operations  14.3 us (9%)
  local copies, waits for them, and re-layouts  3.4 us (2%)
    ppermute x8, starting transfers between devices, ring(): lax.ppermute(value, 'tensor', [(i, (i + step) % ways) for i in range(ways)])  30.9 us
    all_to_all x1, blocking collectives, on_device(): pieces = lax.all_to_all(pieces, CHIPS, 0, 0, tiled=True)  30.3 us
    all_to_all x1, blocking collectives, on_device(): own_half = lax.all_to_all(copies, CHIPS, 0, 0, tiled=True)  23.9 us
    ppermute x8, waiting for transfers between devices, ring(): lax.ppermute(value, 'tensor', [(i, (i + step) % ways) for i in range(ways)])  14.4 us
    pallas_call x1, Pallas kernels, finish(): pl.pallas_call(finish_kernel, out_shape=(jax.ShapeDtypeStruct((2, rows, w...  10.4 us
    ppermute x1, starting transfers between devices, on_device(): other_half = lax.ppermute(own_half, 'core', SWAP)  6.86 us
    ppermute x1, starting transfers between devices, on_device(): got = lax.ppermute(send, 'core', SWAP)  6.45 us
    pallas_call x1, Pallas kernels, gradients(): pl.pallas_call(functools.partial(gradient_kernel, places=[(shift, start)...  5.22 us
  transfers between devices with their start and end apart: 11, of which 6 were waited for; matrix products, arithmetic and copies ran while one was open for 0% of the time, Pallas kernels for 9%

profile of v4, /device:TPU:1, one launch (start us, length us, event | category | flops | bytes accessed | tf_op | source)
XLA Modules:
  0.0 153.6 jit_solution(2597797436774176380)
XLA Ops:
  7.2 0.0 reduce-scatter.2.cloned.1.call-start
  7.2 4.0 %collective-permute-start = (bf16[384,512]{1,0:T(8,128)(2,1)}, bf16[384,512]{1,0:T(8,128)(2,1)S(1)}, u32[]{:S(2)}, u32[]{:S(2)}) collective-permute-start(bf16[384,512]{1,0:T(8,128)(2,1)} %refs_0_.3), channel_id=1, source_target_pairs={{0,1},{1,2},{2,3},{3,4},{4,5},{5,6},{6,7},{7,0},{8,9},{9,10},{10,1... | collective-permute-start | bytes 1179656 | tf_op jit(solution)/shard_map/ppermute | solution.py:343
  11.3 3.8 %collective-permute-start.3 = (bf16[384,512]{1,0:T(8,128)(2,1)}, bf16[384,512]{1,0:T(8,128)(2,1)S(1)}, u32[]{:S(2)}, u32[]{:S(2)}) collective-permute-start(bf16[384,512]{1,0:T(8,128)(2,1)} %refs_0_.3), channel_id=1, source_target_pairs={{0,7},{1,0},{2,1},{3,2},{4,3},{5,4},{6,5},{7,6},{8,15},{9,8},{10,9... | collective-permute-start | bytes 1179656 | tf_op jit(solution)/shard_map/ppermute | solution.py:343
  15.1 3.4 %collective-permute-done.refs_1_ = bf16[384,512]{1,0:T(8,128)(2,1)S(1)} collective-permute-done((bf16[384,512]{1,0:T(8,128)(2,1)}, bf16[384,512]{1,0:T(8,128)(2,1)S(1)}, u32[]{:S(2)}, u32[]{:S(2)}) %collective-permute-start) | collective-permute-done | bytes 393248 | tf_op jit(solution)/shard_map/ppermute | solution.py:343
  18.5 4.0 %collective-permute-start.1 = (bf16[384,512]{1,0:T(8,128)(2,1)S(1)}, bf16[384,512]{1,0:T(8,128)(2,1)S(1)}, u32[]{:S(2)}, u32[]{:S(2)}) collective-permute-start(bf16[384,512]{1,0:T(8,128)(2,1)S(1)} %collective-permute-done.refs_1_), channel_id=1, source_target_pairs={{0,1},{1,2},{2,3},{3,4},{4,5},{5,6},{6,7},{7,0},{8,9},{9,10},{10,1... | collective-permute-start | bytes 1179656 | tf_op jit(solution)/shard_map/ppermute | solution.py:343
  22.6 4.6 %collective-permute-start.4 = (bf16[384,512]{1,0:T(8,128)(2,1)S(1)}, bf16[384,512]{1,0:T(8,128)(2,1)S(1)}, u32[]{:S(2)}, u32[]{:S(2)}) collective-permute-start(bf16[384,512]{1,0:T(8,128)(2,1)S(1)} %collective-permute-done.3.refs_2_), channel_id=1, source_target_pairs={{0,7},{1,0},{2,1},{3,2},{4,3},{5,4},{6,5},{7,6},{8,15},{9,8},{10,9... | collective-permute-start | bytes 1179656 | tf_op jit(solution)/shard_map/ppermute | solution.py:343
  27.2 3.2 %collective-permute-done.1.refs_3_ = bf16[384,512]{1,0:T(8,128)(2,1)S(1)} collective-permute-done((bf16[384,512]{1,0:T(8,128)(2,1)S(1)}, bf16[384,512]{1,0:T(8,128)(2,1)S(1)}, u32[]{:S(2)}, u32[]{:S(2)}) %collective-permute-start.1) | collective-permute-done | bytes 393248 | tf_op jit(solution)/shard_map/ppermute | solution.py:343
  30.4 3.0 %collective-permute-start.2 = (bf16[384,512]{1,0:T(8,128)(2,1)S(1)}, bf16[384,512]{1,0:T(8,128)(2,1)S(1)}, u32[]{:S(2)}, u32[]{:S(2)}) collective-permute-start(bf16[384,512]{1,0:T(8,128)(2,1)S(1)} %collective-permute-done.1.refs_3_), channel_id=1, source_target_pairs={{0,1},{1,2},{2,3},{3,4},{4,5},{5,6},{6,7},{7,0},{8,9},{9,10},{10,1... | collective-permute-start | bytes 1179656 | tf_op jit(solution)/shard_map/ppermute | solution.py:343
  33.4 4.7 %collective-permute-start.5 = (bf16[384,512]{1,0:T(8,128)(2,1)S(1)}, bf16[384,512]{1,0:T(8,128)(2,1)S(1)}, u32[]{:S(2)}, u32[]{:S(2)}) collective-permute-start(bf16[384,512]{1,0:T(8,128)(2,1)S(1)} %collective-permute-done.4.refs_4_), channel_id=1, source_target_pairs={{0,7},{1,0},{2,1},{3,2},{4,3},{5,4},{6,5},{7,6},{8,15},{9,8},{10,9... | collective-permute-start | bytes 1179656 | tf_op jit(solution)/shard_map/ppermute | solution.py:343
  38.1 0.1 pad_add_fusion.where_ref
  38.2 1.1 copy-done
  39.3 1.1 copy-done.2
  40.4 1.0 copy-done.4
  41.4 1.3 early_products.1.pre_ref
  42.7 2.4 %collective-permute-done.5.refs_6_ = bf16[384,512]{1,0:T(8,128)(2,1)S(1)} collective-permute-done((bf16[384,512]{1,0:T(8,128)(2,1)S(1)}, bf16[384,512]{1,0:T(8,128)(2,1)S(1)}, u32[]{:S(2)}, u32[]{:S(2)}) %collective-permute-start.5) | collective-permute-done | bytes 393248 | tf_op jit(solution)/shard_map/ppermute | solution.py:343
  45.1 4.8 %collective-permute-start.6 = (bf16[384,256]{1,0:T(8,128)(2,1)S(1)}, bf16[384,256]{1,0:T(8,128)(2,1)S(1)}, u32[]{:S(2)}, u32[]{:S(2)}) collective-permute-start(bf16[384,256]{1,0:T(8,128)(2,1)S(1)} %slice.8), channel_id=1, source_target_pairs={{0,1},{1,2},{2,3},{3,4},{4,5},{5,6},{6,7},{7,0},{8,9},{9,10},{10,1... | collective-permute-start | bytes 589832 | tf_op jit(solution)/shard_map/ppermute | solution.py:343
  50.0 1.9 %collective-permute-start.7 = (bf16[384,256]{1,0:T(8,128)(2,1)S(1)}, bf16[384,256]{1,0:T(8,128)(2,1)S(1)}, u32[]{:S(2)}, u32[]{:S(2)}) collective-permute-start(bf16[384,256]{1,0:T(8,128)(2,1)S(1)} %slice.9), channel_id=1, source_target_pairs={{0,7},{1,0},{2,1},{3,2},{4,3},{5,4},{6,5},{7,6},{8,15},{9,8},{10,9... | collective-permute-start | bytes 589832 | tf_op jit(solution)/shard_map/ppermute | solution.py:343
  51.9 0.9 collective-permute-done.6.refs_7_
  52.7 4.5 %collective-permute-done.7.refs_8_ = bf16[384,256]{1,0:T(8,128)(2,1)S(1)} collective-permute-done((bf16[384,256]{1,0:T(8,128)(2,1)S(1)}, bf16[384,256]{1,0:T(8,128)(2,1)S(1)}, u32[]{:S(2)}, u32[]{:S(2)}) %collective-permute-start.7) | collective-permute-done | bytes 196640 | tf_op jit(solution)/shard_map/ppermute | solution.py:343
  57.4 5.2 %gradients.1 = (bf16[160,384]{1,0:T(8,128)(2,1)S(1)}, bf16[32,80,128]{2,1,0:T(8,128)(2,1)}, bf16[32,80,128]{2,1,0:T(8,128)(2,1)}, f32[160,4096]{1,0:T(8,128)}) custom-call(s32[2]{0:T(128)S(1)} %pad_add_fusion.where_ref, f32[160,384]{1,0:T(8,128)S(1)} %early_products.1.pre_ref, bf16[80,4096]{1,0:T(8,128)(2,1)S(1)} %copy-done, bf16[80,4096]{1,0:T(8,128)(2,1)S(1)} %copy-done.2, ...), custom_call_target="tpu_custom_call" | custom-call | tf_op jit(solution)/shard_map/gradients/pallas_call | solution.py:230
  62.6 6.4 %collective-permute-start.8 = (bf16[32,80,128]{2,1,0:T(8,128)(2,1)}, bf16[32,80,128]{2,1,0:T(8,128)(2,1)S(1)}, u32[]{:S(2)}, u32[]{:S(2)}) collective-permute-start(bf16[32,80,128]{2,1,0:T(8,128)(2,1)} %get-tuple-element.18), channel_id=1, source_target_pairs={{0,8},{8,0},{1,9},{9,1},{2,10},{10,2},{3,11},{11,3},{4,12},{12,4},... | collective-permute-start | bytes 1966088 | tf_op jit(solution)/shard_map/ppermute | solution.py:367
  69.1 2.6 %act_terms.1 = bf16[384,4096]{1,0:T(8,128)(2,1)} custom-call(bf16[160,384]{1,0:T(8,128)(2,1)S(1)} %get-tuple-element.19.d_ref, bf16[80,4096]{1,0:T(8,128)(2,1)S(1)} %copy-done.1, bf16[80,4096]{1,0:T(8,128)(2,1)S(1)} %copy-done.3), custom_call_target="tpu_custom_call" | custom-call | tf_op jit(solution)/shard_map/act_terms/pallas_call | solution.py:270
  71.7 1.7 %pair_sum.1 = bf16[32,80,128]{2,1,0:T(8,128)(2,1)S(1)} custom-call(bf16[32,80,128]{2,1,0:T(8,128)(2,1)} %get-tuple-element.17.keep_hbm, bf16[32,80,128]{2,1,0:T(8,128)(2,1)S(1)} %collective-permute-done.8.got_hbm), custom_call_target="tpu_custom_call" | custom-call | tf_op jit(solution)/shard_map/pair_sum/pallas_call | solution.py:305
  73.5 30.3 %all_to_all.10.pieces_ref = bf16[32,80,128]{2,1,0:T(8,128)(2,1)S(1)} all-to-all(bf16[32,80,128]{2,1,0:T(8,128)(2,1)S(1)} %pair_sum.1), channel_id=1, replica_groups=mesh['x'=4,'z'=8,'core'=2,'tensor'=8] {'x','z'}, dimensions={0} | all-to-all | bytes 1310720 | tf_op jit(solution)/shard_map/all_to_all | solution.py:371
  103.8 0.1 mean_copies.1
  103.9 23.9 %all_to_all.11.own_ref = bf16[32,80,128]{2,1,0:T(8,128)(2,1)S(1)} all-to-all(bf16[32,80,128]{2,1,0:T(8,128)(2,1)S(1)} %mean_copies.1), channel_id=1, replica_groups=mesh['x'=4,'z'=8,'core'=2,'tensor'=8] {'x','z'}, dimensions={0} | all-to-all | bytes 1310720 | tf_op jit(solution)/shard_map/all_to_all | solution.py:373
  127.8 6.9 %collective-permute-start.9 = (bf16[32,80,128]{2,1,0:T(8,128)(2,1)S(1)}, bf16[32,80,128]{2,1,0:T(8,128)(2,1)S(1)}, u32[]{:S(2)}, u32[]{:S(2)}) collective-permute-start(bf16[32,80,128]{2,1,0:T(8,128)(2,1)S(1)} %all_to_all.11.own_ref), channel_id=1, source_target_pairs={{0,8},{8,0},{1,9},{9,1},{2,10},{10,2},{3,11},{11,3},{4,12},{12,4},... | collective-permute-start | bytes 1966088 | tf_op jit(solution)/shard_map/ppermute | solution.py:374
  134.7 0.1 copy.9
  134.7 0.1 reshape.16.q_ref
  134.8 1.5 collective-permute-done.9.other_ref
  136.4 10.4 %finish.1 = (bf16[2,80,4096]{2,1,0:T(8,128)(2,1)}, f32[2,64,80]{2,1,0:T(8,128)}) custom-call(s32[2]{0:T(128)S(1)} %pad_add_fusion.where_ref, bf16[32,80,128]{2,1,0:T(8,128)(2,1)S(1)} %all_to_all.11.own_ref, bf16[32,80,128]{2,1,0:T(8,128)(2,1)S(1)} %collective-permute-done.9.other_ref, f32[64,160]{1,0:T(8,128)S(1)} %reshape.16.q_ref, ...), custom_call_target="tpu_custom_call" | custom-call | tf_op jit(solution)/shard_map/finish/pallas_call | solution.py:106
  146.8 0.0 reduce-scatter.2.cloned.1.call-done
  (32 shorter events, 0.1 us)
Async XLA Ops:
  7.2 139.6 %reduce-scatter.2.cloned.1.call-start = ((), (), s32[]{:S(2)}) async-start(), calls=%async_computation.3 | async-start | bytes 3538944 | tf_op jit(solution)/shard_map/reduce_scatter | solution.py:370
  7.2 11.3 %collective-permute-start = (bf16[384,512]{1,0:T(8,128)(2,1)}, bf16[384,512]{1,0:T(8,128)(2,1)S(1)}, u32[]{:S(2)}, u32[]{:S(2)}) collective-permute-start(bf16[384,512]{1,0:T(8,128)(2,1)} %refs_0_.3), channel_id=1, source_target_pairs={{0,1},{1,2},{2,3},{3,4},{4,5},{5,6},{6,7},{7,0},{8,9},{9,10},{10,1... | collective-permute-start | bytes 1179656 | tf_op jit(solution)/shard_map/ppermute | solution.py:343
  11.3 11.3 %collective-permute-start.3 = (bf16[384,512]{1,0:T(8,128)(2,1)}, bf16[384,512]{1,0:T(8,128)(2,1)S(1)}, u32[]{:S(2)}, u32[]{:S(2)}) collective-permute-start(bf16[384,512]{1,0:T(8,128)(2,1)} %refs_0_.3), channel_id=1, source_target_pairs={{0,7},{1,0},{2,1},{3,2},{4,3},{5,4},{6,5},{7,6},{8,15},{9,8},{10,9... | collective-permute-start | bytes 1179656 | tf_op jit(solution)/shard_map/ppermute | solution.py:343
  18.5 38.8 %copy-start.5 = (bf16[384,512]{1,0:T(8,128)(2,1)}, bf16[384,512]{1,0:T(8,128)(2,1)S(1)}, u32[]{:S(2)}) copy-start(bf16[384,512]{1,0:T(8,128)(2,1)S(1)} %collective-permute-done.refs_1_) | copy-start | bytes 1179652
  18.5 11.9 %collective-permute-start.1 = (bf16[384,512]{1,0:T(8,128)(2,1)S(1)}, bf16[384,512]{1,0:T(8,128)(2,1)S(1)}, u32[]{:S(2)}, u32[]{:S(2)}) collective-permute-start(bf16[384,512]{1,0:T(8,128)(2,1)S(1)} %collective-permute-done.refs_1_), channel_id=1, source_target_pairs={{0,1},{1,2},{2,3},{3,4},{4,5},{5,6},{6,7},{7,0},{8,9},{9,10},{10,1... | collective-permute-start | bytes 1179656 | tf_op jit(solution)/shard_map/ppermute | solution.py:343
  22.5 34.8 %copy-start.6 = (bf16[384,512]{1,0:T(8,128)(2,1)}, bf16[384,512]{1,0:T(8,128)(2,1)S(1)}, u32[]{:S(2)}) copy-start(bf16[384,512]{1,0:T(8,128)(2,1)S(1)} %collective-permute-done.3.refs_2_) | copy-start | bytes 1179652
  22.6 10.8 %collective-permute-start.4 = (bf16[384,512]{1,0:T(8,128)(2,1)S(1)}, bf16[384,512]{1,0:T(8,128)(2,1)S(1)}, u32[]{:S(2)}, u32[]{:S(2)}) collective-permute-start(bf16[384,512]{1,0:T(8,128)(2,1)S(1)} %collective-permute-done.3.refs_2_), channel_id=1, source_target_pairs={{0,7},{1,0},{2,1},{3,2},{4,3},{5,4},{6,5},{7,6},{8,15},{9,8},{10,9... | collective-permute-start | bytes 1179656 | tf_op jit(solution)/shard_map/ppermute | solution.py:343
  30.4 26.9 %copy-start.7 = (bf16[384,512]{1,0:T(8,128)(2,1)}, bf16[384,512]{1,0:T(8,128)(2,1)S(1)}, u32[]{:S(2)}) copy-start(bf16[384,512]{1,0:T(8,128)(2,1)S(1)} %collective-permute-done.1.refs_3_) | copy-start | bytes 1179652
  30.4 12.3 %collective-permute-start.2 = (bf16[384,512]{1,0:T(8,128)(2,1)S(1)}, bf16[384,512]{1,0:T(8,128)(2,1)S(1)}, u32[]{:S(2)}, u32[]{:S(2)}) collective-permute-start(bf16[384,512]{1,0:T(8,128)(2,1)S(1)} %collective-permute-done.1.refs_3_), channel_id=1, source_target_pairs={{0,1},{1,2},{2,3},{3,4},{4,5},{5,6},{6,7},{7,0},{8,9},{9,10},{10,1... | collective-permute-start | bytes 1179656 | tf_op jit(solution)/shard_map/ppermute | solution.py:343
  33.4 23.9 %copy-start.8 = (bf16[384,512]{1,0:T(8,128)(2,1)}, bf16[384,512]{1,0:T(8,128)(2,1)S(1)}, u32[]{:S(2)}) copy-start(bf16[384,512]{1,0:T(8,128)(2,1)S(1)} %collective-permute-done.4.refs_4_) | copy-start | bytes 1179652
  33.4 11.7 %collective-permute-start.5 = (bf16[384,512]{1,0:T(8,128)(2,1)S(1)}, bf16[384,512]{1,0:T(8,128)(2,1)S(1)}, u32[]{:S(2)}, u32[]{:S(2)}) collective-permute-start(bf16[384,512]{1,0:T(8,128)(2,1)S(1)} %collective-permute-done.4.refs_4_), channel_id=1, source_target_pairs={{0,7},{1,0},{2,1},{3,2},{4,3},{5,4},{6,5},{7,6},{8,15},{9,8},{10,9... | collective-permute-start | bytes 1179656 | tf_op jit(solution)/shard_map/ppermute | solution.py:343
  38.2 1.1 copy-start
  39.3 1.1 copy-start.2
  40.4 1.0 copy-start.4
  41.4 16.0 %copy-start.9 = (bf16[1,2,80,4096]{3,2,1,0:T(8,128)(2,1)S(1)}, bf16[1,2,80,4096]{3,2,1,0:T(8,128)(2,1)}, u32[]{:S(2)}) copy-start(bf16[1,2,80,4096]{3,2,1,0:T(8,128)(2,1)} %param.10) | copy-start | bytes 3932164
  41.4 16.0 %copy-start.10 = (bf16[384,80]{0,1:T(8,128)(2,1)S(1)}, bf16[384,80]{0,1:T(8,128)(2,1)}, u32[]{:S(2)}) copy-start(bf16[384,80]{0,1:T(8,128)(2,1)} %param.9) | copy-start | bytes 184324
  42.7 14.6 %copy-start.11 = (bf16[384,512]{1,0:T(8,128)(2,1)}, bf16[384,512]{1,0:T(8,128)(2,1)S(1)}, u32[]{:S(2)}) copy-start(bf16[384,512]{1,0:T(8,128)(2,1)S(1)} %collective-permute-done.2.refs_5_) | copy-start | bytes 1179652
  45.1 12.2 %copy-start.12 = (bf16[384,512]{1,0:T(8,128)(2,1)}, bf16[384,512]{1,0:T(8,128)(2,1)S(1)}, u32[]{:S(2)}) copy-start(bf16[384,512]{1,0:T(8,128)(2,1)S(1)} %collective-permute-done.5.refs_6_) | copy-start | bytes 1179652
  45.1 7.6 %collective-permute-start.6 = (bf16[384,256]{1,0:T(8,128)(2,1)S(1)}, bf16[384,256]{1,0:T(8,128)(2,1)S(1)}, u32[]{:S(2)}, u32[]{:S(2)}) collective-permute-start(bf16[384,256]{1,0:T(8,128)(2,1)S(1)} %slice.8), channel_id=1, source_target_pairs={{0,1},{1,2},{2,3},{3,4},{4,5},{5,6},{6,7},{7,0},{8,9},{9,10},{10,1... | collective-permute-start | bytes 589832 | tf_op jit(solution)/shard_map/ppermute | solution.py:343
  50.0 7.3 %collective-permute-start.7 = (bf16[384,256]{1,0:T(8,128)(2,1)S(1)}, bf16[384,256]{1,0:T(8,128)(2,1)S(1)}, u32[]{:S(2)}, u32[]{:S(2)}) collective-permute-start(bf16[384,256]{1,0:T(8,128)(2,1)S(1)} %slice.9), channel_id=1, source_target_pairs={{0,7},{1,0},{2,1},{3,2},{4,3},{5,4},{6,5},{7,6},{8,15},{9,8},{10,9... | collective-permute-start | bytes 589832 | tf_op jit(solution)/shard_map/ppermute | solution.py:343
  57.4 11.7 %copy-start.1 = (bf16[80,4096]{1,0:T(8,128)(2,1)S(1)}, bf16[80,4096]{1,0:T(8,128)(2,1)}, u32[]{:S(2)}) copy-start(bf16[80,4096]{1,0:T(8,128)(2,1)} %gate_ref.5) | copy-start | bytes 1966084
  57.4 11.7 %copy-start.3 = (bf16[80,4096]{1,0:T(8,128)(2,1)S(1)}, bf16[80,4096]{1,0:T(8,128)(2,1)}, u32[]{:S(2)}) copy-start(bf16[80,4096]{1,0:T(8,128)(2,1)} %up_ref.5) | copy-start | bytes 1966084
  62.6 9.1 %collective-permute-start.8 = (bf16[32,80,128]{2,1,0:T(8,128)(2,1)}, bf16[32,80,128]{2,1,0:T(8,128)(2,1)S(1)}, u32[]{:S(2)}, u32[]{:S(2)}) collective-permute-start(bf16[32,80,128]{2,1,0:T(8,128)(2,1)} %get-tuple-element.18), channel_id=1, source_target_pairs={{0,8},{8,0},{1,9},{9,1},{2,10},{10,2},{3,11},{11,3},{4,12},{12,4},... | collective-permute-start | bytes 1966088 | tf_op jit(solution)/shard_map/ppermute | solution.py:367
  73.5 61.2 %copy-start.13 = (f32[2,80,64]{1,2,0:T(8,128)S(1)}, f32[2,80,64]{1,2,0:T(8,128)}, u32[]{:S(2)}) copy-start(f32[2,80,64]{1,2,0:T(8,128)} %param.11) | copy-start | bytes 122884
  127.8 8.6 %collective-permute-start.9 = (bf16[32,80,128]{2,1,0:T(8,128)(2,1)S(1)}, bf16[32,80,128]{2,1,0:T(8,128)(2,1)S(1)}, u32[]{:S(2)}, u32[]{:S(2)}) collective-permute-start(bf16[32,80,128]{2,1,0:T(8,128)(2,1)S(1)} %all_to_all.11.own_ref), channel_id=1, source_target_pairs={{0,8},{8,0},{1,9},{9,1},{2,10},{10,2},{3,11},{11,3},{4,12},{12,4},... | collective-permute-start | bytes 1966088 | tf_op jit(solution)/shard_map/ppermute | solution.py:374
Sparse Core Ops, SparseCore 0:
  73.6 49.8 reduce-scatter.1

commit v5 on v4

--- a/solution.py
+++ b/solution.py
@@ -52,7 +52,7 @@
     return (rows - ratio * pltpu.roll(rows, 1, 0)) * lax.rsqrt(diagonal - ratio * beside)
 
 
-def finish_kernel(where_ref, own_ref, other_ref, q_ref, merged_hbm, new_ref, q_next_ref, stack_ref, merged_ref, sem):
+def finish_kernel(where_ref, own_ref, other_ref, q_ref, merged_hbm, new_hbm, q_next_ref, stack_ref, merged_ref, new_ref, sem, out_sems):
     load = pltpu.make_async_copy(merged_hbm, merged_ref, sem)
     load.start()
     chunks, rows, lanes = own_ref.shape
@@ -88,6 +88,7 @@
     high, middle, _ = three_parts(weights)
     factors = jnp.concatenate([high, high, middle], 1)
     load.wait()
+    out = []
     for f in range(0, width, step):
         p_high = stack_ref[units : units + rank, f : f + step]
         p_middle = stack_ref[units + rank : units + 2 * rank, f : f + step]
@@ -96,6 +97,12 @@
         fresh = (merged_ref[:, f : f + step] - approximation).astype(jnp.bfloat16)
         new_ref[0, :, f : f + step] = fresh[0:rows]
         new_ref[1, :, f : f + step] = fresh[rows:]
+        at = (slice(None), slice(None), pl.ds(f, step))
+        copy = pltpu.make_async_copy(new_ref.at[at], new_hbm.at[at], out_sems.at[f // step])
+        copy.start()
+        out.append(copy)
+    for copy in out:
+        copy.wait()
 
 
 def finish(where, own, other, q_prev, merged):
@@ -110,11 +117,13 @@
             jax.ShapeDtypeStruct((2, rank, rows), jnp.float32),
         ),
         in_specs=[pl.BlockSpec(memory_space=pltpu.SMEM), vmem, vmem, vmem, pl.BlockSpec(memory_space=pl.ANY)],
-        out_specs=(vmem, vmem),
+        out_specs=(pl.BlockSpec(memory_space=pl.ANY), vmem),
         scratch_shapes=[
             pltpu.VMEM((2 * rows + 3 * rank, width), jnp.bfloat16),
             pltpu.VMEM((2 * rows, width), jnp.float32),
+            pltpu.VMEM((2, rows, width), jnp.bfloat16),
             pltpu.SemaphoreType.DMA,
+            pltpu.SemaphoreType.DMA((width // 1024,)),
         ],
         compiler_params=pltpu.CompilerParams(vmem_limit_bytes=VMEM_BYTES),
         name="finish",
@@ -135,13 +144,13 @@
 
 
 def early_kernel(where_ref, gate_ref, up_ref, *refs, shifts, shard_width, tensor_ways):
-    shards = [(ref, shift, 0) for ref, shift in zip(refs[:-1], shifts)]
-    pre_ref = refs[-1]
-    zeros = jnp.zeros(pre_ref.shape, jnp.float32)
-    pre_ref[...] = add_products(zeros, where_ref, gate_ref, up_ref, shards, shard_width, tensor_ways)
-
-
-def early_products(where, w_gate, w_up, shards, tensor_ways):
+    shards = [(ref, shift, 0) for ref, shift in zip(refs, shifts)]
+    before, pre_ref = refs[len(shifts) : -1], refs[-1]
+    start = before[0][...] if before else jnp.zeros(pre_ref.shape, jnp.float32)
+    pre_ref[...] = add_products(start, where_ref, gate_ref, up_ref, shards, shard_width, tensor_ways)
+
+
+def early_products(where, w_gate, w_up, shards, tensor_ways, before=()):
     vmem = pl.BlockSpec(memory_space=pltpu.VMEM)
     return pl.pallas_call(
         functools.partial(
@@ -151,11 +160,11 @@
             tensor_ways=tensor_ways,
         ),
         out_shape=jax.ShapeDtypeStruct((2 * w_gate.shape[0], shards[0][0].shape[0]), jnp.float32),
-        in_specs=[pl.BlockSpec(memory_space=pltpu.SMEM)] + [vmem] * (2 + len(shards)),
+        in_specs=[pl.BlockSpec(memory_space=pltpu.SMEM)] + [vmem] * (2 + len(shards) + len(before)),
         out_specs=vmem,
         compiler_params=pltpu.CompilerParams(vmem_limit_bytes=VMEM_BYTES),
         name="early_products",
-    )(where, w_gate, w_up, *[shard for shard, _ in shards])
+    )(where, w_gate, w_up, *[shard for shard, _ in shards], *before)
 
 
 def gradient_kernel(where_ref, pre_ref, gate_ref, up_ref, cot_ref, error_ref, *refs, places, early, shard_width, tensor_ways, scale):
@@ -357,8 +366,10 @@
         shards += [(ahead, -k, 0), (behind, k, 0)]
     early = 5
     pre = early_products(where, w_gate, w_up, [shard[:2] for shard in shards[:early]], ways)
-    middle = share // 2
+    middle = share * 3 // 4
     ahead, behind, pre = lax.optimization_barrier((ahead[:, :middle], behind[:, middle:], pre))
+    pre = early_products(where, w_gate, w_up, [shard[:2] for shard in shards[early:]], ways, (pre,))
+    early = len(shards)
     shards += [(ring(ahead, 1), ways // 2, 0), (ring(behind, -1), ways // 2, middle)]
     d_both, send, keep, merged = gradients(
         where, pre, shards, early, w_gate, w_up, d_hidden, error_fb, n_chips, ways

time: 155 us -> 154 us (level)
  waiting for transfers between devices: 16 us -> 14.3 us
    ppermute x8, waiting for transfers between devices: 14.4 us -> 12.7 us  [ring(): lax.ppermute(value, 'tensor', [(i, (i + step) % ways) for i in range(ways)])]
  transfers between devices with their start and end apart: 11 -> 11, of which waited for: 6 -> 5; matrix products, arithmetic and copies ran while one was open for 0% -> 0% of each run, Pallas kernels for 9% -> 10%
where the time goes in v5:
time: 154 us; the launch traced here: 152 us
  blocking collectives  54.2 us (35%)
  starting transfers between devices  44 us (29%)
  Pallas kernels  22 us (14%)
  waiting for transfers between devices  14.3 us (9%)
  between operations  14.3 us (9%)
  local copies, waits for them, and re-layouts  3.42 us (2%)
    ppermute x8, starting transfers between devices, ring(): lax.ppermute(value, 'tensor', [(i, (i + step) % ways) for i in range(ways)])  30.9 us
    all_to_all x1, blocking collectives, on_device(): pieces = lax.all_to_all(pieces, CHIPS, 0, 0, tiled=True)  30.4 us
    all_to_all x1, blocking collectives, on_device(): own_half = lax.all_to_all(copies, CHIPS, 0, 0, tiled=True)  23.8 us
    ppermute x8, waiting for transfers between devices, ring(): lax.ppermute(value, 'tensor', [(i, (i + step) % ways) for i in range(ways)])  12.7 us
    pallas_call x1, Pallas kernels, finish(): pl.pallas_call(finish_kernel, out_shape=(jax.ShapeDtypeStruct((2, rows, w...  10.7 us
    ppermute x1, starting transfers between devices, on_device(): other_half = lax.ppermute(own_half, 'core', SWAP)  6.86 us
    ppermute x1, starting transfers between devices, on_device(): got = lax.ppermute(send, 'core', SWAP)  6.17 us
    pallas_call x1, Pallas kernels, gradients(): pl.pallas_call(functools.partial(gradient_kernel, places=[(shift, start)...  4.63 us
  transfers between devices with their start and end apart: 11, of which 5 were waited for; matrix products, arithmetic and copies ran while one was open for 0% of the time, Pallas kernels for 10%

profile of v5, /device:TPU:1, one launch (start us, length us, event | category | flops | bytes accessed | tf_op | source)
XLA Modules:
  0.0 152.3 jit_solution(12073172384930114988)
XLA Ops:
  7.2 0.0 reduce-scatter.2.cloned.1.call-start
  7.2 4.0 %collective-permute-start = (bf16[384,512]{1,0:T(8,128)(2,1)}, bf16[384,512]{1,0:T(8,128)(2,1)S(1)}, u32[]{:S(2)}, u32[]{:S(2)}) collective-permute-start(bf16[384,512]{1,0:T(8,128)(2,1)} %refs_0_.3), channel_id=1, source_target_pairs={{0,1},{1,2},{2,3},{3,4},{4,5},{5,6},{6,7},{7,0},{8,9},{9,10},{10,1... | collective-permute-start | bytes 1179656 | tf_op jit(solution)/shard_map/ppermute | solution.py:352
  11.3 3.8 %collective-permute-start.3 = (bf16[384,512]{1,0:T(8,128)(2,1)}, bf16[384,512]{1,0:T(8,128)(2,1)S(1)}, u32[]{:S(2)}, u32[]{:S(2)}) collective-permute-start(bf16[384,512]{1,0:T(8,128)(2,1)} %refs_0_.3), channel_id=1, source_target_pairs={{0,7},{1,0},{2,1},{3,2},{4,3},{5,4},{6,5},{7,6},{8,15},{9,8},{10,9... | collective-permute-start | bytes 1179656 | tf_op jit(solution)/shard_map/ppermute | solution.py:352
  15.1 3.4 %collective-permute-done.refs_1_ = bf16[384,512]{1,0:T(8,128)(2,1)S(1)} collective-permute-done((bf16[384,512]{1,0:T(8,128)(2,1)}, bf16[384,512]{1,0:T(8,128)(2,1)S(1)}, u32[]{:S(2)}, u32[]{:S(2)}) %collective-permute-start) | collective-permute-done | bytes 393248 | tf_op jit(solution)/shard_map/ppermute | solution.py:352
  18.5 4.0 %collective-permute-start.1 = (bf16[384,512]{1,0:T(8,128)(2,1)S(1)}, bf16[384,512]{1,0:T(8,128)(2,1)S(1)}, u32[]{:S(2)}, u32[]{:S(2)}) collective-permute-start(bf16[384,512]{1,0:T(8,128)(2,1)S(1)} %collective-permute-done.refs_1_), channel_id=1, source_target_pairs={{0,1},{1,2},{2,3},{3,4},{4,5},{5,6},{6,7},{7,0},{8,9},{9,10},{10,1... | collective-permute-start | bytes 1179656 | tf_op jit(solution)/shard_map/ppermute | solution.py:352
  22.6 4.6 %collective-permute-start.4 = (bf16[384,512]{1,0:T(8,128)(2,1)S(1)}, bf16[384,512]{1,0:T(8,128)(2,1)S(1)}, u32[]{:S(2)}, u32[]{:S(2)}) collective-permute-start(bf16[384,512]{1,0:T(8,128)(2,1)S(1)} %collective-permute-done.3.refs_2_), channel_id=1, source_target_pairs={{0,7},{1,0},{2,1},{3,2},{4,3},{5,4},{6,5},{7,6},{8,15},{9,8},{10,9... | collective-permute-start | bytes 1179656 | tf_op jit(solution)/shard_map/ppermute | solution.py:352
  27.2 3.2 %collective-permute-done.1.refs_3_ = bf16[384,512]{1,0:T(8,128)(2,1)S(1)} collective-permute-done((bf16[384,512]{1,0:T(8,128)(2,1)S(1)}, bf16[384,512]{1,0:T(8,128)(2,1)S(1)}, u32[]{:S(2)}, u32[]{:S(2)}) %collective-permute-start.1) | collective-permute-done | bytes 393248 | tf_op jit(solution)/shard_map/ppermute | solution.py:352
  30.4 3.0 %collective-permute-start.2 = (bf16[384,512]{1,0:T(8,128)(2,1)S(1)}, bf16[384,512]{1,0:T(8,128)(2,1)S(1)}, u32[]{:S(2)}, u32[]{:S(2)}) collective-permute-start(bf16[384,512]{1,0:T(8,128)(2,1)S(1)} %collective-permute-done.1.refs_3_), channel_id=1, source_target_pairs={{0,1},{1,2},{2,3},{3,4},{4,5},{5,6},{6,7},{7,0},{8,9},{9,10},{10,1... | collective-permute-start | bytes 1179656 | tf_op jit(solution)/shard_map/ppermute | solution.py:352
  33.4 4.7 %collective-permute-start.5 = (bf16[384,512]{1,0:T(8,128)(2,1)S(1)}, bf16[384,512]{1,0:T(8,128)(2,1)S(1)}, u32[]{:S(2)}, u32[]{:S(2)}) collective-permute-start(bf16[384,512]{1,0:T(8,128)(2,1)S(1)} %collective-permute-done.4.refs_4_), channel_id=1, source_target_pairs={{0,7},{1,0},{2,1},{3,2},{4,3},{5,4},{6,5},{7,6},{8,15},{9,8},{10,9... | collective-permute-start | bytes 1179656 | tf_op jit(solution)/shard_map/ppermute | solution.py:352
  38.1 0.1 pad_add_fusion.where_ref
  38.2 1.1 copy-done
  39.3 1.1 copy-done.2
  40.4 1.0 copy-done.6
  41.4 1.3 early_products.2.refs_2_
  42.7 2.4 %collective-permute-done.5.refs_1_.refs_6_ = bf16[384,512]{1,0:T(8,128)(2,1)S(1)} collective-permute-done((bf16[384,512]{1,0:T(8,128)(2,1)S(1)}, bf16[384,512]{1,0:T(8,128)(2,1)S(1)}, u32[]{:S(2)}, u32[]{:S(2)}) %collective-permute-start.5) | collective-permute-done | bytes 393248 | tf_op jit(solution)/shard_map/ppermute | solution.py:352
  45.1 4.8 %collective-permute-start.6 = (bf16[384,384]{1,0:T(8,128)(2,1)S(1)}, bf16[384,384]{1,0:T(8,128)(2,1)S(1)}, u32[]{:S(2)}, u32[]{:S(2)}) collective-permute-start(bf16[384,384]{1,0:T(8,128)(2,1)S(1)} %slice.8), channel_id=1, source_target_pairs={{0,1},{1,2},{2,3},{3,4},{4,5},{5,6},{6,7},{7,0},{8,9},{9,10},{10,1... | collective-permute-start | bytes 884744 | tf_op jit(solution)/shard_map/ppermute | solution.py:352
  50.0 1.9 %collective-permute-start.7 = (bf16[384,128]{1,0:T(8,128)(2,1)S(1)}, bf16[384,128]{1,0:T(8,128)(2,1)S(1)}, u32[]{:S(2)}, u32[]{:S(2)}) collective-permute-start(bf16[384,128]{1,0:T(8,128)(2,1)S(1)} %slice.9), channel_id=1, source_target_pairs={{0,7},{1,0},{2,1},{3,2},{4,3},{5,4},{6,5},{7,6},{8,15},{9,8},{10,9... | collective-permute-start | bytes 294920 | tf_op jit(solution)/shard_map/ppermute | solution.py:352
  51.9 0.9 early_products.3.pre_ref
  52.9 3.7 %collective-permute-done.7.refs_8_ = bf16[384,128]{1,0:T(8,128)(2,1)S(1)} collective-permute-done((bf16[384,128]{1,0:T(8,128)(2,1)S(1)}, bf16[384,128]{1,0:T(8,128)(2,1)S(1)}, u32[]{:S(2)}, u32[]{:S(2)}) %collective-permute-start.7) | collective-permute-done | bytes 98336 | tf_op jit(solution)/shard_map/ppermute | solution.py:352
  56.6 4.6 %gradients.1 = (bf16[160,384]{1,0:T(8,128)(2,1)S(1)}, bf16[32,80,128]{2,1,0:T(8,128)(2,1)}, bf16[32,80,128]{2,1,0:T(8,128)(2,1)}, f32[160,4096]{1,0:T(8,128)}) custom-call(s32[2]{0:T(128)S(1)} %pad_add_fusion.where_ref, f32[160,384]{1,0:T(8,128)S(1)} %early_products.3.pre_ref, bf16[80,4096]{1,0:T(8,128)(2,1)S(1)} %copy-done, bf16[80,4096]{1,0:T(8,128)(2,1)S(1)} %copy-done.2, ...), custom_call_target="tpu_custom_call" | custom-call | tf_op jit(solution)/shard_map/gradients/pallas_call | solution.py:239
  61.2 6.2 %collective-permute-start.8 = (bf16[32,80,128]{2,1,0:T(8,128)(2,1)}, bf16[32,80,128]{2,1,0:T(8,128)(2,1)S(1)}, u32[]{:S(2)}, u32[]{:S(2)}) collective-permute-start(bf16[32,80,128]{2,1,0:T(8,128)(2,1)} %get-tuple-element.18), channel_id=1, source_target_pairs={{0,8},{8,0},{1,9},{9,1},{2,10},{10,2},{3,11},{11,3},{4,12},{12,4},... | collective-permute-start | bytes 1966088 | tf_op jit(solution)/shard_map/ppermute | solution.py:378
  67.4 2.6 %act_terms.1 = bf16[384,4096]{1,0:T(8,128)(2,1)} custom-call(bf16[160,384]{1,0:T(8,128)(2,1)S(1)} %get-tuple-element.19.d_ref, bf16[80,4096]{1,0:T(8,128)(2,1)S(1)} %copy-done.1, bf16[80,4096]{1,0:T(8,128)(2,1)S(1)} %copy-done.3), custom_call_target="tpu_custom_call" | custom-call | tf_op jit(solution)/shard_map/act_terms/pallas_call | solution.py:279
  70.1 1.7 %pair_sum.1 = bf16[32,80,128]{2,1,0:T(8,128)(2,1)S(1)} custom-call(bf16[32,80,128]{2,1,0:T(8,128)(2,1)} %get-tuple-element.17.keep_hbm, bf16[32,80,128]{2,1,0:T(8,128)(2,1)S(1)} %collective-permute-done.8.got_hbm), custom_call_target="tpu_custom_call" | custom-call | tf_op jit(solution)/shard_map/pair_sum/pallas_call | solution.py:314
  71.8 30.4 %all_to_all.10.pieces_ref = bf16[32,80,128]{2,1,0:T(8,128)(2,1)S(1)} all-to-all(bf16[32,80,128]{2,1,0:T(8,128)(2,1)S(1)} %pair_sum.1), channel_id=1, replica_groups=mesh['x'=4,'z'=8,'core'=2,'tensor'=8] {'x','z'}, dimensions={0} | all-to-all | bytes 1310720 | tf_op jit(solution)/shard_map/all_to_all | solution.py:382
  102.2 0.1 mean_copies.1
  102.3 23.8 %all_to_all.11.own_ref = bf16[32,80,128]{2,1,0:T(8,128)(2,1)S(1)} all-to-all(bf16[32,80,128]{2,1,0:T(8,128)(2,1)S(1)} %mean_copies.1), channel_id=1, replica_groups=mesh['x'=4,'z'=8,'core'=2,'tensor'=8] {'x','z'}, dimensions={0} | all-to-all | bytes 1310720 | tf_op jit(solution)/shard_map/all_to_all | solution.py:384
  126.1 6.9 %collective-permute-start.9 = (bf16[32,80,128]{2,1,0:T(8,128)(2,1)S(1)}, bf16[32,80,128]{2,1,0:T(8,128)(2,1)S(1)}, u32[]{:S(2)}, u32[]{:S(2)}) collective-permute-start(bf16[32,80,128]{2,1,0:T(8,128)(2,1)S(1)} %all_to_all.11.own_ref), channel_id=1, source_target_pairs={{0,8},{8,0},{1,9},{9,1},{2,10},{10,2},{3,11},{11,3},{4,12},{12,4},... | collective-permute-start | bytes 1966088 | tf_op jit(solution)/shard_map/ppermute | solution.py:385
  133.0 0.1 copy.9
  133.1 0.1 reshape.16.q_ref
  133.2 1.5 %collective-permute-done.9.other_ref = bf16[32,80,128]{2,1,0:T(8,128)(2,1)S(1)} collective-permute-done((bf16[32,80,128]{2,1,0:T(8,128)(2,1)S(1)}, bf16[32,80,128]{2,1,0:T(8,128)(2,1)S(1)}, u32[]{:S(2)}, u32[]{:S(2)}) %collective-permute-start.9) | collective-permute-done | bytes 655392 | tf_op jit(solution)/shard_map/ppermute | solution.py:385
  134.7 10.7 %finish.1 = (bf16[2,80,4096]{2,1,0:T(8,128)(2,1)}, f32[2,64,80]{2,1,0:T(8,128)}) custom-call(s32[2]{0:T(128)S(1)} %pad_add_fusion.where_ref, bf16[32,80,128]{2,1,0:T(8,128)(2,1)S(1)} %all_to_all.11.own_ref, bf16[32,80,128]{2,1,0:T(8,128)(2,1)S(1)} %collective-permute-done.9.other_ref, f32[64,160]{1,0:T(8,128)S(1)} %reshape.16.q_ref, ...), custom_call_target="tpu_custom_call" | custom-call | tf_op jit(solution)/shard_map/finish/pallas_call | solution.py:113
  145.4 0.0 reduce-scatter.2.cloned.1.call-done
  (33 shorter events, 0.1 us)
Async XLA Ops:
  7.2 138.3 %reduce-scatter.2.cloned.1.call-start = ((), (), s32[]{:S(2)}) async-start(), calls=%async_computation.3 | async-start | bytes 3538944 | tf_op jit(solution)/shard_map/reduce_scatter | solution.py:381
  7.2 11.3 %collective-permute-start = (bf16[384,512]{1,0:T(8,128)(2,1)}, bf16[384,512]{1,0:T(8,128)(2,1)S(1)}, u32[]{:S(2)}, u32[]{:S(2)}) collective-permute-start(bf16[384,512]{1,0:T(8,128)(2,1)} %refs_0_.3), channel_id=1, source_target_pairs={{0,1},{1,2},{2,3},{3,4},{4,5},{5,6},{6,7},{7,0},{8,9},{9,10},{10,1... | collective-permute-start | bytes 1179656 | tf_op jit(solution)/shard_map/ppermute | solution.py:352
  11.3 11.3 %collective-permute-start.3 = (bf16[384,512]{1,0:T(8,128)(2,1)}, bf16[384,512]{1,0:T(8,128)(2,1)S(1)}, u32[]{:S(2)}, u32[]{:S(2)}) collective-permute-start(bf16[384,512]{1,0:T(8,128)(2,1)} %refs_0_.3), channel_id=1, source_target_pairs={{0,7},{1,0},{2,1},{3,2},{4,3},{5,4},{6,5},{7,6},{8,15},{9,8},{10,9... | collective-permute-start | bytes 1179656 | tf_op jit(solution)/shard_map/ppermute | solution.py:352
  18.5 34.3 %copy-start.7 = (bf16[384,512]{1,0:T(8,128)(2,1)}, bf16[384,512]{1,0:T(8,128)(2,1)S(1)}, u32[]{:S(2)}) copy-start(bf16[384,512]{1,0:T(8,128)(2,1)S(1)} %collective-permute-done.refs_1_) | copy-start | bytes 1179652
  18.5 11.9 %collective-permute-start.1 = (bf16[384,512]{1,0:T(8,128)(2,1)S(1)}, bf16[384,512]{1,0:T(8,128)(2,1)S(1)}, u32[]{:S(2)}, u32[]{:S(2)}) collective-permute-start(bf16[384,512]{1,0:T(8,128)(2,1)S(1)} %collective-permute-done.refs_1_), channel_id=1, source_target_pairs={{0,1},{1,2},{2,3},{3,4},{4,5},{5,6},{6,7},{7,0},{8,9},{9,10},{10,1... | collective-permute-start | bytes 1179656 | tf_op jit(solution)/shard_map/ppermute | solution.py:352
  22.5 30.3 %copy-start.8 = (bf16[384,512]{1,0:T(8,128)(2,1)}, bf16[384,512]{1,0:T(8,128)(2,1)S(1)}, u32[]{:S(2)}) copy-start(bf16[384,512]{1,0:T(8,128)(2,1)S(1)} %collective-permute-done.3.refs_2_) | copy-start | bytes 1179652
  22.6 10.8 %collective-permute-start.4 = (bf16[384,512]{1,0:T(8,128)(2,1)S(1)}, bf16[384,512]{1,0:T(8,128)(2,1)S(1)}, u32[]{:S(2)}, u32[]{:S(2)}) collective-permute-start(bf16[384,512]{1,0:T(8,128)(2,1)S(1)} %collective-permute-done.3.refs_2_), channel_id=1, source_target_pairs={{0,7},{1,0},{2,1},{3,2},{4,3},{5,4},{6,5},{7,6},{8,15},{9,8},{10,9... | collective-permute-start | bytes 1179656 | tf_op jit(solution)/shard_map/ppermute | solution.py:352
  30.4 22.5 %copy-start.9 = (bf16[384,512]{1,0:T(8,128)(2,1)}, bf16[384,512]{1,0:T(8,128)(2,1)S(1)}, u32[]{:S(2)}) copy-start(bf16[384,512]{1,0:T(8,128)(2,1)S(1)} %collective-permute-done.1.refs_3_) | copy-start | bytes 1179652
  30.4 12.3 %collective-permute-start.2 = (bf16[384,512]{1,0:T(8,128)(2,1)S(1)}, bf16[384,512]{1,0:T(8,128)(2,1)S(1)}, u32[]{:S(2)}, u32[]{:S(2)}) collective-permute-start(bf16[384,512]{1,0:T(8,128)(2,1)S(1)} %collective-permute-done.1.refs_3_), channel_id=1, source_target_pairs={{0,1},{1,2},{2,3},{3,4},{4,5},{5,6},{6,7},{7,0},{8,9},{9,10},{10,1... | collective-permute-start | bytes 1179656 | tf_op jit(solution)/shard_map/ppermute | solution.py:352
  33.4 19.5 %copy-start.10 = (bf16[384,512]{1,0:T(8,128)(2,1)}, bf16[384,512]{1,0:T(8,128)(2,1)S(1)}, u32[]{:S(2)}) copy-start(bf16[384,512]{1,0:T(8,128)(2,1)S(1)} %collective-permute-done.4.refs_4_) | copy-start | bytes 1179652
  33.4 11.7 %collective-permute-start.5 = (bf16[384,512]{1,0:T(8,128)(2,1)S(1)}, bf16[384,512]{1,0:T(8,128)(2,1)S(1)}, u32[]{:S(2)}, u32[]{:S(2)}) collective-permute-start(bf16[384,512]{1,0:T(8,128)(2,1)S(1)} %collective-permute-done.4.refs_4_), channel_id=1, source_target_pairs={{0,7},{1,0},{2,1},{3,2},{4,3},{5,4},{6,5},{7,6},{8,15},{9,8},{10,9... | collective-permute-start | bytes 1179656 | tf_op jit(solution)/shard_map/ppermute | solution.py:352
  38.2 1.1 copy-start
  39.3 1.1 copy-start.2
  40.4 1.0 copy-start.6
  41.4 15.2 %copy-start.11 = (bf16[1,2,80,4096]{3,2,1,0:T(8,128)(2,1)S(1)}, bf16[1,2,80,4096]{3,2,1,0:T(8,128)(2,1)}, u32[]{:S(2)}) copy-start(bf16[1,2,80,4096]{3,2,1,0:T(8,128)(2,1)} %param.10) | copy-start | bytes 3932164
  41.4 15.2 %copy-start.12 = (bf16[384,80]{0,1:T(8,128)(2,1)S(1)}, bf16[384,80]{0,1:T(8,128)(2,1)}, u32[]{:S(2)}) copy-start(bf16[384,80]{0,1:T(8,128)(2,1)} %param.9) | copy-start | bytes 184324
  42.7 13.9 %copy-start.4 = (bf16[384,512]{1,0:T(8,128)(2,1)}, bf16[384,512]{1,0:T(8,128)(2,1)S(1)}, u32[]{:S(2)}) copy-start(bf16[384,512]{1,0:T(8,128)(2,1)S(1)} %collective-permute-done.2.refs_0_.refs_5_) | copy-start | bytes 1179652
  45.1 11.4 %copy-start.5 = (bf16[384,512]{1,0:T(8,128)(2,1)}, bf16[384,512]{1,0:T(8,128)(2,1)S(1)}, u32[]{:S(2)}) copy-start(bf16[384,512]{1,0:T(8,128)(2,1)S(1)} %collective-permute-done.5.refs_1_.refs_6_) | copy-start | bytes 1179652
  45.1 11.4 %collective-permute-start.6 = (bf16[384,384]{1,0:T(8,128)(2,1)S(1)}, bf16[384,384]{1,0:T(8,128)(2,1)S(1)}, u32[]{:S(2)}, u32[]{:S(2)}) collective-permute-start(bf16[384,384]{1,0:T(8,128)(2,1)S(1)} %slice.8), channel_id=1, source_target_pairs={{0,1},{1,2},{2,3},{3,4},{4,5},{5,6},{6,7},{7,0},{8,9},{9,10},{10,1... | collective-permute-start | bytes 884744 | tf_op jit(solution)/shard_map/ppermute | solution.py:352
  50.0 6.6 %collective-permute-start.7 = (bf16[384,128]{1,0:T(8,128)(2,1)S(1)}, bf16[384,128]{1,0:T(8,128)(2,1)S(1)}, u32[]{:S(2)}, u32[]{:S(2)}) collective-permute-start(bf16[384,128]{1,0:T(8,128)(2,1)S(1)} %slice.9), channel_id=1, source_target_pairs={{0,7},{1,0},{2,1},{3,2},{4,3},{5,4},{6,5},{7,6},{8,15},{9,8},{10,9... | collective-permute-start | bytes 294920 | tf_op jit(solution)/shard_map/ppermute | solution.py:352
  56.6 10.8 %copy-start.1 = (bf16[80,4096]{1,0:T(8,128)(2,1)S(1)}, bf16[80,4096]{1,0:T(8,128)(2,1)}, u32[]{:S(2)}) copy-start(bf16[80,4096]{1,0:T(8,128)(2,1)} %gate_ref.7) | copy-start | bytes 1966084
  56.6 10.8 %copy-start.3 = (bf16[80,4096]{1,0:T(8,128)(2,1)S(1)}, bf16[80,4096]{1,0:T(8,128)(2,1)}, u32[]{:S(2)}) copy-start(bf16[80,4096]{1,0:T(8,128)(2,1)} %up_ref.7) | copy-start | bytes 1966084
  61.2 8.8 %collective-permute-start.8 = (bf16[32,80,128]{2,1,0:T(8,128)(2,1)}, bf16[32,80,128]{2,1,0:T(8,128)(2,1)S(1)}, u32[]{:S(2)}, u32[]{:S(2)}) collective-permute-start(bf16[32,80,128]{2,1,0:T(8,128)(2,1)} %get-tuple-element.18), channel_id=1, source_target_pairs={{0,8},{8,0},{1,9},{9,1},{2,10},{10,2},{3,11},{11,3},{4,12},{12,4},... | collective-permute-start | bytes 1966088 | tf_op jit(solution)/shard_map/ppermute | solution.py:378
  71.8 61.2 %copy-start.13 = (f32[2,80,64]{1,2,0:T(8,128)S(1)}, f32[2,80,64]{1,2,0:T(8,128)}, u32[]{:S(2)}) copy-start(f32[2,80,64]{1,2,0:T(8,128)} %param.11) | copy-start | bytes 122884
  126.1 8.6 %collective-permute-start.9 = (bf16[32,80,128]{2,1,0:T(8,128)(2,1)S(1)}, bf16[32,80,128]{2,1,0:T(8,128)(2,1)S(1)}, u32[]{:S(2)}, u32[]{:S(2)}) collective-permute-start(bf16[32,80,128]{2,1,0:T(8,128)(2,1)S(1)} %all_to_all.11.own_ref), channel_id=1, source_target_pairs={{0,8},{8,0},{1,9},{9,1},{2,10},{10,2},{3,11},{11,3},{4,12},{12,4},... | collective-permute-start | bytes 1966088 | tf_op jit(solution)/shard_map/ppermute | solution.py:385
Sparse Core Ops, SparseCore 0:
  71.9 49.5 reduce-scatter.1

commit v6 on v5

--- a/solution.py
+++ b/solution.py
@@ -29,27 +29,25 @@
     work = jnp.concatenate([gram, jnp.where(row_ids == col_ids, 1.0, 0.0)], 1)
     blocks = [work[8 * k : 8 * k + 8] for k in range(n // 8)]
     below = lax.broadcasted_iota(jnp.int32, (8, 2 * n), 0)
-    for j in range(0, n - 2, 2):
+    pivot = jnp.broadcast_to(blocks[0][0:1, 0:1], (1, 2 * n))
+    for j in range(n - 1):
         k, i = divmod(j, 8)
-        upper, lower = blocks[k][i : i + 1], blocks[k][i + 1 : i + 2]
-        a, b, c = upper[:, j : j + 1], upper[:, j + 1 : j + 2], lower[:, j + 1 : j + 2]
-        shrink = 1.0 / (a * c - b * b)
-        first = (c * upper - b * lower) * shrink
-        second = (a * lower - b * upper) * shrink
+        inverse = 1.0 / pivot
+        scaled = blocks[k][i : i + 1] * inverse
+        after, at = divmod(j + 1, 8)
+        following = blocks[after][at : at + 1]
+        beside = jnp.broadcast_to(following[:, j : j + 1], (1, 2 * n))
+        pivot = jnp.broadcast_to(following[:, j + 1 : j + 2], (1, 2 * n)) - beside * beside * inverse
         for m in range(k, n // 8):
-            left = jnp.broadcast_to(blocks[m][:, j : j + 1], (8, 2 * n))
-            right = jnp.broadcast_to(blocks[m][:, j + 1 : j + 2], (8, 2 * n))
-            change = left * first + right * second
+            if m == k and i == 7:
+                continue
+            factor = jnp.broadcast_to(blocks[m][:, j : j + 1], (8, 2 * n))
             if m == k:
-                change = jnp.where(below > i + 1, change, 0.0)
-            blocks[m] = blocks[m] - change
+                factor = jnp.where(below > i, factor, 0.0)
+            blocks[m] = blocks[m] - factor * scaled
     work = jnp.concatenate(blocks, 0)
-    pivots, rows = work[:, :n], work[:, n:]
-    odd = (row_ids[:, 0:1] & 1) == 1
-    diagonal = jnp.sum(jnp.where(row_ids == col_ids, pivots, 0.0), 1, keepdims=True)
-    beside = jnp.sum(jnp.where(row_ids == col_ids + 1, pivots, 0.0), 1, keepdims=True)
-    ratio = jnp.where(odd, beside / pltpu.roll(diagonal, 1, 0), 0.0)
-    return (rows - ratio * pltpu.roll(rows, 1, 0)) * lax.rsqrt(diagonal - ratio * beside)
+    pivots = jnp.sum(jnp.where(row_ids == col_ids, work[:, :n], 0.0), 1, keepdims=True)
+    return work[:, n:] * lax.rsqrt(pivots)
 
 
 def finish_kernel(where_ref, own_ref, other_ref, q_ref, merged_hbm, new_hbm, q_next_ref, stack_ref, merged_ref, new_ref, sem, out_sems):
@@ -265,44 +263,46 @@
     )(where, pre, w_gate, w_up, cot.T, error_fb.reshape(2, rows, width), *operands)
 
 
-def act_kernel(d_ref, gate_ref, up_ref, act_ref):
+def act_kernel(d_ref, gate_ref, up_ref, act_hbm, act_ref, sems):
     d_both = d_ref[...].T
-    step = 1024
-    for f in range(0, act_ref.shape[1], step):
-        at = slice(f, f + step)
+    parts = sems.shape[0]
+    step = act_ref.shape[1] // parts
+    out = []
+    for k in range(parts):
+        at = slice(k * step, (k + 1) * step)
         weights = jnp.concatenate([gate_ref[:, at], up_ref[:, at]], 0)
         act_ref[:, at] = jnp.dot(d_both, weights, preferred_element_type=jnp.float32).astype(jnp.bfloat16)
+        columns = (slice(None), pl.ds(k * step, step))
+        out.append(pltpu.make_async_copy(act_ref.at[columns], act_hbm.at[columns], sems.at[k]))
+        out[-1].start()
+    for copy in out:
+        copy.wait()
 
 
 def act_terms(d_both, w_gate, w_up):
     vmem = pl.BlockSpec(memory_space=pltpu.VMEM)
+    shape = (d_both.shape[1], w_gate.shape[1])
     return pl.pallas_call(
         act_kernel,
-        out_shape=jax.ShapeDtypeStruct((d_both.shape[1], w_gate.shape[1]), jnp.bfloat16),
+        out_shape=jax.ShapeDtypeStruct(shape, jnp.bfloat16),
         in_specs=[vmem] * 3,
-        out_specs=vmem,
+        out_specs=pl.BlockSpec(memory_space=pl.ANY),
+        scratch_shapes=[pltpu.VMEM(shape, jnp.bfloat16), pltpu.SemaphoreType.DMA((8,))],
         compiler_params=pltpu.CompilerParams(vmem_limit_bytes=VMEM_BYTES),
         name="act_terms",
     )(d_both, w_gate, w_up)
 
 
-def pair_kernel(keep_hbm, got_hbm, sum_ref, keep_ref, got_ref, sems):
-    parts = sems.shape[1]
+def pair_kernel(keep_hbm, got_ref, sum_ref, keep_ref, sems):
+    parts = sems.shape[0]
     step = sum_ref.shape[0] // parts
-
-    def load(k):
+    loads = []
+    for k in range(parts):
         at = pl.ds(k * step, step)
-        return (
-            pltpu.make_async_copy(keep_hbm.at[at], keep_ref.at[at], sems.at[0, k]),
-            pltpu.make_async_copy(got_hbm.at[at], got_ref.at[at], sems.at[1, k]),
-        )
-
+        loads.append(pltpu.make_async_copy(keep_hbm.at[at], keep_ref.at[at], sems.at[k]))
+        loads[-1].start()
     for k in range(parts):
-        for copy in load(k):
-            copy.start()
-    for k in range(parts):
-        for copy in load(k):
-            copy.wait()
+        loads[k].wait()
         for i in range(k * step, (k + 1) * step):
             total = keep_ref[i].astype(jnp.float32) + got_ref[i].astype(jnp.float32)
             sum_ref[i] = total.astype(jnp.bfloat16)
@@ -310,17 +310,12 @@
 
 def pair_sum(keep, got):
     vmem = pl.BlockSpec(memory_space=pltpu.VMEM)
-    here = pl.BlockSpec(memory_space=pl.ANY)
     return pl.pallas_call(
         pair_kernel,
         out_shape=jax.ShapeDtypeStruct(keep.shape, jnp.bfloat16),
-        in_specs=[here] * 2,
+        in_specs=[pl.BlockSpec(memory_space=pl.ANY), vmem],
         out_specs=vmem,
-        scratch_shapes=[
-            pltpu.VMEM(keep.shape, jnp.bfloat16),
-            pltpu.VMEM(keep.shape, jnp.bfloat16),
-            pltpu.SemaphoreType.DMA((2, 4)),
-        ],
+        scratch_shapes=[pltpu.VMEM(keep.shape, jnp.bfloat16), pltpu.SemaphoreType.DMA((4,))],
         compiler_params=pltpu.CompilerParams(vmem_limit_bytes=VMEM_BYTES),
         name="pair_sum",
     )(pltpu.with_memory_space_constraint(keep, pltpu.HBM), got)

time: 154 us -> 152 us (0.987)
  Pallas kernels: 22 us -> 20.3 us
where the time goes in v6:
time: 152 us; the launch traced here: 151 us
  blocking collectives  54.2 us (36%)
  starting transfers between devices  44 us (29%)
  Pallas kernels  20.3 us (13%)
  between operations  14.4 us (9%)
  waiting for transfers between devices  14.3 us (9%)
  local copies, waits for them, and re-layouts  3.42 us (2%)
    ppermute x8, starting transfers between devices, ring(): lax.ppermute(value, 'tensor', [(i, (i + step) % ways) for i in range(ways)])  30.9 us
    all_to_all x1, blocking collectives, on_device(): pieces = lax.all_to_all(pieces, CHIPS, 0, 0, tiled=True)  29.5 us
    all_to_all x1, blocking collectives, on_device(): own_half = lax.all_to_all(copies, CHIPS, 0, 0, tiled=True)  24.7 us
    ppermute x8, waiting for transfers between devices, ring(): lax.ppermute(value, 'tensor', [(i, (i + step) % ways) for i in range(ways)])  12.7 us
    pallas_call x1, Pallas kernels, finish(): pl.pallas_call(finish_kernel, out_shape=(jax.ShapeDtypeStruct((2, rows, w...  10.1 us
    ppermute x1, starting transfers between devices, on_device(): other_half = lax.ppermute(own_half, 'core', SWAP)  6.83 us
    ppermute x1, starting transfers between devices, on_device(): got = lax.ppermute(send, 'core', SWAP)  6.17 us
    pallas_call x1, Pallas kernels, gradients(): pl.pallas_call(functools.partial(gradient_kernel, places=[(shift, start)...  4.63 us
  transfers between devices with their start and end apart: 11, of which 5 were waited for; matrix products, arithmetic and copies ran while one was open for 0% of the time, Pallas kernels for 10%

profile of v6, /device:TPU:1, one launch (start us, length us, event | category | flops | bytes accessed | tf_op | source)
XLA Modules:
  0.0 150.6 jit_solution(9375982604621182143)
XLA Ops:
  7.2 0.0 reduce-scatter.2.cloned.1.call-start
  7.2 4.0 %collective-permute-start = (bf16[384,512]{1,0:T(8,128)(2,1)}, bf16[384,512]{1,0:T(8,128)(2,1)S(1)}, u32[]{:S(2)}, u32[]{:S(2)}) collective-permute-start(bf16[384,512]{1,0:T(8,128)(2,1)} %refs_0_.3), channel_id=1, source_target_pairs={{0,1},{1,2},{2,3},{3,4},{4,5},{5,6},{6,7},{7,0},{8,9},{9,10},{10,1... | collective-permute-start | bytes 1179656 | tf_op jit(solution)/shard_map/ppermute | solution.py:347
  11.3 3.8 %collective-permute-start.3 = (bf16[384,512]{1,0:T(8,128)(2,1)}, bf16[384,512]{1,0:T(8,128)(2,1)S(1)}, u32[]{:S(2)}, u32[]{:S(2)}) collective-permute-start(bf16[384,512]{1,0:T(8,128)(2,1)} %refs_0_.3), channel_id=1, source_target_pairs={{0,7},{1,0},{2,1},{3,2},{4,3},{5,4},{6,5},{7,6},{8,15},{9,8},{10,9... | collective-permute-start | bytes 1179656 | tf_op jit(solution)/shard_map/ppermute | solution.py:347
  15.1 3.4 %collective-permute-done.refs_1_ = bf16[384,512]{1,0:T(8,128)(2,1)S(1)} collective-permute-done((bf16[384,512]{1,0:T(8,128)(2,1)}, bf16[384,512]{1,0:T(8,128)(2,1)S(1)}, u32[]{:S(2)}, u32[]{:S(2)}) %collective-permute-start) | collective-permute-done | bytes 393248 | tf_op jit(solution)/shard_map/ppermute | solution.py:347
  18.5 4.0 %collective-permute-start.1 = (bf16[384,512]{1,0:T(8,128)(2,1)S(1)}, bf16[384,512]{1,0:T(8,128)(2,1)S(1)}, u32[]{:S(2)}, u32[]{:S(2)}) collective-permute-start(bf16[384,512]{1,0:T(8,128)(2,1)S(1)} %collective-permute-done.refs_1_), channel_id=1, source_target_pairs={{0,1},{1,2},{2,3},{3,4},{4,5},{5,6},{6,7},{7,0},{8,9},{9,10},{10,1... | collective-permute-start | bytes 1179656 | tf_op jit(solution)/shard_map/ppermute | solution.py:347
  22.6 4.6 %collective-permute-start.4 = (bf16[384,512]{1,0:T(8,128)(2,1)S(1)}, bf16[384,512]{1,0:T(8,128)(2,1)S(1)}, u32[]{:S(2)}, u32[]{:S(2)}) collective-permute-start(bf16[384,512]{1,0:T(8,128)(2,1)S(1)} %collective-permute-done.3.refs_2_), channel_id=1, source_target_pairs={{0,7},{1,0},{2,1},{3,2},{4,3},{5,4},{6,5},{7,6},{8,15},{9,8},{10,9... | collective-permute-start | bytes 1179656 | tf_op jit(solution)/shard_map/ppermute | solution.py:347
  27.2 3.2 %collective-permute-done.1.refs_3_ = bf16[384,512]{1,0:T(8,128)(2,1)S(1)} collective-permute-done((bf16[384,512]{1,0:T(8,128)(2,1)S(1)}, bf16[384,512]{1,0:T(8,128)(2,1)S(1)}, u32[]{:S(2)}, u32[]{:S(2)}) %collective-permute-start.1) | collective-permute-done | bytes 393248 | tf_op jit(solution)/shard_map/ppermute | solution.py:347
  30.4 3.0 %collective-permute-start.2 = (bf16[384,512]{1,0:T(8,128)(2,1)S(1)}, bf16[384,512]{1,0:T(8,128)(2,1)S(1)}, u32[]{:S(2)}, u32[]{:S(2)}) collective-permute-start(bf16[384,512]{1,0:T(8,128)(2,1)S(1)} %collective-permute-done.1.refs_3_), channel_id=1, source_target_pairs={{0,1},{1,2},{2,3},{3,4},{4,5},{5,6},{6,7},{7,0},{8,9},{9,10},{10,1... | collective-permute-start | bytes 1179656 | tf_op jit(solution)/shard_map/ppermute | solution.py:347
  33.4 4.7 %collective-permute-start.5 = (bf16[384,512]{1,0:T(8,128)(2,1)S(1)}, bf16[384,512]{1,0:T(8,128)(2,1)S(1)}, u32[]{:S(2)}, u32[]{:S(2)}) collective-permute-start(bf16[384,512]{1,0:T(8,128)(2,1)S(1)} %collective-permute-done.4.refs_4_), channel_id=1, source_target_pairs={{0,7},{1,0},{2,1},{3,2},{4,3},{5,4},{6,5},{7,6},{8,15},{9,8},{10,9... | collective-permute-start | bytes 1179656 | tf_op jit(solution)/shard_map/ppermute | solution.py:347
  38.1 0.1 pad_add_fusion.where_ref
  38.2 1.1 copy-done
  39.3 1.1 copy-done.2
  40.4 1.0 copy-done.6
  41.4 1.3 early_products.2.refs_2_
  42.7 2.4 %collective-permute-done.5.refs_1_.refs_6_ = bf16[384,512]{1,0:T(8,128)(2,1)S(1)} collective-permute-done((bf16[384,512]{1,0:T(8,128)(2,1)S(1)}, bf16[384,512]{1,0:T(8,128)(2,1)S(1)}, u32[]{:S(2)}, u32[]{:S(2)}) %collective-permute-start.5) | collective-permute-done | bytes 393248 | tf_op jit(solution)/shard_map/ppermute | solution.py:347
  45.1 4.8 %collective-permute-start.6 = (bf16[384,384]{1,0:T(8,128)(2,1)S(1)}, bf16[384,384]{1,0:T(8,128)(2,1)S(1)}, u32[]{:S(2)}, u32[]{:S(2)}) collective-permute-start(bf16[384,384]{1,0:T(8,128)(2,1)S(1)} %slice.8), channel_id=1, source_target_pairs={{0,1},{1,2},{2,3},{3,4},{4,5},{5,6},{6,7},{7,0},{8,9},{9,10},{10,1... | collective-permute-start | bytes 884744 | tf_op jit(solution)/shard_map/ppermute | solution.py:347
  50.0 1.9 %collective-permute-start.7 = (bf16[384,128]{1,0:T(8,128)(2,1)S(1)}, bf16[384,128]{1,0:T(8,128)(2,1)S(1)}, u32[]{:S(2)}, u32[]{:S(2)}) collective-permute-start(bf16[384,128]{1,0:T(8,128)(2,1)S(1)} %slice.9), channel_id=1, source_target_pairs={{0,7},{1,0},{2,1},{3,2},{4,3},{5,4},{6,5},{7,6},{8,15},{9,8},{10,9... | collective-permute-start | bytes 294920 | tf_op jit(solution)/shard_map/ppermute | solution.py:347
  51.9 0.9 early_products.3.pre_ref
  52.9 3.7 %collective-permute-done.7.refs_8_ = bf16[384,128]{1,0:T(8,128)(2,1)S(1)} collective-permute-done((bf16[384,128]{1,0:T(8,128)(2,1)S(1)}, bf16[384,128]{1,0:T(8,128)(2,1)S(1)}, u32[]{:S(2)}, u32[]{:S(2)}) %collective-permute-start.7) | collective-permute-done | bytes 98336 | tf_op jit(solution)/shard_map/ppermute | solution.py:347
  56.6 4.6 %gradients.1 = (bf16[160,384]{1,0:T(8,128)(2,1)S(1)}, bf16[32,80,128]{2,1,0:T(8,128)(2,1)}, bf16[32,80,128]{2,1,0:T(8,128)(2,1)}, f32[160,4096]{1,0:T(8,128)}) custom-call(s32[2]{0:T(128)S(1)} %pad_add_fusion.where_ref, f32[160,384]{1,0:T(8,128)S(1)} %early_products.3.pre_ref, bf16[80,4096]{1,0:T(8,128)(2,1)S(1)} %copy-done, bf16[80,4096]{1,0:T(8,128)(2,1)S(1)} %copy-done.2, ...), custom_call_target="tpu_custom_call" | custom-call | tf_op jit(solution)/shard_map/gradients/pallas_call | solution.py:237
  61.2 6.2 %collective-permute-start.8 = (bf16[32,80,128]{2,1,0:T(8,128)(2,1)}, bf16[32,80,128]{2,1,0:T(8,128)(2,1)S(1)}, u32[]{:S(2)}, u32[]{:S(2)}) collective-permute-start(bf16[32,80,128]{2,1,0:T(8,128)(2,1)} %get-tuple-element.18), channel_id=1, source_target_pairs={{0,8},{8,0},{1,9},{9,1},{2,10},{10,2},{3,11},{11,3},{4,12},{12,4},... | collective-permute-start | bytes 1966088 | tf_op jit(solution)/shard_map/ppermute | solution.py:373
  67.4 2.0 %act_terms.1 = bf16[384,4096]{1,0:T(8,128)(2,1)} custom-call(bf16[160,384]{1,0:T(8,128)(2,1)S(1)} %get-tuple-element.19.d_ref, bf16[80,4096]{1,0:T(8,128)(2,1)S(1)} %copy-done.1, bf16[80,4096]{1,0:T(8,128)(2,1)S(1)} %copy-done.3), custom_call_target="tpu_custom_call" | custom-call | tf_op jit(solution)/shard_map/act_terms/pallas_call | solution.py:285
  69.5 1.2 pair_sum.1
  70.7 29.5 %all_to_all.10.pieces_ref = bf16[32,80,128]{2,1,0:T(8,128)(2,1)S(1)} all-to-all(bf16[32,80,128]{2,1,0:T(8,128)(2,1)S(1)} %pair_sum.1), channel_id=1, replica_groups=mesh['x'=4,'z'=8,'core'=2,'tensor'=8] {'x','z'}, dimensions={0} | all-to-all | bytes 1310720 | tf_op jit(solution)/shard_map/all_to_all | solution.py:377
  100.3 0.1 mean_copies.1
  100.4 24.7 %all_to_all.11.own_ref = bf16[32,80,128]{2,1,0:T(8,128)(2,1)S(1)} all-to-all(bf16[32,80,128]{2,1,0:T(8,128)(2,1)S(1)} %mean_copies.1), channel_id=1, replica_groups=mesh['x'=4,'z'=8,'core'=2,'tensor'=8] {'x','z'}, dimensions={0} | all-to-all | bytes 1310720 | tf_op jit(solution)/shard_map/all_to_all | solution.py:379
  125.1 6.8 %collective-permute-start.9 = (bf16[32,80,128]{2,1,0:T(8,128)(2,1)S(1)}, bf16[32,80,128]{2,1,0:T(8,128)(2,1)S(1)}, u32[]{:S(2)}, u32[]{:S(2)}) collective-permute-start(bf16[32,80,128]{2,1,0:T(8,128)(2,1)S(1)} %all_to_all.11.own_ref), channel_id=1, source_target_pairs={{0,8},{8,0},{1,9},{9,1},{2,10},{10,2},{3,11},{11,3},{4,12},{12,4},... | collective-permute-start | bytes 1966088 | tf_op jit(solution)/shard_map/ppermute | solution.py:380
  131.9 0.1 copy.9
  132.0 0.1 reshape.16.q_ref
  132.1 1.5 %collective-permute-done.9.other_ref = bf16[32,80,128]{2,1,0:T(8,128)(2,1)S(1)} collective-permute-done((bf16[32,80,128]{2,1,0:T(8,128)(2,1)S(1)}, bf16[32,80,128]{2,1,0:T(8,128)(2,1)S(1)}, u32[]{:S(2)}, u32[]{:S(2)}) %collective-permute-start.9) | collective-permute-done | bytes 655392 | tf_op jit(solution)/shard_map/ppermute | solution.py:380
  133.6 10.1 %finish.1 = (bf16[2,80,4096]{2,1,0:T(8,128)(2,1)}, f32[2,64,80]{2,1,0:T(8,128)}) custom-call(s32[2]{0:T(128)S(1)} %pad_add_fusion.where_ref, bf16[32,80,128]{2,1,0:T(8,128)(2,1)S(1)} %all_to_all.11.own_ref, bf16[32,80,128]{2,1,0:T(8,128)(2,1)S(1)} %collective-permute-done.9.other_ref, f32[64,160]{1,0:T(8,128)S(1)} %reshape.16.q_ref, ...), custom_call_target="tpu_custom_call" | custom-call | tf_op jit(solution)/shard_map/finish/pallas_call | solution.py:111
  143.7 0.0 reduce-scatter.2.cloned.1.call-done
  (33 shorter events, 0.1 us)
Async XLA Ops:
  7.2 136.6 %reduce-scatter.2.cloned.1.call-start = ((), (), s32[]{:S(2)}) async-start(), calls=%async_computation.3 | async-start | bytes 3538944 | tf_op jit(solution)/shard_map/reduce_scatter | solution.py:376
  7.2 11.3 %collective-permute-start = (bf16[384,512]{1,0:T(8,128)(2,1)}, bf16[384,512]{1,0:T(8,128)(2,1)S(1)}, u32[]{:S(2)}, u32[]{:S(2)}) collective-permute-start(bf16[384,512]{1,0:T(8,128)(2,1)} %refs_0_.3), channel_id=1, source_target_pairs={{0,1},{1,2},{2,3},{3,4},{4,5},{5,6},{6,7},{7,0},{8,9},{9,10},{10,1... | collective-permute-start | bytes 1179656 | tf_op jit(solution)/shard_map/ppermute | solution.py:347
  11.3 11.3 %collective-permute-start.3 = (bf16[384,512]{1,0:T(8,128)(2,1)}, bf16[384,512]{1,0:T(8,128)(2,1)S(1)}, u32[]{:S(2)}, u32[]{:S(2)}) collective-permute-start(bf16[384,512]{1,0:T(8,128)(2,1)} %refs_0_.3), channel_id=1, source_target_pairs={{0,7},{1,0},{2,1},{3,2},{4,3},{5,4},{6,5},{7,6},{8,15},{9,8},{10,9... | collective-permute-start | bytes 1179656 | tf_op jit(solution)/shard_map/ppermute | solution.py:347
  18.5 34.3 %copy-start.7 = (bf16[384,512]{1,0:T(8,128)(2,1)}, bf16[384,512]{1,0:T(8,128)(2,1)S(1)}, u32[]{:S(2)}) copy-start(bf16[384,512]{1,0:T(8,128)(2,1)S(1)} %collective-permute-done.refs_1_) | copy-start | bytes 1179652
  18.5 11.9 %collective-permute-start.1 = (bf16[384,512]{1,0:T(8,128)(2,1)S(1)}, bf16[384,512]{1,0:T(8,128)(2,1)S(1)}, u32[]{:S(2)}, u32[]{:S(2)}) collective-permute-start(bf16[384,512]{1,0:T(8,128)(2,1)S(1)} %collective-permute-done.refs_1_), channel_id=1, source_target_pairs={{0,1},{1,2},{2,3},{3,4},{4,5},{5,6},{6,7},{7,0},{8,9},{9,10},{10,1... | collective-permute-start | bytes 1179656 | tf_op jit(solution)/shard_map/ppermute | solution.py:347
  22.5 30.3 %copy-start.8 = (bf16[384,512]{1,0:T(8,128)(2,1)}, bf16[384,512]{1,0:T(8,128)(2,1)S(1)}, u32[]{:S(2)}) copy-start(bf16[384,512]{1,0:T(8,128)(2,1)S(1)} %collective-permute-done.3.refs_2_) | copy-start | bytes 1179652
  22.6 10.8 %collective-permute-start.4 = (bf16[384,512]{1,0:T(8,128)(2,1)S(1)}, bf16[384,512]{1,0:T(8,128)(2,1)S(1)}, u32[]{:S(2)}, u32[]{:S(2)}) collective-permute-start(bf16[384,512]{1,0:T(8,128)(2,1)S(1)} %collective-permute-done.3.refs_2_), channel_id=1, source_target_pairs={{0,7},{1,0},{2,1},{3,2},{4,3},{5,4},{6,5},{7,6},{8,15},{9,8},{10,9... | collective-permute-start | bytes 1179656 | tf_op jit(solution)/shard_map/ppermute | solution.py:347
  30.4 22.5 %copy-start.9 = (bf16[384,512]{1,0:T(8,128)(2,1)}, bf16[384,512]{1,0:T(8,128)(2,1)S(1)}, u32[]{:S(2)}) copy-start(bf16[384,512]{1,0:T(8,128)(2,1)S(1)} %collective-permute-done.1.refs_3_) | copy-start | bytes 1179652
  30.4 12.3 %collective-permute-start.2 = (bf16[384,512]{1,0:T(8,128)(2,1)S(1)}, bf16[384,512]{1,0:T(8,128)(2,1)S(1)}, u32[]{:S(2)}, u32[]{:S(2)}) collective-permute-start(bf16[384,512]{1,0:T(8,128)(2,1)S(1)} %collective-permute-done.1.refs_3_), channel_id=1, source_target_pairs={{0,1},{1,2},{2,3},{3,4},{4,5},{5,6},{6,7},{7,0},{8,9},{9,10},{10,1... | collective-permute-start | bytes 1179656 | tf_op jit(solution)/shard_map/ppermute | solution.py:347
  33.4 19.5 %copy-start.10 = (bf16[384,512]{1,0:T(8,128)(2,1)}, bf16[384,512]{1,0:T(8,128)(2,1)S(1)}, u32[]{:S(2)}) copy-start(bf16[384,512]{1,0:T(8,128)(2,1)S(1)} %collective-permute-done.4.refs_4_) | copy-start | bytes 1179652
  33.4 11.7 %collective-permute-start.5 = (bf16[384,512]{1,0:T(8,128)(2,1)S(1)}, bf16[384,512]{1,0:T(8,128)(2,1)S(1)}, u32[]{:S(2)}, u32[]{:S(2)}) collective-permute-start(bf16[384,512]{1,0:T(8,128)(2,1)S(1)} %collective-permute-done.4.refs_4_), channel_id=1, source_target_pairs={{0,7},{1,0},{2,1},{3,2},{4,3},{5,4},{6,5},{7,6},{8,15},{9,8},{10,9... | collective-permute-start | bytes 1179656 | tf_op jit(solution)/shard_map/ppermute | solution.py:347
  38.2 1.1 copy-start
  39.3 1.1 copy-start.2
  40.4 1.0 copy-start.6
  41.4 15.2 %copy-start.11 = (bf16[1,2,80,4096]{3,2,1,0:T(8,128)(2,1)S(1)}, bf16[1,2,80,4096]{3,2,1,0:T(8,128)(2,1)}, u32[]{:S(2)}) copy-start(bf16[1,2,80,4096]{3,2,1,0:T(8,128)(2,1)} %param.10) | copy-start | bytes 3932164
  41.4 15.2 %copy-start.12 = (bf16[384,80]{0,1:T(8,128)(2,1)S(1)}, bf16[384,80]{0,1:T(8,128)(2,1)}, u32[]{:S(2)}) copy-start(bf16[384,80]{0,1:T(8,128)(2,1)} %param.9) | copy-start | bytes 184324
  42.7 13.9 %copy-start.4 = (bf16[384,512]{1,0:T(8,128)(2,1)}, bf16[384,512]{1,0:T(8,128)(2,1)S(1)}, u32[]{:S(2)}) copy-start(bf16[384,512]{1,0:T(8,128)(2,1)S(1)} %collective-permute-done.2.refs_0_.refs_5_) | copy-start | bytes 1179652
  45.1 11.4 %copy-start.5 = (bf16[384,512]{1,0:T(8,128)(2,1)}, bf16[384,512]{1,0:T(8,128)(2,1)S(1)}, u32[]{:S(2)}) copy-start(bf16[384,512]{1,0:T(8,128)(2,1)S(1)} %collective-permute-done.5.refs_1_.refs_6_) | copy-start | bytes 1179652
  45.1 11.4 %collective-permute-start.6 = (bf16[384,384]{1,0:T(8,128)(2,1)S(1)}, bf16[384,384]{1,0:T(8,128)(2,1)S(1)}, u32[]{:S(2)}, u32[]{:S(2)}) collective-permute-start(bf16[384,384]{1,0:T(8,128)(2,1)S(1)} %slice.8), channel_id=1, source_target_pairs={{0,1},{1,2},{2,3},{3,4},{4,5},{5,6},{6,7},{7,0},{8,9},{9,10},{10,1... | collective-permute-start | bytes 884744 | tf_op jit(solution)/shard_map/ppermute | solution.py:347
  50.0 6.6 %collective-permute-start.7 = (bf16[384,128]{1,0:T(8,128)(2,1)S(1)}, bf16[384,128]{1,0:T(8,128)(2,1)S(1)}, u32[]{:S(2)}, u32[]{:S(2)}) collective-permute-start(bf16[384,128]{1,0:T(8,128)(2,1)S(1)} %slice.9), channel_id=1, source_target_pairs={{0,7},{1,0},{2,1},{3,2},{4,3},{5,4},{6,5},{7,6},{8,15},{9,8},{10,9... | collective-permute-start | bytes 294920 | tf_op jit(solution)/shard_map/ppermute | solution.py:347
  56.6 10.8 %copy-start.1 = (bf16[80,4096]{1,0:T(8,128)(2,1)S(1)}, bf16[80,4096]{1,0:T(8,128)(2,1)}, u32[]{:S(2)}) copy-start(bf16[80,4096]{1,0:T(8,128)(2,1)} %gate_ref.7) | copy-start | bytes 1966084
  56.6 10.8 %copy-start.3 = (bf16[80,4096]{1,0:T(8,128)(2,1)S(1)}, bf16[80,4096]{1,0:T(8,128)(2,1)}, u32[]{:S(2)}) copy-start(bf16[80,4096]{1,0:T(8,128)(2,1)} %up_ref.7) | copy-start | bytes 1966084
  61.2 8.2 %collective-permute-start.8 = (bf16[32,80,128]{2,1,0:T(8,128)(2,1)}, bf16[32,80,128]{2,1,0:T(8,128)(2,1)S(1)}, u32[]{:S(2)}, u32[]{:S(2)}) collective-permute-start(bf16[32,80,128]{2,1,0:T(8,128)(2,1)} %get-tuple-element.18), channel_id=1, source_target_pairs={{0,8},{8,0},{1,9},{9,1},{2,10},{10,2},{3,11},{11,3},{4,12},{12,4},... | collective-permute-start | bytes 1966088 | tf_op jit(solution)/shard_map/ppermute | solution.py:373
  70.7 61.2 %copy-start.13 = (f32[2,80,64]{1,2,0:T(8,128)S(1)}, f32[2,80,64]{1,2,0:T(8,128)}, u32[]{:S(2)}) copy-start(f32[2,80,64]{1,2,0:T(8,128)} %param.11) | copy-start | bytes 122884
  125.1 8.5 %collective-permute-start.9 = (bf16[32,80,128]{2,1,0:T(8,128)(2,1)S(1)}, bf16[32,80,128]{2,1,0:T(8,128)(2,1)S(1)}, u32[]{:S(2)}, u32[]{:S(2)}) collective-permute-start(bf16[32,80,128]{2,1,0:T(8,128)(2,1)S(1)} %all_to_all.11.own_ref), channel_id=1, source_target_pairs={{0,8},{8,0},{1,9},{9,1},{2,10},{10,2},{3,11},{11,3},{4,12},{12,4},... | collective-permute-start | bytes 1966088 | tf_op jit(solution)/shard_map/ppermute | solution.py:380
Sparse Core Ops, SparseCore 0:
  70.9 49.8 reduce-scatter.1

commit v7 on v6

--- a/solution.py
+++ b/solution.py
@@ -362,7 +362,8 @@
     early = 5
     pre = early_products(where, w_gate, w_up, [shard[:2] for shard in shards[:early]], ways)
     middle = share * 3 // 4
-    ahead, behind, pre = lax.optimization_barrier((ahead[:, :middle], behind[:, middle:], pre))
+    ahead, pre = lax.optimization_barrier((ahead[:, :middle], pre))
+    behind = behind[:, middle:]
     pre = early_products(where, w_gate, w_up, [shard[:2] for shard in shards[early:]], ways, (pre,))
     early = len(shards)
     shards += [(ring(ahead, 1), ways // 2, 0), (ring(behind, -1), ways // 2, middle)]

time: 152 us -> 150 us (0.987)
  waiting for transfers between devices: 14.3 us -> 9.88 us
  blocking collectives: 54.2 us -> 55.8 us
    ppermute x8, waiting for transfers between devices: 12.7 us -> 8.31 us  [ring(): lax.ppermute(value, 'tensor', [(i, (i + step) % ways) for i in range(ways)])]
    all_to_all x1, blocking collectives: 29.5 us -> 31.1 us  [on_device(): pieces = lax.all_to_all(pieces, CHIPS, 0, 0, tiled=True)]
  transfers between devices with their start and end apart: 11 -> 11, of which waited for: 5 -> 4; matrix products, arithmetic and copies ran while one was open for 0% -> 0% of each run, Pallas kernels for 10% -> 10%
where the time goes in v7:
time: 150 us; the launch traced here: 149 us
  blocking collectives  55.8 us (37%)
  starting transfers between devices  45.1 us (30%)
  Pallas kernels  20.3 us (14%)
  between operations  14.4 us (10%)
  waiting for transfers between devices  9.88 us (7%)
  local copies, waits for them, and re-layouts  3.42 us (2%)
    all_to_all x1, blocking collectives, on_device(): pieces = lax.all_to_all(pieces, CHIPS, 0, 0, tiled=True)  31.1 us
    ppermute x8, starting transfers between devices, ring(): lax.ppermute(value, 'tensor', [(i, (i + step) % ways) for i in range(ways)])  30.7 us
    all_to_all x1, blocking collectives, on_device(): own_half = lax.all_to_all(copies, CHIPS, 0, 0, tiled=True)  24.7 us
    pallas_call x1, Pallas kernels, finish(): pl.pallas_call(finish_kernel, out_shape=(jax.ShapeDtypeStruct((2, rows, w...  10.1 us
    ppermute x8, waiting for transfers between devices, ring(): lax.ppermute(value, 'tensor', [(i, (i + step) % ways) for i in range(ways)])  8.31 us
    ppermute x1, starting transfers between devices, on_device(): got = lax.ppermute(send, 'core', SWAP)  7.53 us
    ppermute x1, starting transfers between devices, on_device(): other_half = lax.ppermute(own_half, 'core', SWAP)  6.83 us
    pallas_call x1, Pallas kernels, gradients(): pl.pallas_call(functools.partial(gradient_kernel, places=[(shift, start)...  4.62 us
  transfers between devices with their start and end apart: 11, of which 4 were waited for; matrix products, arithmetic and copies ran while one was open for 0% of the time, Pallas kernels for 10%

profile of v7, /device:TPU:1, one launch (start us, length us, event | category | flops | bytes accessed | tf_op | source)
XLA Modules:
  0.0 148.9 jit_solution(2186468158360935507)
XLA Ops:
  7.2 0.0 reduce-scatter.2.cloned.1.call-start
  7.2 4.0 %collective-permute-start = (bf16[384,512]{1,0:T(8,128)(2,1)}, bf16[384,512]{1,0:T(8,128)(2,1)S(1)}, u32[]{:S(2)}, u32[]{:S(2)}) collective-permute-start(bf16[384,512]{1,0:T(8,128)(2,1)} %refs_0_.3), channel_id=1, source_target_pairs={{0,1},{1,2},{2,3},{3,4},{4,5},{5,6},{6,7},{7,0},{8,9},{9,10},{10,1... | collective-permute-start | bytes 1179656 | tf_op jit(solution)/shard_map/ppermute | solution.py:347
  11.3 3.8 %collective-permute-start.3 = (bf16[384,512]{1,0:T(8,128)(2,1)}, bf16[384,512]{1,0:T(8,128)(2,1)S(1)}, u32[]{:S(2)}, u32[]{:S(2)}) collective-permute-start(bf16[384,512]{1,0:T(8,128)(2,1)} %refs_0_.3), channel_id=1, source_target_pairs={{0,7},{1,0},{2,1},{3,2},{4,3},{5,4},{6,5},{7,6},{8,15},{9,8},{10,9... | collective-permute-start | bytes 1179656 | tf_op jit(solution)/shard_map/ppermute | solution.py:347
  15.1 3.4 %collective-permute-done.refs_1_ = bf16[384,512]{1,0:T(8,128)(2,1)S(1)} collective-permute-done((bf16[384,512]{1,0:T(8,128)(2,1)}, bf16[384,512]{1,0:T(8,128)(2,1)S(1)}, u32[]{:S(2)}, u32[]{:S(2)}) %collective-permute-start) | collective-permute-done | bytes 393248 | tf_op jit(solution)/shard_map/ppermute | solution.py:347
  18.5 4.0 %collective-permute-start.1 = (bf16[384,512]{1,0:T(8,128)(2,1)S(1)}, bf16[384,512]{1,0:T(8,128)(2,1)S(1)}, u32[]{:S(2)}, u32[]{:S(2)}) collective-permute-start(bf16[384,512]{1,0:T(8,128)(2,1)S(1)} %collective-permute-done.refs_1_), channel_id=1, source_target_pairs={{0,1},{1,2},{2,3},{3,4},{4,5},{5,6},{6,7},{7,0},{8,9},{9,10},{10,1... | collective-permute-start | bytes 1179656 | tf_op jit(solution)/shard_map/ppermute | solution.py:347
  22.6 4.6 %collective-permute-start.4 = (bf16[384,512]{1,0:T(8,128)(2,1)S(1)}, bf16[384,512]{1,0:T(8,128)(2,1)S(1)}, u32[]{:S(2)}, u32[]{:S(2)}) collective-permute-start(bf16[384,512]{1,0:T(8,128)(2,1)S(1)} %collective-permute-done.3.refs_2_), channel_id=1, source_target_pairs={{0,7},{1,0},{2,1},{3,2},{4,3},{5,4},{6,5},{7,6},{8,15},{9,8},{10,9... | collective-permute-start | bytes 1179656 | tf_op jit(solution)/shard_map/ppermute | solution.py:347
  27.2 3.2 %collective-permute-done.1.refs_3_ = bf16[384,512]{1,0:T(8,128)(2,1)S(1)} collective-permute-done((bf16[384,512]{1,0:T(8,128)(2,1)S(1)}, bf16[384,512]{1,0:T(8,128)(2,1)S(1)}, u32[]{:S(2)}, u32[]{:S(2)}) %collective-permute-start.1) | collective-permute-done | bytes 393248 | tf_op jit(solution)/shard_map/ppermute | solution.py:347
  30.4 3.0 %collective-permute-start.2 = (bf16[384,512]{1,0:T(8,128)(2,1)S(1)}, bf16[384,512]{1,0:T(8,128)(2,1)S(1)}, u32[]{:S(2)}, u32[]{:S(2)}) collective-permute-start(bf16[384,512]{1,0:T(8,128)(2,1)S(1)} %collective-permute-done.1.refs_3_), channel_id=1, source_target_pairs={{0,1},{1,2},{2,3},{3,4},{4,5},{5,6},{6,7},{7,0},{8,9},{9,10},{10,1... | collective-permute-start | bytes 1179656 | tf_op jit(solution)/shard_map/ppermute | solution.py:347
  33.4 4.7 %collective-permute-start.5 = (bf16[384,512]{1,0:T(8,128)(2,1)S(1)}, bf16[384,512]{1,0:T(8,128)(2,1)S(1)}, u32[]{:S(2)}, u32[]{:S(2)}) collective-permute-start(bf16[384,512]{1,0:T(8,128)(2,1)S(1)} %collective-permute-done.4.refs_4_), channel_id=1, source_target_pairs={{0,7},{1,0},{2,1},{3,2},{4,3},{5,4},{6,5},{7,6},{8,15},{9,8},{10,9... | collective-permute-start | bytes 1179656 | tf_op jit(solution)/shard_map/ppermute | solution.py:347
  38.1 0.1 pad_add_fusion.where_ref
  38.2 1.1 copy-done
  39.3 1.1 copy-done.2
  40.4 1.0 copy-done.6
  41.4 1.3 early_products.2.refs_2_
  42.7 2.5 %collective-permute-start.6 = (bf16[384,384]{1,0:T(8,128)(2,1)S(1)}, bf16[384,384]{1,0:T(8,128)(2,1)S(1)}, u32[]{:S(2)}, u32[]{:S(2)}) collective-permute-start(bf16[384,384]{1,0:T(8,128)(2,1)S(1)} %slice.8), channel_id=1, source_target_pairs={{0,1},{1,2},{2,3},{3,4},{4,5},{5,6},{6,7},{7,0},{8,9},{9,10},{10,1... | collective-permute-start | bytes 884744 | tf_op jit(solution)/shard_map/ppermute | solution.py:347
  45.3 4.0 %collective-permute-start.7 = (bf16[384,128]{1,0:T(8,128)(2,1)S(1)}, bf16[384,128]{1,0:T(8,128)(2,1)S(1)}, u32[]{:S(2)}, u32[]{:S(2)}) collective-permute-start(bf16[384,128]{1,0:T(8,128)(2,1)S(1)} %slice.9), channel_id=1, source_target_pairs={{0,7},{1,0},{2,1},{3,2},{4,3},{5,4},{6,5},{7,6},{8,15},{9,8},{10,9... | collective-permute-start | bytes 294920 | tf_op jit(solution)/shard_map/ppermute | solution.py:347
  49.3 0.9 early_products.3.pre_ref
  50.3 1.7 %collective-permute-done.7.refs_8_ = bf16[384,128]{1,0:T(8,128)(2,1)S(1)} collective-permute-done((bf16[384,128]{1,0:T(8,128)(2,1)S(1)}, bf16[384,128]{1,0:T(8,128)(2,1)S(1)}, u32[]{:S(2)}, u32[]{:S(2)}) %collective-permute-start.7) | collective-permute-done | bytes 98336 | tf_op jit(solution)/shard_map/ppermute | solution.py:347
  52.0 4.6 %gradients.1 = (bf16[160,384]{1,0:T(8,128)(2,1)S(1)}, bf16[32,80,128]{2,1,0:T(8,128)(2,1)}, bf16[32,80,128]{2,1,0:T(8,128)(2,1)}, f32[160,4096]{1,0:T(8,128)}) custom-call(s32[2]{0:T(128)S(1)} %pad_add_fusion.where_ref, f32[160,384]{1,0:T(8,128)S(1)} %early_products.3.pre_ref, bf16[80,4096]{1,0:T(8,128)(2,1)S(1)} %copy-done, bf16[80,4096]{1,0:T(8,128)(2,1)S(1)} %copy-done.2, ...), custom_call_target="tpu_custom_call" | custom-call | tf_op jit(solution)/shard_map/gradients/pallas_call | solution.py:237
  56.6 7.5 %collective-permute-start.8 = (bf16[32,80,128]{2,1,0:T(8,128)(2,1)}, bf16[32,80,128]{2,1,0:T(8,128)(2,1)S(1)}, u32[]{:S(2)}, u32[]{:S(2)}) collective-permute-start(bf16[32,80,128]{2,1,0:T(8,128)(2,1)} %get-tuple-element.16), channel_id=1, source_target_pairs={{0,8},{8,0},{1,9},{9,1},{2,10},{10,2},{3,11},{11,3},{4,12},{12,4},... | collective-permute-start | bytes 1966088 | tf_op jit(solution)/shard_map/ppermute | solution.py:374
  64.2 2.0 %act_terms.1 = bf16[384,4096]{1,0:T(8,128)(2,1)} custom-call(bf16[160,384]{1,0:T(8,128)(2,1)S(1)} %get-tuple-element.17.d_ref, bf16[80,4096]{1,0:T(8,128)(2,1)S(1)} %copy-done.1, bf16[80,4096]{1,0:T(8,128)(2,1)S(1)} %copy-done.3), custom_call_target="tpu_custom_call" | custom-call | tf_op jit(solution)/shard_map/act_terms/pallas_call | solution.py:285
  66.2 1.2 pair_sum.1
  67.5 0.0 reduce-scatter.2.cloned.1.call-update
  67.5 31.1 %all_to_all.10.pieces_ref = bf16[32,80,128]{2,1,0:T(8,128)(2,1)S(1)} all-to-all(bf16[32,80,128]{2,1,0:T(8,128)(2,1)S(1)} %pair_sum.1), channel_id=1, replica_groups=mesh['x'=4,'z'=8,'core'=2,'tensor'=8] {'x','z'}, dimensions={0} | all-to-all | bytes 1310720 | tf_op jit(solution)/shard_map/all_to_all | solution.py:378
  98.6 0.1 mean_copies.1
  98.7 24.7 %all_to_all.11.own_ref = bf16[32,80,128]{2,1,0:T(8,128)(2,1)S(1)} all-to-all(bf16[32,80,128]{2,1,0:T(8,128)(2,1)S(1)} %mean_copies.1), channel_id=1, replica_groups=mesh['x'=4,'z'=8,'core'=2,'tensor'=8] {'x','z'}, dimensions={0} | all-to-all | bytes 1310720 | tf_op jit(solution)/shard_map/all_to_all | solution.py:380
  123.4 6.8 %collective-permute-start.9 = (bf16[32,80,128]{2,1,0:T(8,128)(2,1)S(1)}, bf16[32,80,128]{2,1,0:T(8,128)(2,1)S(1)}, u32[]{:S(2)}, u32[]{:S(2)}) collective-permute-start(bf16[32,80,128]{2,1,0:T(8,128)(2,1)S(1)} %all_to_all.11.own_ref), channel_id=1, source_target_pairs={{0,8},{8,0},{1,9},{9,1},{2,10},{10,2},{3,11},{11,3},{4,12},{12,4},... | collective-permute-start | bytes 1966088 | tf_op jit(solution)/shard_map/ppermute | solution.py:381
  130.3 0.1 copy.9
  130.3 0.1 reshape.16.q_ref
  130.4 1.5 %collective-permute-done.9.other_ref = bf16[32,80,128]{2,1,0:T(8,128)(2,1)S(1)} collective-permute-done((bf16[32,80,128]{2,1,0:T(8,128)(2,1)S(1)}, bf16[32,80,128]{2,1,0:T(8,128)(2,1)S(1)}, u32[]{:S(2)}, u32[]{:S(2)}) %collective-permute-start.9) | collective-permute-done | bytes 655392 | tf_op jit(solution)/shard_map/ppermute | solution.py:381
  132.0 10.1 %finish.1 = (bf16[2,80,4096]{2,1,0:T(8,128)(2,1)}, f32[2,64,80]{2,1,0:T(8,128)}) custom-call(s32[2]{0:T(128)S(1)} %pad_add_fusion.where_ref, bf16[32,80,128]{2,1,0:T(8,128)(2,1)S(1)} %all_to_all.11.own_ref, bf16[32,80,128]{2,1,0:T(8,128)(2,1)S(1)} %collective-permute-done.9.other_ref, f32[64,160]{1,0:T(8,128)S(1)} %reshape.16.q_ref, ...), custom_call_target="tpu_custom_call" | custom-call | tf_op jit(solution)/shard_map/finish/pallas_call | solution.py:111
  142.0 0.0 reduce-scatter.2.cloned.1.call-done
  (33 shorter events, 0.1 us)
Async XLA Ops:
  7.2 134.9 %reduce-scatter.2.cloned.1.call-start = ((), (), s32[]{:S(2)}) async-start(), calls=%async_computation.3 | async-start | bytes 3538944 | tf_op jit(solution)/shard_map/reduce_scatter | solution.py:377
  7.2 11.3 %collective-permute-start = (bf16[384,512]{1,0:T(8,128)(2,1)}, bf16[384,512]{1,0:T(8,128)(2,1)S(1)}, u32[]{:S(2)}, u32[]{:S(2)}) collective-permute-start(bf16[384,512]{1,0:T(8,128)(2,1)} %refs_0_.3), channel_id=1, source_target_pairs={{0,1},{1,2},{2,3},{3,4},{4,5},{5,6},{6,7},{7,0},{8,9},{9,10},{10,1... | collective-permute-start | bytes 1179656 | tf_op jit(solution)/shard_map/ppermute | solution.py:347
  11.3 11.3 %collective-permute-start.3 = (bf16[384,512]{1,0:T(8,128)(2,1)}, bf16[384,512]{1,0:T(8,128)(2,1)S(1)}, u32[]{:S(2)}, u32[]{:S(2)}) collective-permute-start(bf16[384,512]{1,0:T(8,128)(2,1)} %refs_0_.3), channel_id=1, source_target_pairs={{0,7},{1,0},{2,1},{3,2},{4,3},{5,4},{6,5},{7,6},{8,15},{9,8},{10,9... | collective-permute-start | bytes 1179656 | tf_op jit(solution)/shard_map/ppermute | solution.py:347
  18.5 31.7 %copy-start.7 = (bf16[384,512]{1,0:T(8,128)(2,1)}, bf16[384,512]{1,0:T(8,128)(2,1)S(1)}, u32[]{:S(2)}) copy-start(bf16[384,512]{1,0:T(8,128)(2,1)S(1)} %collective-permute-done.refs_1_) | copy-start | bytes 1179652
  18.5 11.9 %collective-permute-start.1 = (bf16[384,512]{1,0:T(8,128)(2,1)S(1)}, bf16[384,512]{1,0:T(8,128)(2,1)S(1)}, u32[]{:S(2)}, u32[]{:S(2)}) collective-permute-start(bf16[384,512]{1,0:T(8,128)(2,1)S(1)} %collective-permute-done.refs_1_), channel_id=1, source_target_pairs={{0,1},{1,2},{2,3},{3,4},{4,5},{5,6},{6,7},{7,0},{8,9},{9,10},{10,1... | collective-permute-start | bytes 1179656 | tf_op jit(solution)/shard_map/ppermute | solution.py:347
  22.5 27.7 %copy-start.8 = (bf16[384,512]{1,0:T(8,128)(2,1)}, bf16[384,512]{1,0:T(8,128)(2,1)S(1)}, u32[]{:S(2)}) copy-start(bf16[384,512]{1,0:T(8,128)(2,1)S(1)} %collective-permute-done.3.refs_2_) | copy-start | bytes 1179652
  22.6 10.8 %collective-permute-start.4 = (bf16[384,512]{1,0:T(8,128)(2,1)S(1)}, bf16[384,512]{1,0:T(8,128)(2,1)S(1)}, u32[]{:S(2)}, u32[]{:S(2)}) collective-permute-start(bf16[384,512]{1,0:T(8,128)(2,1)S(1)} %collective-permute-done.3.refs_2_), channel_id=1, source_target_pairs={{0,7},{1,0},{2,1},{3,2},{4,3},{5,4},{6,5},{7,6},{8,15},{9,8},{10,9... | collective-permute-start | bytes 1179656 | tf_op jit(solution)/shard_map/ppermute | solution.py:347
  30.4 19.9 %copy-start.9 = (bf16[384,512]{1,0:T(8,128)(2,1)}, bf16[384,512]{1,0:T(8,128)(2,1)S(1)}, u32[]{:S(2)}) copy-start(bf16[384,512]{1,0:T(8,128)(2,1)S(1)} %collective-permute-done.1.refs_3_) | copy-start | bytes 1179652
  30.4 12.3 %collective-permute-start.2 = (bf16[384,512]{1,0:T(8,128)(2,1)S(1)}, bf16[384,512]{1,0:T(8,128)(2,1)S(1)}, u32[]{:S(2)}, u32[]{:S(2)}) collective-permute-start(bf16[384,512]{1,0:T(8,128)(2,1)S(1)} %collective-permute-done.1.refs_3_), channel_id=1, source_target_pairs={{0,1},{1,2},{2,3},{3,4},{4,5},{5,6},{6,7},{7,0},{8,9},{9,10},{10,1... | collective-permute-start | bytes 1179656 | tf_op jit(solution)/shard_map/ppermute | solution.py:347
  33.4 16.9 %copy-start.10 = (bf16[384,512]{1,0:T(8,128)(2,1)}, bf16[384,512]{1,0:T(8,128)(2,1)S(1)}, u32[]{:S(2)}) copy-start(bf16[384,512]{1,0:T(8,128)(2,1)S(1)} %collective-permute-done.4.refs_4_) | copy-start | bytes 1179652
  33.4 11.8 %collective-permute-start.5 = (bf16[384,512]{1,0:T(8,128)(2,1)S(1)}, bf16[384,512]{1,0:T(8,128)(2,1)S(1)}, u32[]{:S(2)}, u32[]{:S(2)}) collective-permute-start(bf16[384,512]{1,0:T(8,128)(2,1)S(1)} %collective-permute-done.4.refs_4_), channel_id=1, source_target_pairs={{0,7},{1,0},{2,1},{3,2},{4,3},{5,4},{6,5},{7,6},{8,15},{9,8},{10,9... | collective-permute-start | bytes 1179656 | tf_op jit(solution)/shard_map/ppermute | solution.py:347
  38.2 1.1 copy-start
  39.3 1.1 copy-start.2
  40.4 1.0 copy-start.6
  41.4 10.6 %copy-start.11 = (bf16[1,2,80,4096]{3,2,1,0:T(8,128)(2,1)S(1)}, bf16[1,2,80,4096]{3,2,1,0:T(8,128)(2,1)}, u32[]{:S(2)}) copy-start(bf16[1,2,80,4096]{3,2,1,0:T(8,128)(2,1)} %param.10) | copy-start | bytes 3932164
  41.4 10.6 %copy-start.12 = (bf16[384,80]{0,1:T(8,128)(2,1)S(1)}, bf16[384,80]{0,1:T(8,128)(2,1)}, u32[]{:S(2)}) copy-start(bf16[384,80]{0,1:T(8,128)(2,1)} %param.9) | copy-start | bytes 184324
  42.7 9.3 %copy-start.4 = (bf16[384,512]{1,0:T(8,128)(2,1)}, bf16[384,512]{1,0:T(8,128)(2,1)S(1)}, u32[]{:S(2)}) copy-start(bf16[384,512]{1,0:T(8,128)(2,1)S(1)} %collective-permute-done.2.refs_0_.refs_5_) | copy-start | bytes 1179652
  42.7 9.2 %collective-permute-start.6 = (bf16[384,384]{1,0:T(8,128)(2,1)S(1)}, bf16[384,384]{1,0:T(8,128)(2,1)S(1)}, u32[]{:S(2)}, u32[]{:S(2)}) collective-permute-start(bf16[384,384]{1,0:T(8,128)(2,1)S(1)} %slice.8), channel_id=1, source_target_pairs={{0,1},{1,2},{2,3},{3,4},{4,5},{5,6},{6,7},{7,0},{8,9},{9,10},{10,1... | collective-permute-start | bytes 884744 | tf_op jit(solution)/shard_map/ppermute | solution.py:347
  45.2 6.7 %copy-start.5 = (bf16[384,512]{1,0:T(8,128)(2,1)}, bf16[384,512]{1,0:T(8,128)(2,1)S(1)}, u32[]{:S(2)}) copy-start(bf16[384,512]{1,0:T(8,128)(2,1)S(1)} %collective-permute-done.5.refs_1_.refs_6_) | copy-start | bytes 1179652
  45.3 6.7 %collective-permute-start.7 = (bf16[384,128]{1,0:T(8,128)(2,1)S(1)}, bf16[384,128]{1,0:T(8,128)(2,1)S(1)}, u32[]{:S(2)}, u32[]{:S(2)}) collective-permute-start(bf16[384,128]{1,0:T(8,128)(2,1)S(1)} %slice.9), channel_id=1, source_target_pairs={{0,7},{1,0},{2,1},{3,2},{4,3},{5,4},{6,5},{7,6},{8,15},{9,8},{10,9... | collective-permute-start | bytes 294920 | tf_op jit(solution)/shard_map/ppermute | solution.py:347
  52.0 12.2 %copy-start.1 = (bf16[80,4096]{1,0:T(8,128)(2,1)S(1)}, bf16[80,4096]{1,0:T(8,128)(2,1)}, u32[]{:S(2)}) copy-start(bf16[80,4096]{1,0:T(8,128)(2,1)} %gate_ref.7) | copy-start | bytes 1966084
  52.0 12.2 %copy-start.3 = (bf16[80,4096]{1,0:T(8,128)(2,1)S(1)}, bf16[80,4096]{1,0:T(8,128)(2,1)}, u32[]{:S(2)}) copy-start(bf16[80,4096]{1,0:T(8,128)(2,1)} %up_ref.7) | copy-start | bytes 1966084
  56.6 9.6 %collective-permute-start.8 = (bf16[32,80,128]{2,1,0:T(8,128)(2,1)}, bf16[32,80,128]{2,1,0:T(8,128)(2,1)S(1)}, u32[]{:S(2)}, u32[]{:S(2)}) collective-permute-start(bf16[32,80,128]{2,1,0:T(8,128)(2,1)} %get-tuple-element.16), channel_id=1, source_target_pairs={{0,8},{8,0},{1,9},{9,1},{2,10},{10,2},{3,11},{11,3},{4,12},{12,4},... | collective-permute-start | bytes 1966088 | tf_op jit(solution)/shard_map/ppermute | solution.py:374
  67.5 62.8 %copy-start.13 = (f32[2,80,64]{1,2,0:T(8,128)S(1)}, f32[2,80,64]{1,2,0:T(8,128)}, u32[]{:S(2)}) copy-start(f32[2,80,64]{1,2,0:T(8,128)} %param.11) | copy-start | bytes 122884
  123.4 8.5 %collective-permute-start.9 = (bf16[32,80,128]{2,1,0:T(8,128)(2,1)S(1)}, bf16[32,80,128]{2,1,0:T(8,128)(2,1)S(1)}, u32[]{:S(2)}, u32[]{:S(2)}) collective-permute-start(bf16[32,80,128]{2,1,0:T(8,128)(2,1)S(1)} %all_to_all.11.own_ref), channel_id=1, source_target_pairs={{0,8},{8,0},{1,9},{9,1},{2,10},{10,2},{3,11},{11,3},{4,12},{12,4},... | collective-permute-start | bytes 1966088 | tf_op jit(solution)/shard_map/ppermute | solution.py:381
Sparse Core Ops, SparseCore 0:
  67.6 51.3 reduce-scatter.1

commit v8 on v7

--- a/solution.py
+++ b/solution.py
@@ -69,10 +69,15 @@
         for k, part in enumerate(three_parts(p_mean)):
             stack_ref[units + k * rank : units + (k + 1) * rank, f : f + step] = part
     products = lax.dot_general(
-        stack_ref[...], stack_ref[units:, :], (((1,), (1,)), ((), ())), preferred_element_type=jnp.float32
+        stack_ref[0 : units + 2 * rank, :],
+        stack_ref[units:, :],
+        (((1,), (1,)), ((), ())),
+        preferred_element_type=jnp.float32,
     )
+    lowest = products[units:, 2 * rank :]
     products = products[:, 0:rank] + products[:, rank : 2 * rank] + products[:, 2 * rank :]
-    gram = products[units : units + rank] + products[units + rank : units + 2 * rank] + products[units + 2 * rank :]
+    lowest = lowest[0:rank] + lowest[rank:]
+    gram = products[units : units + rank] + products[units + rank :] + lowest.T
     inverse = inverse_cholesky(gram)
     for k in range(2):
         q_next_ref[k] = lax.dot_general(

time: 150 us -> 150 us (level)
  no operation moved by 1% of the time
where the time goes in v8:
time: 150 us; the launch traced here: 149 us
  blocking collectives  55.8 us (37%)
  starting transfers between devices  45.1 us (30%)
  Pallas kernels  20.2 us (13%)
  between operations  14.4 us (10%)
  waiting for transfers between devices  9.88 us (7%)
  local copies, waits for them, and re-layouts  3.42 us (2%)
    all_to_all x1, blocking collectives, on_device(): pieces = lax.all_to_all(pieces, CHIPS, 0, 0, tiled=True)  31.1 us
    ppermute x8, starting transfers between devices, ring(): lax.ppermute(value, 'tensor', [(i, (i + step) % ways) for i in range(ways)])  30.7 us
    all_to_all x1, blocking collectives, on_device(): own_half = lax.all_to_all(copies, CHIPS, 0, 0, tiled=True)  24.7 us
    pallas_call x1, Pallas kernels, finish(): pl.pallas_call(finish_kernel, out_shape=(jax.ShapeDtypeStruct((2, rows, w...  9.94 us
    ppermute x8, waiting for transfers between devices, ring(): lax.ppermute(value, 'tensor', [(i, (i + step) % ways) for i in range(ways)])  8.31 us
    ppermute x1, starting transfers between devices, on_device(): got = lax.ppermute(send, 'core', SWAP)  7.53 us
    ppermute x1, starting transfers between devices, on_device(): other_half = lax.ppermute(own_half, 'core', SWAP)  6.83 us
    pallas_call x1, Pallas kernels, gradients(): pl.pallas_call(functools.partial(gradient_kernel, places=[(shift, start)...  4.62 us
  transfers between devices with their start and end apart: 11, of which 4 were waited for; matrix products, arithmetic and copies ran while one was open for 0% of the time, Pallas kernels for 10%

profile of v8, /device:TPU:1, one launch (start us, length us, event | category | flops | bytes accessed | tf_op | source)
XLA Modules:
  0.0 148.8 jit_solution(12014154564232604600)
XLA Ops:
  7.2 0.0 reduce-scatter.2.cloned.1.call-start
  7.2 4.0 %collective-permute-start = (bf16[384,512]{1,0:T(8,128)(2,1)}, bf16[384,512]{1,0:T(8,128)(2,1)S(1)}, u32[]{:S(2)}, u32[]{:S(2)}) collective-permute-start(bf16[384,512]{1,0:T(8,128)(2,1)} %refs_0_.3), channel_id=1, source_target_pairs={{0,1},{1,2},{2,3},{3,4},{4,5},{5,6},{6,7},{7,0},{8,9},{9,10},{10,1... | collective-permute-start | bytes 1179656 | tf_op jit(solution)/shard_map/ppermute | solution.py:352
  11.3 3.8 %collective-permute-start.3 = (bf16[384,512]{1,0:T(8,128)(2,1)}, bf16[384,512]{1,0:T(8,128)(2,1)S(1)}, u32[]{:S(2)}, u32[]{:S(2)}) collective-permute-start(bf16[384,512]{1,0:T(8,128)(2,1)} %refs_0_.3), channel_id=1, source_target_pairs={{0,7},{1,0},{2,1},{3,2},{4,3},{5,4},{6,5},{7,6},{8,15},{9,8},{10,9... | collective-permute-start | bytes 1179656 | tf_op jit(solution)/shard_map/ppermute | solution.py:352
  15.1 3.4 %collective-permute-done.refs_1_ = bf16[384,512]{1,0:T(8,128)(2,1)S(1)} collective-permute-done((bf16[384,512]{1,0:T(8,128)(2,1)}, bf16[384,512]{1,0:T(8,128)(2,1)S(1)}, u32[]{:S(2)}, u32[]{:S(2)}) %collective-permute-start) | collective-permute-done | bytes 393248 | tf_op jit(solution)/shard_map/ppermute | solution.py:352
  18.5 4.0 %collective-permute-start.1 = (bf16[384,512]{1,0:T(8,128)(2,1)S(1)}, bf16[384,512]{1,0:T(8,128)(2,1)S(1)}, u32[]{:S(2)}, u32[]{:S(2)}) collective-permute-start(bf16[384,512]{1,0:T(8,128)(2,1)S(1)} %collective-permute-done.refs_1_), channel_id=1, source_target_pairs={{0,1},{1,2},{2,3},{3,4},{4,5},{5,6},{6,7},{7,0},{8,9},{9,10},{10,1... | collective-permute-start | bytes 1179656 | tf_op jit(solution)/shard_map/ppermute | solution.py:352
  22.6 4.6 %collective-permute-start.4 = (bf16[384,512]{1,0:T(8,128)(2,1)S(1)}, bf16[384,512]{1,0:T(8,128)(2,1)S(1)}, u32[]{:S(2)}, u32[]{:S(2)}) collective-permute-start(bf16[384,512]{1,0:T(8,128)(2,1)S(1)} %collective-permute-done.3.refs_2_), channel_id=1, source_target_pairs={{0,7},{1,0},{2,1},{3,2},{4,3},{5,4},{6,5},{7,6},{8,15},{9,8},{10,9... | collective-permute-start | bytes 1179656 | tf_op jit(solution)/shard_map/ppermute | solution.py:352
  27.2 3.2 %collective-permute-done.1.refs_3_ = bf16[384,512]{1,0:T(8,128)(2,1)S(1)} collective-permute-done((bf16[384,512]{1,0:T(8,128)(2,1)S(1)}, bf16[384,512]{1,0:T(8,128)(2,1)S(1)}, u32[]{:S(2)}, u32[]{:S(2)}) %collective-permute-start.1) | collective-permute-done | bytes 393248 | tf_op jit(solution)/shard_map/ppermute | solution.py:352
  30.4 3.0 %collective-permute-start.2 = (bf16[384,512]{1,0:T(8,128)(2,1)S(1)}, bf16[384,512]{1,0:T(8,128)(2,1)S(1)}, u32[]{:S(2)}, u32[]{:S(2)}) collective-permute-start(bf16[384,512]{1,0:T(8,128)(2,1)S(1)} %collective-permute-done.1.refs_3_), channel_id=1, source_target_pairs={{0,1},{1,2},{2,3},{3,4},{4,5},{5,6},{6,7},{7,0},{8,9},{9,10},{10,1... | collective-permute-start | bytes 1179656 | tf_op jit(solution)/shard_map/ppermute | solution.py:352
  33.4 4.7 %collective-permute-start.5 = (bf16[384,512]{1,0:T(8,128)(2,1)S(1)}, bf16[384,512]{1,0:T(8,128)(2,1)S(1)}, u32[]{:S(2)}, u32[]{:S(2)}) collective-permute-start(bf16[384,512]{1,0:T(8,128)(2,1)S(1)} %collective-permute-done.4.refs_4_), channel_id=1, source_target_pairs={{0,7},{1,0},{2,1},{3,2},{4,3},{5,4},{6,5},{7,6},{8,15},{9,8},{10,9... | collective-permute-start | bytes 1179656 | tf_op jit(solution)/shard_map/ppermute | solution.py:352
  38.1 0.1 pad_add_fusion.where_ref
  38.2 1.1 copy-done
  39.3 1.1 copy-done.2
  40.4 1.0 copy-done.6
  41.4 1.3 early_products.2.refs_2_
  42.7 2.5 %collective-permute-start.6 = (bf16[384,384]{1,0:T(8,128)(2,1)S(1)}, bf16[384,384]{1,0:T(8,128)(2,1)S(1)}, u32[]{:S(2)}, u32[]{:S(2)}) collective-permute-start(bf16[384,384]{1,0:T(8,128)(2,1)S(1)} %slice.8), channel_id=1, source_target_pairs={{0,1},{1,2},{2,3},{3,4},{4,5},{5,6},{6,7},{7,0},{8,9},{9,10},{10,1... | collective-permute-start | bytes 884744 | tf_op jit(solution)/shard_map/ppermute | solution.py:352
  45.3 4.0 %collective-permute-start.7 = (bf16[384,128]{1,0:T(8,128)(2,1)S(1)}, bf16[384,128]{1,0:T(8,128)(2,1)S(1)}, u32[]{:S(2)}, u32[]{:S(2)}) collective-permute-start(bf16[384,128]{1,0:T(8,128)(2,1)S(1)} %slice.9), channel_id=1, source_target_pairs={{0,7},{1,0},{2,1},{3,2},{4,3},{5,4},{6,5},{7,6},{8,15},{9,8},{10,9... | collective-permute-start | bytes 294920 | tf_op jit(solution)/shard_map/ppermute | solution.py:352
  49.3 0.9 early_products.3.pre_ref
  50.3 1.7 %collective-permute-done.7.refs_8_ = bf16[384,128]{1,0:T(8,128)(2,1)S(1)} collective-permute-done((bf16[384,128]{1,0:T(8,128)(2,1)S(1)}, bf16[384,128]{1,0:T(8,128)(2,1)S(1)}, u32[]{:S(2)}, u32[]{:S(2)}) %collective-permute-start.7) | collective-permute-done | bytes 98336 | tf_op jit(solution)/shard_map/ppermute | solution.py:352
  52.0 4.6 %gradients.1 = (bf16[160,384]{1,0:T(8,128)(2,1)S(1)}, bf16[32,80,128]{2,1,0:T(8,128)(2,1)}, bf16[32,80,128]{2,1,0:T(8,128)(2,1)}, f32[160,4096]{1,0:T(8,128)}) custom-call(s32[2]{0:T(128)S(1)} %pad_add_fusion.where_ref, f32[160,384]{1,0:T(8,128)S(1)} %early_products.3.pre_ref, bf16[80,4096]{1,0:T(8,128)(2,1)S(1)} %copy-done, bf16[80,4096]{1,0:T(8,128)(2,1)S(1)} %copy-done.2, ...), custom_call_target="tpu_custom_call" | custom-call | tf_op jit(solution)/shard_map/gradients/pallas_call | solution.py:242
  56.6 7.5 %collective-permute-start.8 = (bf16[32,80,128]{2,1,0:T(8,128)(2,1)}, bf16[32,80,128]{2,1,0:T(8,128)(2,1)S(1)}, u32[]{:S(2)}, u32[]{:S(2)}) collective-permute-start(bf16[32,80,128]{2,1,0:T(8,128)(2,1)} %get-tuple-element.16), channel_id=1, source_target_pairs={{0,8},{8,0},{1,9},{9,1},{2,10},{10,2},{3,11},{11,3},{4,12},{12,4},... | collective-permute-start | bytes 1966088 | tf_op jit(solution)/shard_map/ppermute | solution.py:379
  64.2 2.0 %act_terms.1 = bf16[384,4096]{1,0:T(8,128)(2,1)} custom-call(bf16[160,384]{1,0:T(8,128)(2,1)S(1)} %get-tuple-element.17.d_ref, bf16[80,4096]{1,0:T(8,128)(2,1)S(1)} %copy-done.1, bf16[80,4096]{1,0:T(8,128)(2,1)S(1)} %copy-done.3), custom_call_target="tpu_custom_call" | custom-call | tf_op jit(solution)/shard_map/act_terms/pallas_call | solution.py:290
  66.2 1.2 pair_sum.1
  67.5 0.0 reduce-scatter.2.cloned.1.call-update
  67.5 31.1 %all_to_all.10.pieces_ref = bf16[32,80,128]{2,1,0:T(8,128)(2,1)S(1)} all-to-all(bf16[32,80,128]{2,1,0:T(8,128)(2,1)S(1)} %pair_sum.1), channel_id=1, replica_groups=mesh['x'=4,'z'=8,'core'=2,'tensor'=8] {'x','z'}, dimensions={0} | all-to-all | bytes 1310720 | tf_op jit(solution)/shard_map/all_to_all | solution.py:383
  98.6 0.1 mean_copies.1
  98.7 24.7 %all_to_all.11.own_ref = bf16[32,80,128]{2,1,0:T(8,128)(2,1)S(1)} all-to-all(bf16[32,80,128]{2,1,0:T(8,128)(2,1)S(1)} %mean_copies.1), channel_id=1, replica_groups=mesh['x'=4,'z'=8,'core'=2,'tensor'=8] {'x','z'}, dimensions={0} | all-to-all | bytes 1310720 | tf_op jit(solution)/shard_map/all_to_all | solution.py:385
  123.4 6.8 %collective-permute-start.9 = (bf16[32,80,128]{2,1,0:T(8,128)(2,1)S(1)}, bf16[32,80,128]{2,1,0:T(8,128)(2,1)S(1)}, u32[]{:S(2)}, u32[]{:S(2)}) collective-permute-start(bf16[32,80,128]{2,1,0:T(8,128)(2,1)S(1)} %all_to_all.11.own_ref), channel_id=1, source_target_pairs={{0,8},{8,0},{1,9},{9,1},{2,10},{10,2},{3,11},{11,3},{4,12},{12,4},... | collective-permute-start | bytes 1966088 | tf_op jit(solution)/shard_map/ppermute | solution.py:386
  130.3 0.1 copy.9
  130.3 0.1 reshape.16.q_ref
  130.4 1.5 %collective-permute-done.9.other_ref = bf16[32,80,128]{2,1,0:T(8,128)(2,1)S(1)} collective-permute-done((bf16[32,80,128]{2,1,0:T(8,128)(2,1)S(1)}, bf16[32,80,128]{2,1,0:T(8,128)(2,1)S(1)}, u32[]{:S(2)}, u32[]{:S(2)}) %collective-permute-start.9) | collective-permute-done | bytes 655392 | tf_op jit(solution)/shard_map/ppermute | solution.py:386
  132.0 9.9 %finish.1 = (bf16[2,80,4096]{2,1,0:T(8,128)(2,1)}, f32[2,64,80]{2,1,0:T(8,128)}) custom-call(s32[2]{0:T(128)S(1)} %pad_add_fusion.where_ref, bf16[32,80,128]{2,1,0:T(8,128)(2,1)S(1)} %all_to_all.11.own_ref, bf16[32,80,128]{2,1,0:T(8,128)(2,1)S(1)} %collective-permute-done.9.other_ref, f32[64,160]{1,0:T(8,128)S(1)} %reshape.16.q_ref, ...), custom_call_target="tpu_custom_call" | custom-call | tf_op jit(solution)/shard_map/finish/pallas_call | solution.py:116
  141.9 0.0 reduce-scatter.2.cloned.1.call-done
  (33 shorter events, 0.1 us)
Async XLA Ops:
  7.2 134.8 %reduce-scatter.2.cloned.1.call-start = ((), (), s32[]{:S(2)}) async-start(), calls=%async_computation.3 | async-start | bytes 3538944 | tf_op jit(solution)/shard_map/reduce_scatter | solution.py:382
  7.2 11.3 %collective-permute-start = (bf16[384,512]{1,0:T(8,128)(2,1)}, bf16[384,512]{1,0:T(8,128)(2,1)S(1)}, u32[]{:S(2)}, u32[]{:S(2)}) collective-permute-start(bf16[384,512]{1,0:T(8,128)(2,1)} %refs_0_.3), channel_id=1, source_target_pairs={{0,1},{1,2},{2,3},{3,4},{4,5},{5,6},{6,7},{7,0},{8,9},{9,10},{10,1... | collective-permute-start | bytes 1179656 | tf_op jit(solution)/shard_map/ppermute | solution.py:352
  11.3 11.3 %collective-permute-start.3 = (bf16[384,512]{1,0:T(8,128)(2,1)}, bf16[384,512]{1,0:T(8,128)(2,1)S(1)}, u32[]{:S(2)}, u32[]{:S(2)}) collective-permute-start(bf16[384,512]{1,0:T(8,128)(2,1)} %refs_0_.3), channel_id=1, source_target_pairs={{0,7},{1,0},{2,1},{3,2},{4,3},{5,4},{6,5},{7,6},{8,15},{9,8},{10,9... | collective-permute-start | bytes 1179656 | tf_op jit(solution)/shard_map/ppermute | solution.py:352
  18.5 31.7 %copy-start.7 = (bf16[384,512]{1,0:T(8,128)(2,1)}, bf16[384,512]{1,0:T(8,128)(2,1)S(1)}, u32[]{:S(2)}) copy-start(bf16[384,512]{1,0:T(8,128)(2,1)S(1)} %collective-permute-done.refs_1_) | copy-start | bytes 1179652
  18.5 11.9 %collective-permute-start.1 = (bf16[384,512]{1,0:T(8,128)(2,1)S(1)}, bf16[384,512]{1,0:T(8,128)(2,1)S(1)}, u32[]{:S(2)}, u32[]{:S(2)}) collective-permute-start(bf16[384,512]{1,0:T(8,128)(2,1)S(1)} %collective-permute-done.refs_1_), channel_id=1, source_target_pairs={{0,1},{1,2},{2,3},{3,4},{4,5},{5,6},{6,7},{7,0},{8,9},{9,10},{10,1... | collective-permute-start | bytes 1179656 | tf_op jit(solution)/shard_map/ppermute | solution.py:352
  22.5 27.7 %copy-start.8 = (bf16[384,512]{1,0:T(8,128)(2,1)}, bf16[384,512]{1,0:T(8,128)(2,1)S(1)}, u32[]{:S(2)}) copy-start(bf16[384,512]{1,0:T(8,128)(2,1)S(1)} %collective-permute-done.3.refs_2_) | copy-start | bytes 1179652
  22.6 10.8 %collective-permute-start.4 = (bf16[384,512]{1,0:T(8,128)(2,1)S(1)}, bf16[384,512]{1,0:T(8,128)(2,1)S(1)}, u32[]{:S(2)}, u32[]{:S(2)}) collective-permute-start(bf16[384,512]{1,0:T(8,128)(2,1)S(1)} %collective-permute-done.3.refs_2_), channel_id=1, source_target_pairs={{0,7},{1,0},{2,1},{3,2},{4,3},{5,4},{6,5},{7,6},{8,15},{9,8},{10,9... | collective-permute-start | bytes 1179656 | tf_op jit(solution)/shard_map/ppermute | solution.py:352
  30.4 19.9 %copy-start.9 = (bf16[384,512]{1,0:T(8,128)(2,1)}, bf16[384,512]{1,0:T(8,128)(2,1)S(1)}, u32[]{:S(2)}) copy-start(bf16[384,512]{1,0:T(8,128)(2,1)S(1)} %collective-permute-done.1.refs_3_) | copy-start | bytes 1179652
  30.4 12.3 %collective-permute-start.2 = (bf16[384,512]{1,0:T(8,128)(2,1)S(1)}, bf16[384,512]{1,0:T(8,128)(2,1)S(1)}, u32[]{:S(2)}, u32[]{:S(2)}) collective-permute-start(bf16[384,512]{1,0:T(8,128)(2,1)S(1)} %collective-permute-done.1.refs_3_), channel_id=1, source_target_pairs={{0,1},{1,2},{2,3},{3,4},{4,5},{5,6},{6,7},{7,0},{8,9},{9,10},{10,1... | collective-permute-start | bytes 1179656 | tf_op jit(solution)/shard_map/ppermute | solution.py:352
  33.4 16.9 %copy-start.10 = (bf16[384,512]{1,0:T(8,128)(2,1)}, bf16[384,512]{1,0:T(8,128)(2,1)S(1)}, u32[]{:S(2)}) copy-start(bf16[384,512]{1,0:T(8,128)(2,1)S(1)} %collective-permute-done.4.refs_4_) | copy-start | bytes 1179652
  33.4 11.8 %collective-permute-start.5 = (bf16[384,512]{1,0:T(8,128)(2,1)S(1)}, bf16[384,512]{1,0:T(8,128)(2,1)S(1)}, u32[]{:S(2)}, u32[]{:S(2)}) collective-permute-start(bf16[384,512]{1,0:T(8,128)(2,1)S(1)} %collective-permute-done.4.refs_4_), channel_id=1, source_target_pairs={{0,7},{1,0},{2,1},{3,2},{4,3},{5,4},{6,5},{7,6},{8,15},{9,8},{10,9... | collective-permute-start | bytes 1179656 | tf_op jit(solution)/shard_map/ppermute | solution.py:352
  38.2 1.1 copy-start
  39.3 1.1 copy-start.2
  40.4 1.0 copy-start.6
  41.4 10.6 %copy-start.11 = (bf16[1,2,80,4096]{3,2,1,0:T(8,128)(2,1)S(1)}, bf16[1,2,80,4096]{3,2,1,0:T(8,128)(2,1)}, u32[]{:S(2)}) copy-start(bf16[1,2,80,4096]{3,2,1,0:T(8,128)(2,1)} %param.10) | copy-start | bytes 3932164
  41.4 10.6 %copy-start.12 = (bf16[384,80]{0,1:T(8,128)(2,1)S(1)}, bf16[384,80]{0,1:T(8,128)(2,1)}, u32[]{:S(2)}) copy-start(bf16[384,80]{0,1:T(8,128)(2,1)} %param.9) | copy-start | bytes 184324
  42.7 9.3 %copy-start.4 = (bf16[384,512]{1,0:T(8,128)(2,1)}, bf16[384,512]{1,0:T(8,128)(2,1)S(1)}, u32[]{:S(2)}) copy-start(bf16[384,512]{1,0:T(8,128)(2,1)S(1)} %collective-permute-done.2.refs_0_.refs_5_) | copy-start | bytes 1179652
  42.7 9.2 %collective-permute-start.6 = (bf16[384,384]{1,0:T(8,128)(2,1)S(1)}, bf16[384,384]{1,0:T(8,128)(2,1)S(1)}, u32[]{:S(2)}, u32[]{:S(2)}) collective-permute-start(bf16[384,384]{1,0:T(8,128)(2,1)S(1)} %slice.8), channel_id=1, source_target_pairs={{0,1},{1,2},{2,3},{3,4},{4,5},{5,6},{6,7},{7,0},{8,9},{9,10},{10,1... | collective-permute-start | bytes 884744 | tf_op jit(solution)/shard_map/ppermute | solution.py:352
  45.2 6.7 %copy-start.5 = (bf16[384,512]{1,0:T(8,128)(2,1)}, bf16[384,512]{1,0:T(8,128)(2,1)S(1)}, u32[]{:S(2)}) copy-start(bf16[384,512]{1,0:T(8,128)(2,1)S(1)} %collective-permute-done.5.refs_1_.refs_6_) | copy-start | bytes 1179652
  45.3 6.7 %collective-permute-start.7 = (bf16[384,128]{1,0:T(8,128)(2,1)S(1)}, bf16[384,128]{1,0:T(8,128)(2,1)S(1)}, u32[]{:S(2)}, u32[]{:S(2)}) collective-permute-start(bf16[384,128]{1,0:T(8,128)(2,1)S(1)} %slice.9), channel_id=1, source_target_pairs={{0,7},{1,0},{2,1},{3,2},{4,3},{5,4},{6,5},{7,6},{8,15},{9,8},{10,9... | collective-permute-start | bytes 294920 | tf_op jit(solution)/shard_map/ppermute | solution.py:352
  52.0 12.2 %copy-start.1 = (bf16[80,4096]{1,0:T(8,128)(2,1)S(1)}, bf16[80,4096]{1,0:T(8,128)(2,1)}, u32[]{:S(2)}) copy-start(bf16[80,4096]{1,0:T(8,128)(2,1)} %gate_ref.7) | copy-start | bytes 1966084
  52.0 12.2 %copy-start.3 = (bf16[80,4096]{1,0:T(8,128)(2,1)S(1)}, bf16[80,4096]{1,0:T(8,128)(2,1)}, u32[]{:S(2)}) copy-start(bf16[80,4096]{1,0:T(8,128)(2,1)} %up_ref.7) | copy-start | bytes 1966084
  56.6 9.6 %collective-permute-start.8 = (bf16[32,80,128]{2,1,0:T(8,128)(2,1)}, bf16[32,80,128]{2,1,0:T(8,128)(2,1)S(1)}, u32[]{:S(2)}, u32[]{:S(2)}) collective-permute-start(bf16[32,80,128]{2,1,0:T(8,128)(2,1)} %get-tuple-element.16), channel_id=1, source_target_pairs={{0,8},{8,0},{1,9},{9,1},{2,10},{10,2},{3,11},{11,3},{4,12},{12,4},... | collective-permute-start | bytes 1966088 | tf_op jit(solution)/shard_map/ppermute | solution.py:379
  67.5 62.8 %copy-start.13 = (f32[2,80,64]{1,2,0:T(8,128)S(1)}, f32[2,80,64]{1,2,0:T(8,128)}, u32[]{:S(2)}) copy-start(f32[2,80,64]{1,2,0:T(8,128)} %param.11) | copy-start | bytes 122884
  123.4 8.5 %collective-permute-start.9 = (bf16[32,80,128]{2,1,0:T(8,128)(2,1)S(1)}, bf16[32,80,128]{2,1,0:T(8,128)(2,1)S(1)}, u32[]{:S(2)}, u32[]{:S(2)}) collective-permute-start(bf16[32,80,128]{2,1,0:T(8,128)(2,1)S(1)} %all_to_all.11.own_ref), channel_id=1, source_target_pairs={{0,8},{8,0},{1,9},{9,1},{2,10},{10,2},{3,11},{11,3},{4,12},{12,4},... | collective-permute-start | bytes 1966088 | tf_op jit(solution)/shard_map/ppermute | solution.py:386
Sparse Core Ops, SparseCore 0:
  67.6 51.3 reduce-scatter.1
